TPU v7x, 32 devices: a whole 2x2x4 slice. The times are simulated.
32 devices in a mesh: section: 2 (over x), lat: 4 (over y, core), lon: 4 (over z).
Axes of the slice: x: 2, y: 2, z: 4, core: 2. Of those that a mesh axis runs over, the one named last changes fastest.
Arguments:
- window_input: bfloat16 [2, 16, 272, 256], P(None, 'lat', 'lon'), may hold values from -8 to 8
- output_cotangent: bfloat16 [2, 16, 272, 256], P(None, 'lat', 'lon'), may hold values from -6 to 6
- ocean_mask: int32 [16, 272], P('lat', 'lon'), may hold values 0 or 1
- dw_kernel: bfloat16 [2, 49, 256], P('section'), may hold values from -1.5 to 1.5
- channel_params: bfloat16 [2, 5, 256], P('section'), may hold values from -1.5 to 1.5
- up_weight: bfloat16 [2, 256, 1024], P('section'), may hold values from -0.375 to 0.375
- up_bias: bfloat16 [2, 1024], P('section'), may hold values from -3 to 3
- down_weight: bfloat16 [2, 1024, 256], P('section'), may hold values from -0.1875 to 0.1875
Outputs:
- boundary: bfloat16 [2, 2, 16, 272, 256], P('section', None, 'lat', 'lon')
- grad_kernel: float32 [2, 49, 256], P('section')
- grad_channels: float32 [2, 5, 256], P('section')
- grad_up: float32 [2, 256, 1024], P('section')
- grad_up_bias: float32 [2, 1024], P('section')
- grad_down: float32 [2, 1024, 256], P('section')
All inputs are finite; a program needn't handle non-finite values. No bound on the sum of `ocean_mask` on one device may be relied on, other than what follows from the above.
Results may differ from a plain program's by a relative error of at most 0.012.
Values may be sent and summed in bfloat16 or wider, within the bound.
No kernel may reach another device: no remote copies, remote signals or barrier semaphores. Data moves between devices by JAX's collectives and lax.ppermute only.
A program may use at most 128 MiB of HBM per device.

v0:
```python
import math

import jax
import jax.numpy as jnp
from jax import lax
from jax.sharding import PartitionSpec as P

KERNEL = 7
ROWS_DEV = 4
COLS_DEV = 68
BATCH = 2


norm_eps = 1e-06
gelu_scale = 0.7978845608028654
gelu_cubic = 0.044715
rows_contract = (((0,), (0,)), ((), ()))
cols_contract = (((1,), (1,)), ((), ()))


def padded_2(block, sides, width, periodic):
    for axis, dim in sides:
        count = lax.axis_size(axis)
        forward = [(i, i + 1) for i in range(count - 1)]
        if periodic:
            forward.append((count - 1, 0))
        backward = [(target, source) for source, target in forward]
        low = lax.ppermute(
            lax.slice_in_dim(block, block.shape[dim] - width, None, axis=dim), axis, forward
        )
        high = lax.ppermute(lax.slice_in_dim(block, 0, width, axis=dim), axis, backward)
        block = jnp.concatenate([low, block, high], axis=dim)
    return block


def from_behind(value, axis, by):
    count = lax.axis_size(axis)
    pairs = [(i, i + by) for i in range(count) if 0 <= i + by < count]
    return lax.ppermute(value, axis, pairs)


def gelu_value(values):
    inner = gelu_scale * (values + gelu_cubic * values * values * values)
    return 0.5 * values * (1.0 + jnp.tanh(inner))


def gelu_slope(values):
    tangent = jnp.tanh(gelu_scale * (values + gelu_cubic * values * values * values))
    return 0.5 * (1.0 + tangent) + 0.5 * values * (1.0 - tangent * tangent) * gelu_scale * (
        1.0 + 3.0 * gelu_cubic * values * values
    )


def depthwise(padded, kernel, row_count, col_count):
    summed = jnp.zeros((padded.shape[0], row_count, col_count, padded.shape[3]), jnp.float32)
    for offset in range(KERNEL * KERNEL):
        row_off, col_off = divmod(offset, KERNEL)
        window = padded[:, row_off : row_off + row_count, col_off : col_off + col_count, :]
        summed = summed + window.astype(jnp.float32) * kernel[offset].astype(jnp.float32)
    return summed


def kernel_grads(padded, grad_conv, row_count, col_count):
    channels = grad_conv.shape[-1]
    grad_wide = grad_conv.astype(jnp.float32)
    tap_sums = []
    for offset in range(KERNEL * KERNEL):
        row_off, col_off = divmod(offset, KERNEL)
        window = padded[:, row_off : row_off + row_count, col_off : col_off + col_count, :].astype(
            jnp.float32
        )
        tap_sums.append(jnp.sum((grad_wide * window).reshape(-1, channels), axis=0))
    return (jnp.stack(tap_sums), jnp.sum(grad_wide.reshape(-1, channels), axis=0))


def cell_forward(conv_out, inputs, sea_mask, params, w_up, b_up, w_down):
    average = jnp.mean(conv_out, axis=-1, keepdims=True)
    centered = conv_out - average
    inverse = lax.rsqrt(jnp.mean(centered * centered, axis=-1, keepdims=True) + norm_eps)
    normed = centered * inverse
    scaled = (normed * params[1].astype(jnp.float32) + params[2].astype(jnp.float32)).astype(
        jnp.bfloat16
    )
    channels = scaled.shape[-1]
    flat_rows = scaled.reshape(-1, channels)
    hidden = jnp.dot(flat_rows, w_up, preferred_element_type=jnp.float32) + b_up.astype(jnp.float32)
    active = gelu_value(hidden).astype(jnp.bfloat16)
    branch = jnp.dot(active, w_down, preferred_element_type=jnp.float32) + params[3].astype(
        jnp.float32
    )
    branch = branch.reshape(conv_out.shape)
    output = (
        sea_mask * (inputs.astype(jnp.float32) + params[4].astype(jnp.float32) * branch)
    ).astype(jnp.bfloat16)
    return (output, (normed, inverse, flat_rows, hidden, active, branch))


def cell_backward(saved, sea_mask, cotangent, params, w_up, w_down):
    normed, inverse, flat_rows, hidden, active, branch = saved
    channels = normed.shape[-1]
    upstream = sea_mask * cotangent.astype(jnp.float32)
    grad_scale = jnp.sum((upstream * branch).reshape(-1, channels), axis=0)
    grad_branch = (
        (params[4].astype(jnp.float32) * upstream).astype(jnp.bfloat16).reshape(-1, channels)
    )
    grad_down = lax.dot_general(
        active, grad_branch, rows_contract, preferred_element_type=jnp.float32
    )
    grad_out_bias = jnp.sum(grad_branch.astype(jnp.float32), axis=0)
    grad_active = lax.dot_general(
        grad_branch, w_down, cols_contract, preferred_element_type=jnp.float32
    )
    grad_hidden = (grad_active * gelu_slope(hidden)).astype(jnp.bfloat16)
    grad_up = lax.dot_general(
        flat_rows, grad_hidden, rows_contract, preferred_element_type=jnp.float32
    )
    grad_up_bias = jnp.sum(grad_hidden.astype(jnp.float32), axis=0)
    grad_scaled = lax.dot_general(
        grad_hidden, w_up, cols_contract, preferred_element_type=jnp.float32
    )
    grad_scaled = grad_scaled.reshape(normed.shape)
    grad_gain = jnp.sum((grad_scaled * normed).reshape(-1, channels), axis=0)
    grad_shift = jnp.sum(grad_scaled.reshape(-1, channels), axis=0)
    grad_normed = grad_scaled * params[1].astype(jnp.float32)
    first_mean = jnp.mean(grad_normed, axis=-1, keepdims=True)
    second_mean = jnp.mean(grad_normed * normed, axis=-1, keepdims=True)
    grad_conv = (inverse * (grad_normed - first_mean - normed * second_mean)).astype(jnp.bfloat16)
    small = (grad_gain, grad_shift, grad_out_bias, grad_scale)
    return (grad_conv, upstream, small, grad_up, grad_up_bias, grad_down)


def halo_field(field):
    reach = KERNEL // 2
    beside_all = padded_2(field, (("lon", 2),), reach, True)
    return padded_2(beside_all, (("lat", 1),), reach, False)


def run_forward(field, sea_mask, weights):
    kernel, params, w_up, b_up, w_down = weights
    padded = halo_field(field)
    conv_out = depthwise(padded, kernel, field.shape[1], field.shape[2]) + params[0].astype(
        jnp.float32
    )
    output, saved = cell_forward(conv_out, field, sea_mask, params, w_up, b_up, w_down)
    return (output, (padded, saved))


def run_backward(stored, sea_mask, weights, cotangent):
    kernel, params, w_up, b_up, w_down = weights
    padded, saved = stored
    row_count, col_count = (cotangent.shape[1], cotangent.shape[2])
    grad_conv, upstream, small, grad_up, grad_bias, grad_down = cell_backward(
        saved, sea_mask, cotangent, params, w_up, w_down
    )
    tap_sums, bias_sum = kernel_grads(padded, grad_conv, row_count, col_count)
    spread = depthwise(halo_field(grad_conv), kernel[::-1], row_count, col_count)
    grad_input = (upstream + spread).astype(jnp.bfloat16)
    return (grad_input, (tap_sums, jnp.stack((bias_sum,) + small), grad_up, grad_bias, grad_down))


def on_device(
    window_input,
    output_cotangent,
    ocean_mask,
    dw_kernel,
    channel_params,
    up_weight,
    up_bias,
    down_weight,
):
    section = lax.axis_index("section")
    first_section = section == 0
    sea_mask = ocean_mask.astype(jnp.float32)[None, :, :, None]
    batch_size = window_input.shape[0]
    local = (dw_kernel[0], channel_params[0], up_weight[0], up_bias[0], down_weight[0])
    micro = 1
    size_micro = batch_size // micro
    zero_field = jnp.zeros((size_micro,) + window_input.shape[1:], jnp.bfloat16)
    received = zero_field
    stored = []
    outputs = []
    for tick in range(micro + 1):
        if tick < micro:
            own_part = window_input
        else:
            own_part = zero_field
        current = jnp.where(first_section, own_part, received)
        result, kept = run_forward(current, sea_mask, local)
        stored.append(kept)
        outputs.append(result)
        if tick < micro:
            received = from_behind(result, "section", 1)
    received = zero_field
    grad_inputs = []
    totals = None
    for tick in range(micro + 1):
        if tick < micro:
            own_part = output_cotangent
        else:
            own_part = zero_field
        current = jnp.where(first_section, received, own_part)
        kept = jax.tree.map(
            lambda before, behind: jnp.where(first_section, before, behind),
            stored[max(tick - 1, 0)],
            stored[min(tick + 1, micro)],
        )
        grad_input, grads = run_backward(kept, sea_mask, local, current)
        counted = jnp.where(
            first_section, 1.0 if tick >= 1 else 0.0, 1.0 if tick < micro else 0.0
        ).astype(jnp.float32)
        weighted = jax.tree.map(lambda member: member * counted, grads)
        if totals is None:
            totals = weighted
        else:
            totals = jax.tree.map(jnp.add, totals, weighted)
        grad_inputs.append(grad_input)
        if tick < micro:
            received = from_behind(grad_input, "section", -1)
    final = jnp.concatenate(outputs[1:], axis=0)
    starts = jnp.concatenate(grad_inputs[1:], axis=0)
    boundary = jnp.where(first_section, starts, final)[None]
    owned = tuple((member[None] for member in totals))
    summed = lax.psum((owned[0], owned[1], owned[2], owned[3], owned[4]), ("lat", "lon"))
    factor = 1.0 / math.sqrt(BATCH * ROWS_DEV * COLS_DEV)
    return (
        boundary,
        summed[0] * factor,
        summed[1] * factor,
        summed[2] * factor,
        summed[3] * factor,
        summed[4] * factor,
    )


def solution(mesh):
    in_specs = (
        P(None, "lat", "lon", None),
        P(None, "lat", "lon", None),
        P("lat", "lon"),
        P("section", None, None),
        P("section", None, None),
        P("section", None, None),
        P("section", None),
        P("section", None, None),
    )
    out_specs = (
        P("section", None, "lat", "lon", None),
        P("section", None, None),
        P("section", None, None),
        P("section", None, None),
        P("section", None),
        P("section", None, None),
    )
    return jax.shard_map(
        on_device, mesh=mesh, in_specs=in_specs, out_specs=out_specs, check_vma=False
    )
```

profile of v0, /device:TPU:1, one launch (start us, length us, event | category | flops | bytes accessed | tf_op | source)
XLA Modules:
  0.0 315.8 jit_solution(17570287013206209958)
XLA Ops:
  8.4 4.2 %collective-permute-start.1 = (bf16[2,4,3,256]{3,2,1,0:T(4,128)(2,1)S(1)}, bf16[2,4,3,256]{3,2,1,0:T(4,128)(2,1)S(1)}, u32[]{:S(2)}, u32[]{:S(2)}) collective-permute-start(bf16[2,4,3,256]{3,2,1,0:T(4,128)(2,1)S(1)} %get-tuple-element.164), channel_id=1, source_target_pairs={{1,0},{2,1},{3,2},{0,3},{5,4},{6,5},{7,6},{4,7},{9,8},{10,9},{11,1... | collective-permute-start | bytes 36872 | tf_op jit(solution)/shard_map/ppermute | solution.py:31
  14.7 2.3 collective-permute-done
  17.1 5.1 %collective-permute-start.2 = (bf16[2,3,74,256]{3,2,1,0:T(8,128)(2,1)S(1)}, bf16[2,3,74,256]{3,2,1,0:T(8,128)(2,1)S(1)}, u32[]{:S(2)}, u32[]{:S(2)}) collective-permute-start(bf16[2,3,74,256]{3,2,1,0:T(8,128)(2,1)S(1)} %get-tuple-element.153), channel_id=1, source_target_pairs={{0,4},{4,8},{8,12},{1,5},{5,9},{9,13},{2,6},{6,10},{10,14},{3,7},{... | collective-permute-start | bytes 681992 | tf_op jit(solution)/shard_map/ppermute | solution.py:28
  22.3 1.9 collective-permute-start.3
  25.6 4.1 %collective-permute-done.3 = bf16[2,3,74,256]{3,2,1,0:T(8,128)(2,1)S(1)} collective-permute-done((bf16[2,3,74,256]{3,2,1,0:T(8,128)(2,1)S(1)}, bf16[2,3,74,256]{3,2,1,0:T(8,128)(2,1)S(1)}, u32[]{:S(2)}, u32[]{:S(2)}) %collective-permute-start.3) | collective-permute-done | bytes 227360 | tf_op jit(solution)/shard_map/ppermute | solution.py:31
  30.6 5.6 %fusion.257 = (f32[2,4,68]{2,1,0:T(4,128)S(1)}, f32[2,4,68,256]{3,2,1,0:T(8,128)S(1)}) fusion(f32[256]{0:T(256)} %bitcast.49, f32[256]{0:T(256)S(1)} %bitcast.332, bf16[2,7,74,256]{3,2,1,0:T(8,128)(2,1)S(1)} %get-tuple-element.152, f32[256]{0:T(256)S(1)} %bitcast.336, f32[256]{0:T(256)S(1)} %bitcast.224, f32[256]{0:T(256)S(1)} %bitcast.228, ...), kind=kLoop, calls=%fused_computation.622 | loop fusion | flops 23117280 | bytes 12611712 | tf_op jit(solution)/shard_map/reduce_sum | solution.py:77
  37.8 3.1 fusion.4
  41.9 2.0 convolution_add_fusion.1
  46.6 3.1 collective-permute-start.4
  49.8 3.6 %collective-permute-done.4 = bf16[2,4,68,256]{3,2,1,0:T(8,128)(2,1)S(1)} collective-permute-done((bf16[2,4,68,256]{3,2,1,0:T(8,128)(2,1)S(1)}, bf16[2,4,68,256]{3,2,1,0:T(8,128)(2,1)S(1)}, u32[]{:S(2)}, u32[]{:S(2)}) %collective-permute-start.4) | collective-permute-done | bytes 278560 | tf_op jit(solution)/shard_map/ppermute | solution.py:39
  56.1 1.9 collective-permute-done.5
  59.0 4.0 %collective-permute-start.7 = (bf16[2,3,74,256]{3,2,1,0:T(8,128)(2,1)}, bf16[2,3,74,256]{3,2,1,0:T(8,128)(2,1)S(1)}, u32[]{:S(2)}, u32[]{:S(2)}) collective-permute-start(bf16[2,3,74,256]{3,2,1,0:T(8,128)(2,1)} %get-tuple-element.149), channel_id=1, source_target_pairs={{0,4},{4,8},{8,12},{1,5},{5,9},{9,13},{2,6},{6,10},{10,14},{3,7},{... | collective-permute-start | bytes 681992 | tf_op jit(solution)/shard_map/ppermute | solution.py:28
  63.0 2.1 collective-permute-start.8
  67.2 3.6 %collective-permute-done.8 = bf16[2,3,74,256]{3,2,1,0:T(8,128)(2,1)S(1)} collective-permute-done((bf16[2,3,74,256]{3,2,1,0:T(8,128)(2,1)}, bf16[2,3,74,256]{3,2,1,0:T(8,128)(2,1)S(1)}, u32[]{:S(2)}, u32[]{:S(2)}) %collective-permute-start.8) | collective-permute-done | bytes 227360 | tf_op jit(solution)/shard_map/ppermute | solution.py:31
  71.8 5.6 %fusion.255 = (f32[2,4,68]{2,1,0:T(4,128)S(1)}, f32[2,4,68,256]{3,2,1,0:T(8,128)S(1)}) fusion(f32[256]{0:T(256)} %bitcast.49, f32[256]{0:T(256)S(1)} %bitcast.333, bf16[2,7,74,256]{3,2,1,0:T(8,128)(2,1)S(1)} %get-tuple-element.148, f32[256]{0:T(256)S(1)} %bitcast.337, f32[256]{0:T(256)S(1)} %bitcast.225, f32[256]{0:T(256)S(1)} %bitcast.229, ...), kind=kLoop, calls=%fused_computation.621 | loop fusion | flops 23117280 | bytes 12611712 | tf_op jit(solution)/shard_map/reduce_sum | solution.py:77
  78.8 4.7 %fusion.9 = (f32[544,1024]{1,0:T(8,128)S(1)}, bf16[544,1024]{1,0:T(8,128)(2,1)}) fusion(f32[544,1024]{1,0:T(8,128)} %get-tuple-element.224, f32[1024]{0:T(1024)} %bitcast.54, pred[]{:T(512)S(6)} %eq.3, bf16[544,256]{1,0:T(8,128)(2,1)S(1)} %reshape.2387, bf16[1,256,1024]{2,1,0:T(8,128)(2,1)S(1)} %copy-done), kind=kOutput, calls=%fused_computation.115 | convolution fusion | flops 301367296 | bytes 6377473 | tf_op jit(solution)/shard_map/dot_general | solution.py:86
  87.0 2.2 multiply_reduce_fusion.3
  100.2 3.0 collective-permute-start.11
  103.2 2.1 collective-permute-start.12
  105.4 1.9 convolution_add_fusion
  107.7 3.1 collective-permute-done.12
  111.3 4.7 %add_convert_fusion.1 = bf16[2,4,68,256]{3,2,1,0:T(8,128)(2,1)S(1)} fusion(bf16[2,4,68,256]{3,2,1,0:T(8,128)(2,1)S(1)} %get-tuple-element.130, bf16[2,4,3,256]{3,2,1,0:T(4,128)(2,1)S(1)} %collective-permute-done.10, bf16[2,4,3,256]{3,2,1,0:T(4,128)(2,1)S(1)} %collective-permute-done.9, bf16[2,7,74,256]{3,2,1,0:T(8,128)(2,1)S(1)} %get-tuple-element.144, ...), kind=kLoop, calls=%fused_computation.354 | loop fusion | flops 23535616 | bytes 12609601 | tf_op jit(solution)/shard_map/convert_element_type | solution.py:157
  117.4 1.9 reshape.2391
  120.4 3.2 %collective-permute-done.13 = bf16[2,4,68,256]{3,2,1,0:T(8,128)(2,1)S(1)} collective-permute-done((bf16[2,4,68,256]{3,2,1,0:T(8,128)(2,1)S(1)}, bf16[2,4,68,256]{3,2,1,0:T(8,128)(2,1)S(1)}, u32[]{:S(2)}, u32[]{:S(2)}) %collective-permute-start.13) | collective-permute-done | bytes 278560 | tf_op jit(solution)/shard_map/ppermute | solution.py:39
  123.6 2.0 multiply_reduce_fusion.2
  125.7 2.8 convert_reduce_fusion.2
  144.6 54.4 %all-reduce = (f32[1,49,256]{2,0,1:T(1,128)S(1)}, f32[1,5,256]{2,0,1:T(1,128)S(1)}, f32[1,1024]{1,0:T(1,128)S(1)}) all-reduce(f32[1,49,256]{2,0,1:T(1,128)S(1)} %multiply_add_fusion.3, f32[1,5,256]{2,0,1:T(1,128)S(1)} %multiply_add_fusion.4, f32[1,1024]{1,0:T(1,128)S(1)} %bitcast.416), channel_id=1, replica_groups=mesh['section'=2,'lat'=4,'lon'=4] {'lat','lon'}, use_global_device_ids=true, to_apply=%region_106.107 | all-reduce | flops 14848 | bytes 118784 | tf_op jit(solution)/shard_map/psum | solution.py:223
  199.8 8.7 %collective-permute-start.16 = (bf16[2,3,74,256]{3,2,1,0:T(8,128)(2,1)S(1)}, bf16[2,3,74,256]{3,2,1,0:T(8,128)(2,1)S(1)}, u32[]{:S(2)}, u32[]{:S(2)}) collective-permute-start(bf16[2,3,74,256]{3,2,1,0:T(8,128)(2,1)S(1)} %get-tuple-element.141), channel_id=1, source_target_pairs={{0,4},{4,8},{8,12},{1,5},{5,9},{9,13},{2,6},{6,10},{10,14},{3,7},{... | collective-permute-start | bytes 681992 | tf_op jit(solution)/shard_map/ppermute | solution.py:28
  212.1 4.1 %collective-permute-done.17 = bf16[2,3,74,256]{3,2,1,0:T(8,128)(2,1)S(1)} collective-permute-done((bf16[2,3,74,256]{3,2,1,0:T(8,128)(2,1)S(1)}, bf16[2,3,74,256]{3,2,1,0:T(8,128)(2,1)S(1)}, u32[]{:S(2)}, u32[]{:S(2)}) %collective-permute-start.17) | collective-permute-done | bytes 227360 | tf_op jit(solution)/shard_map/ppermute | solution.py:31
  216.6 5.5 %fusion.252 = bf16[1,2,4,68,256]{4,3,2,1,0:T(8,128)(2,1)S(1)} fusion(f32[2,4,68,256]{3,2,1,0:T(8,128)S(1)} %copy-done.5, f32[256]{0:T(256)} %bitcast.50, f32[4,68]{1,0:T(4,128)S(1)} %convert_element_type.1601, f32[256]{0:T(256)S(1)} %bitcast.223, bf16[2,7,74,256]{3,2,1,0:T(8,128)(2,1)S(1)} %get-tuple-element.140, f32[256]{0:T(256)S(1)} %bitcast.343, ...), kind=kLoop, calls=%fused_computation.427 | loop fusion | flops 24510464 | bytes 13446209 | tf_op jit(solution)/shard_map/broadcast_in_dim | solution.py:221
  222.9 82.5 %all-reduce.4.cloned.1.call-done = (f32[1,256,1024]{2,1,0:T(8,128)}, f32[1,1024,256]{2,1,0:T(8,128)}) async-done(((f32[1,256,1024]{2,1,0:T(8,128)}, f32[1,1024,256]{2,1,0:T(8,128)}), (f32[1,256,1024]{2,1,0:T(8,128)}, f32[1,1024,256]{2,1,0:T(8,128)})) %all-reduce.4.cloned.1.call-update) | async-done | bytes 2097168 | tf_op jit(solution)/shard_map/psum | solution.py:223
  305.4 2.4 broadcast_multiply_fusion.1
  (570 shorter events, 56.7 us)
Async XLA Ops:
  7.2 30.6 %copy-start = (bf16[1,256,1024]{2,1,0:T(8,128)(2,1)S(1)}, bf16[1,256,1024]{2,1,0:T(8,128)(2,1)}, u32[]{:S(2)}) copy-start(bf16[1,256,1024]{2,1,0:T(8,128)(2,1)} %param.13) | copy-start | bytes 1572868
  7.2 298.2 %all-reduce.4.cloned.1.call-start = ((), (), s32[]{:S(2)}) async-start(), calls=%async_computation | async-start | bytes 4194304 | tf_op jit(solution)/shard_map/psum | solution.py:223
  7.2 17.0 %copy-start.173 = (bf16[1,5,256]{2,1,0:T(8,128)(2,1)S(1)}, bf16[1,5,256]{2,1,0:T(8,128)(2,1)}, u32[]{:S(2)}) copy-start(bf16[1,5,256]{2,1,0:T(8,128)(2,1)} %param.12) | copy-start | bytes 7684
  7.2 17.5 %copy-start.182 = (bf16[1,1024]{1,0:T(2,128)(2,1)S(1)}, bf16[1,1024]{1,0:T(2,128)(2,1)}, u32[]{:S(2)}) copy-start(bf16[1,1024]{1,0:T(2,128)(2,1)} %param.14) | copy-start | bytes 6148
  7.3 18.1 %copy-start.184 = (s32[4,68]{1,0:T(4,128)S(1)}, s32[4,68]{1,0:T(4,128)}, u32[]{:S(2)}) copy-start(s32[4,68]{1,0:T(4,128)} %param.10) | copy-start | bytes 3268
  7.3 18.1 %copy-start.32 = (bf16[1,49,256]{2,1,0:T(8,128)(2,1)S(1)}, bf16[1,49,256]{2,1,0:T(8,128)(2,1)}, u32[]{:S(2)}) copy-start(bf16[1,49,256]{2,1,0:T(8,128)(2,1)} %param.11) | copy-start | bytes 75268
  8.4 6.3 %collective-permute-start.1 = (bf16[2,4,3,256]{3,2,1,0:T(4,128)(2,1)S(1)}, bf16[2,4,3,256]{3,2,1,0:T(4,128)(2,1)S(1)}, u32[]{:S(2)}, u32[]{:S(2)}) collective-permute-start(bf16[2,4,3,256]{3,2,1,0:T(4,128)(2,1)S(1)} %get-tuple-element.164), channel_id=1, source_target_pairs={{1,0},{2,1},{3,2},{0,3},{5,4},{6,5},{7,6},{4,7},{9,8},{10,9},{11,1... | collective-permute-start | bytes 36872 | tf_op jit(solution)/shard_map/ppermute | solution.py:31
  12.6 4.4 %collective-permute-start = (bf16[2,4,3,256]{3,2,1,0:T(4,128)(2,1)S(1)}, bf16[2,4,3,256]{3,2,1,0:T(4,128)(2,1)S(1)}, u32[]{:S(2)}, u32[]{:S(2)}) collective-permute-start(bf16[2,4,3,256]{3,2,1,0:T(4,128)(2,1)S(1)} %get-tuple-element.163), channel_id=1, source_target_pairs={{0,1},{1,2},{2,3},{3,0},{4,5},{5,6},{6,7},{7,4},{8,9},{9,10},{10,1... | collective-permute-start | bytes 36872 | tf_op jit(solution)/shard_map/ppermute | solution.py:28
  13.6 16.9 %copy-start.39 = (f32[1,1,256]{2,1,0:T(1,128)}, f32[1,1,256]{2,1,0:T(1,128)S(1)}, u32[]{:S(2)}) copy-start(f32[1,1,256]{2,1,0:T(1,128)S(1)} %get-tuple-element.180) | copy-start | bytes 3076
  13.6 16.9 %copy-start.42 = (f32[1,1,256]{2,1,0:T(1,128)}, f32[1,1,256]{2,1,0:T(1,128)S(1)}, u32[]{:S(2)}) copy-start(f32[1,1,256]{2,1,0:T(1,128)S(1)} %get-tuple-element.181) | copy-start | bytes 3076
  13.6 16.9 %copy-start.45 = (f32[1,1,256]{2,1,0:T(1,128)}, f32[1,1,256]{2,1,0:T(1,128)S(1)}, u32[]{:S(2)}) copy-start(f32[1,1,256]{2,1,0:T(1,128)S(1)} %get-tuple-element.182) | copy-start | bytes 3076
  13.6 16.9 %copy-start.48 = (f32[1,1,256]{2,1,0:T(1,128)}, f32[1,1,256]{2,1,0:T(1,128)S(1)}, u32[]{:S(2)}) copy-start(f32[1,1,256]{2,1,0:T(1,128)S(1)} %get-tuple-element.183) | copy-start | bytes 3076
  13.6 57.8 %copy-start.33 = (f32[1,1,256]{2,1,0:T(1,128)}, f32[1,1,256]{2,1,0:T(1,128)S(1)}, u32[]{:S(2)}) copy-start(f32[1,1,256]{2,1,0:T(1,128)S(1)} %get-tuple-element.177) | copy-start | bytes 3076
  13.6 57.8 %copy-start.35 = (f32[1,1,256]{2,1,0:T(1,128)}, f32[1,1,256]{2,1,0:T(1,128)S(1)}, u32[]{:S(2)}) copy-start(f32[1,1,256]{2,1,0:T(1,128)S(1)} %get-tuple-element.178) | copy-start | bytes 3076
  13.6 57.8 %copy-start.37 = (f32[1,1,256]{2,1,0:T(1,128)}, f32[1,1,256]{2,1,0:T(1,128)S(1)}, u32[]{:S(2)}) copy-start(f32[1,1,256]{2,1,0:T(1,128)S(1)} %get-tuple-element.179) | copy-start | bytes 3076
  17.1 8.5 %collective-permute-start.2 = (bf16[2,3,74,256]{3,2,1,0:T(8,128)(2,1)S(1)}, bf16[2,3,74,256]{3,2,1,0:T(8,128)(2,1)S(1)}, u32[]{:S(2)}, u32[]{:S(2)}) collective-permute-start(bf16[2,3,74,256]{3,2,1,0:T(8,128)(2,1)S(1)} %get-tuple-element.153), channel_id=1, source_target_pairs={{0,4},{4,8},{8,12},{1,5},{5,9},{9,13},{2,6},{6,10},{10,14},{3,7},{... | collective-permute-start | bytes 681992 | tf_op jit(solution)/shard_map/ppermute | solution.py:28
  22.3 7.5 %collective-permute-start.3 = (bf16[2,3,74,256]{3,2,1,0:T(8,128)(2,1)S(1)}, bf16[2,3,74,256]{3,2,1,0:T(8,128)(2,1)S(1)}, u32[]{:S(2)}, u32[]{:S(2)}) collective-permute-start(bf16[2,3,74,256]{3,2,1,0:T(8,128)(2,1)S(1)} %get-tuple-element.154), channel_id=1, source_target_pairs={{4,0},{8,4},{12,8},{5,1},{9,5},{13,9},{6,2},{10,6},{14,10},{7,3},{... | collective-permute-start | bytes 681992 | tf_op jit(solution)/shard_map/ppermute | solution.py:31
  45.0 32.4 %copy-start.4 = (f32[2,4,68,256]{3,2,1,0:T(8,128)}, f32[2,4,68,256]{3,2,1,0:T(8,128)S(1)}, u32[]{:S(2)}) copy-start(f32[2,4,68,256]{3,2,1,0:T(8,128)S(1)} %reshape.2385) | copy-start | bytes 1671172
  46.6 6.8 %collective-permute-start.4 = (bf16[2,4,68,256]{3,2,1,0:T(8,128)(2,1)S(1)}, bf16[2,4,68,256]{3,2,1,0:T(8,128)(2,1)S(1)}, u32[]{:S(2)}, u32[]{:S(2)}) collective-permute-start(bf16[2,4,68,256]{3,2,1,0:T(8,128)(2,1)S(1)} %get-tuple-element.222), channel_id=1, source_target_pairs={{0,16},{1,17},{2,18},{3,19},{4,20},{5,21},{6,22},{7,23},{8,24},{9,... | collective-permute-start | bytes 835592 | tf_op jit(solution)/shard_map/ppermute | solution.py:39
  53.5 2.6 collective-permute-start.6
  53.7 4.4 %collective-permute-start.5 = (bf16[2,4,3,256]{3,2,1,0:T(4,128)(2,1)S(1)}, bf16[2,4,3,256]{3,2,1,0:T(4,128)(2,1)S(1)}, u32[]{:S(2)}, u32[]{:S(2)}) collective-permute-start(bf16[2,4,3,256]{3,2,1,0:T(4,128)(2,1)S(1)} %get-tuple-element.161), channel_id=1, source_target_pairs={{0,1},{1,2},{2,3},{3,0},{4,5},{5,6},{6,7},{7,4},{8,9},{9,10},{10,1... | collective-permute-start | bytes 36872 | tf_op jit(solution)/shard_map/ppermute | solution.py:28
  59.0 8.2 %collective-permute-start.7 = (bf16[2,3,74,256]{3,2,1,0:T(8,128)(2,1)}, bf16[2,3,74,256]{3,2,1,0:T(8,128)(2,1)S(1)}, u32[]{:S(2)}, u32[]{:S(2)}) collective-permute-start(bf16[2,3,74,256]{3,2,1,0:T(8,128)(2,1)} %get-tuple-element.149), channel_id=1, source_target_pairs={{0,4},{4,8},{8,12},{1,5},{5,9},{9,13},{2,6},{6,10},{10,14},{3,7},{... | collective-permute-start | bytes 681992 | tf_op jit(solution)/shard_map/ppermute | solution.py:28
  63.0 7.7 %collective-permute-start.8 = (bf16[2,3,74,256]{3,2,1,0:T(8,128)(2,1)}, bf16[2,3,74,256]{3,2,1,0:T(8,128)(2,1)S(1)}, u32[]{:S(2)}, u32[]{:S(2)}) collective-permute-start(bf16[2,3,74,256]{3,2,1,0:T(8,128)(2,1)} %get-tuple-element.150), channel_id=1, source_target_pairs={{4,0},{8,4},{12,8},{5,1},{9,5},{13,9},{6,2},{10,6},{14,10},{7,3},{... | collective-permute-start | bytes 681992 | tf_op jit(solution)/shard_map/ppermute | solution.py:31
  95.7 2.6 collective-permute-start.10
  95.7 4.4 %collective-permute-start.9 = (bf16[2,4,3,256]{3,2,1,0:T(4,128)(2,1)S(1)}, bf16[2,4,3,256]{3,2,1,0:T(4,128)(2,1)S(1)}, u32[]{:S(2)}, u32[]{:S(2)}) collective-permute-start(bf16[2,4,3,256]{3,2,1,0:T(4,128)(2,1)S(1)} %get-tuple-element.159), channel_id=1, source_target_pairs={{0,1},{1,2},{2,3},{3,0},{4,5},{5,6},{6,7},{7,4},{8,9},{9,10},{10,1... | collective-permute-start | bytes 36872 | tf_op jit(solution)/shard_map/ppermute | solution.py:28
  100.2 7.5 %collective-permute-start.11 = (bf16[2,3,74,256]{3,2,1,0:T(8,128)(2,1)S(1)}, bf16[2,3,74,256]{3,2,1,0:T(8,128)(2,1)S(1)}, u32[]{:S(2)}, u32[]{:S(2)}) collective-permute-start(bf16[2,3,74,256]{3,2,1,0:T(8,128)(2,1)S(1)} %get-tuple-element.145), channel_id=1, source_target_pairs={{0,4},{4,8},{8,12},{1,5},{5,9},{9,13},{2,6},{6,10},{10,14},{3,7},{... | collective-permute-start | bytes 681992 | tf_op jit(solution)/shard_map/ppermute | solution.py:28
  103.2 7.5 %collective-permute-start.12 = (bf16[2,3,74,256]{3,2,1,0:T(8,128)(2,1)S(1)}, bf16[2,3,74,256]{3,2,1,0:T(8,128)(2,1)S(1)}, u32[]{:S(2)}, u32[]{:S(2)}) collective-permute-start(bf16[2,3,74,256]{3,2,1,0:T(8,128)(2,1)S(1)} %get-tuple-element.146), channel_id=1, source_target_pairs={{4,0},{8,4},{12,8},{5,1},{9,5},{13,9},{6,2},{10,6},{14,10},{7,3},{... | collective-permute-start | bytes 681992 | tf_op jit(solution)/shard_map/ppermute | solution.py:31
  116.0 7.6 %collective-permute-start.13 = (bf16[2,4,68,256]{3,2,1,0:T(8,128)(2,1)S(1)}, bf16[2,4,68,256]{3,2,1,0:T(8,128)(2,1)S(1)}, u32[]{:S(2)}, u32[]{:S(2)}) collective-permute-start(bf16[2,4,68,256]{3,2,1,0:T(8,128)(2,1)S(1)} %add_convert_fusion.1), channel_id=1, source_target_pairs={{16,0},{17,1},{18,2},{19,3},{20,4},{21,5},{22,6},{23,7},{24,8},{25... | collective-permute-start | bytes 835592 | tf_op jit(solution)/shard_map/ppermute | solution.py:39
  138.9 60.7 %collective-permute-start.15 = (bf16[2,4,3,256]{3,2,1,0:T(4,128)(2,1)S(1)}, bf16[2,4,3,256]{3,2,1,0:T(4,128)(2,1)S(1)}, u32[]{:S(2)}, u32[]{:S(2)}) collective-permute-start(bf16[2,4,3,256]{3,2,1,0:T(4,128)(2,1)S(1)} %get-tuple-element.158), channel_id=1, source_target_pairs={{1,0},{2,1},{3,2},{0,3},{5,4},{6,5},{7,6},{4,7},{9,8},{10,9},{11,1... | collective-permute-start | bytes 36872 | tf_op jit(solution)/shard_map/ppermute | solution.py:31
  139.0 60.7 %collective-permute-start.14 = (bf16[2,4,3,256]{3,2,1,0:T(4,128)(2,1)S(1)}, bf16[2,4,3,256]{3,2,1,0:T(4,128)(2,1)S(1)}, u32[]{:S(2)}, u32[]{:S(2)}) collective-permute-start(bf16[2,4,3,256]{3,2,1,0:T(4,128)(2,1)S(1)} %get-tuple-element.157), channel_id=1, source_target_pairs={{0,1},{1,2},{2,3},{3,0},{4,5},{5,6},{6,7},{7,4},{8,9},{9,10},{10,1... | collective-permute-start | bytes 36872 | tf_op jit(solution)/shard_map/ppermute | solution.py:28
  199.8 12.2 %collective-permute-start.16 = (bf16[2,3,74,256]{3,2,1,0:T(8,128)(2,1)S(1)}, bf16[2,3,74,256]{3,2,1,0:T(8,128)(2,1)S(1)}, u32[]{:S(2)}, u32[]{:S(2)}) collective-permute-start(bf16[2,3,74,256]{3,2,1,0:T(8,128)(2,1)S(1)} %get-tuple-element.141), channel_id=1, source_target_pairs={{0,4},{4,8},{8,12},{1,5},{5,9},{9,13},{2,6},{6,10},{10,14},{3,7},{... | collective-permute-start | bytes 681992 | tf_op jit(solution)/shard_map/ppermute | solution.py:28
  208.5 7.6 %collective-permute-start.17 = (bf16[2,3,74,256]{3,2,1,0:T(8,128)(2,1)S(1)}, bf16[2,3,74,256]{3,2,1,0:T(8,128)(2,1)S(1)}, u32[]{:S(2)}, u32[]{:S(2)}) collective-permute-start(bf16[2,3,74,256]{3,2,1,0:T(8,128)(2,1)S(1)} %get-tuple-element.142), channel_id=1, source_target_pairs={{4,0},{8,4},{12,8},{5,1},{9,5},{13,9},{6,2},{10,6},{14,10},{7,3},{... | collective-permute-start | bytes 681992 | tf_op jit(solution)/shard_map/ppermute | solution.py:31
  (174 other events, 942.2 us)
Sparse Core Ops, SparseCore 0:
  211.2 94.1 all-reduce.3
where the time goes:
time: 318 us; the launch traced here: 316 us
  waiting for transfers between devices  111 us (35%)
  blocking collectives  54.4 us (17%)
  other arithmetic  51.7 us (16%)
  starting transfers between devices  42.1 us (13%)
  matrix products  23.5 us (7%)
  between operations  17.3 us (5%)
  local copies, waits for them, and re-layouts  15.5 us (5%)
    psum x1, waiting for transfers between devices, on_device(): lax.psum((owned[0], owned[1], owned[2], owned[3], owned[4]), ('lat', 'lon'))  82.5 us
    psum x1, blocking collectives, on_device(): lax.psum((owned[0], owned[1], owned[2], owned[3], owned[4]), ('lat', 'lon'))  54.4 us
    ppermute x8, starting transfers between devices, padded_2(): lax.ppermute(lax.slice_in_dim(block, block.shape[dim] - width, None, axis...  25.1 us
    ppermute x8, waiting for transfers between devices, padded_2(): lax.ppermute(lax.slice_in_dim(block, 0, width, axis=dim), axis, backward)  16 us
    ppermute x8, starting transfers between devices, padded_2(): lax.ppermute(lax.slice_in_dim(block, 0, width, axis=dim), axis, backward)  12.5 us
    reduce_sum x2, other arithmetic, cell_forward(): average = jnp.mean(conv_out, axis=-1, keepdims=True)  11.3 us
    reduce_sum x6, other arithmetic, kernel_grads(): tap_sums.append(jnp.sum((grad_wide * window).reshape(-1, channels), axis=0))  9.19 us
    dot_general x2, matrix products, cell_forward(): jnp.dot(flat_rows, w_up, preferred_element_type=jnp.float32)  7.83 us
  transfers between devices with their start and end apart: 19, of which 11 were waited for; matrix products, arithmetic and copies ran while one was open for 7% of the time, Pallas kernels for 0%

commit v1 on v0

v1 whole, which is shorter than its diff:
```python
import functools
import math

import jax
import jax.numpy as jnp
from jax import lax
from jax.experimental import pallas as pl
from jax.experimental.pallas import tpu as pltpu
from jax.sharding import PartitionSpec as P

KERNEL = 7
TAPS = KERNEL * KERNEL
REACH = KERNEL // 2
ROWS_DEV = 4
COLS_DEV = 68
BATCH = 2
HALF = 128
WIDE = 256
HID = 1024
QUARTERS = HID // WIDE
SIDE_X, SIDE_0, SIDE_1 = 12, 9, 6
W_X, W_0, W_1, W_OWN = 96, 88, 80, 72
CHUNK = 32
SMALL = 64

norm_eps = 1e-06
gelu_scale = 0.7978845608028654
gelu_cubic = 0.044715
f32, bf16 = jnp.float32, jnp.bfloat16

nn = (((1,), (0,)), ((), ()))
nt = (((1,), (1,)), ((), ()))
tn = (((0,), (0,)), ((), ()))


def dot(left, right, dims=nn):
    return lax.dot_general(left, right, dims, preferred_element_type=f32)


def lanes(half):
    return slice(half * HALF, (half + 1) * HALF)


def load_padded(pad, odd, center, first, second, offset=0):
    width = center.shape[1]

    def put(row, value):
        value = value.astype(f32)
        for half in range(2):
            pad[half, row, offset : offset + width, :] = value[:, lanes(half)]

    at_first = jnp.where(odd == 1, 0, REACH + ROWS_DEV)
    at_second = jnp.where(odd == 1, REACH + ROWS_DEV, 0)
    for row in range(ROWS_DEV):
        put(REACH + row, center[row])
    for row in range(REACH):
        put(at_first + row, first[row])
        put(at_second + row, second[row])


def load_taps(taps, small):
    for half in range(2):
        taps[half] = jnp.broadcast_to(small[0:TAPS, lanes(half)][:, None, :], (TAPS, 8, HALF))


def conv_tile(pad, taps, half, start, reverse):
    sums = [None] * ROWS_DEV
    for row in range(ROWS_DEV + KERNEL - 1):
        for col_off in range(KERNEL):
            window = pad[half, row, start + col_off : start + col_off + 8, :]
            for out_row in range(ROWS_DEV):
                row_off = row - out_row
                if 0 <= row_off < KERNEL:
                    tap = row_off * KERNEL + col_off
                    term = window * taps[half, TAPS - 1 - tap if reverse else tap]
                    sums[out_row] = term if sums[out_row] is None else sums[out_row] + term
    return sums


def chunks(count, body, start=0):
    return lax.fori_loop(0, count // CHUNK, lambda i, carry: body(pl.ds(pl.multiple_of(i * CHUNK, CHUNK), CHUNK), carry), start)


def fold(value):
    return jnp.sum(value.reshape(CHUNK // 8, 8, value.shape[-1]), axis=0)


def twice(value):
    return jnp.concatenate([value, value], axis=1)


def send_rows(odd, source, send_first, send_second):
    first, second = jnp.where(odd == 1, 0, 1), jnp.where(odd == 1, 1, 0)
    send_first[...] = source[pl.ds(first, REACH)]
    send_second[...] = source[pl.ds(second, REACH)]


def forward_cells(width, pad, taps, small, mask, w_up, w_down, normed, inverse, z, hidden, active, slope, branch, out):
    count = ROWS_DEV * width
    load_taps(taps, small)
    for tile in range(width // 8):
        start = tile * 8
        halves = [conv_tile(pad, taps, half, start, False) for half in range(2)]
        for row in range(ROWS_DEV):
            u = [halves[half][row] + small[TAPS : TAPS + 1, lanes(half)] for half in range(2)]
            mean = jnp.sum(u[0] + u[1], axis=-1, keepdims=True) * (1.0 / WIDE)
            u = [value - mean for value in u]
            spread = jnp.sum(u[0] * u[0] + u[1] * u[1], axis=-1, keepdims=True) * (1.0 / WIDE)
            scale = lax.rsqrt(spread + norm_eps)
            at = slice(row * width + start, row * width + start + 8)
            inverse[at, :] = jnp.broadcast_to(scale, (8, HALF))
            for half in range(2):
                normed[at, lanes(half)] = u[half] * scale

    def scaled(at, carry):
        z[at, :] = (normed[at, :] * small[TAPS + 1 : TAPS + 2, :] + small[TAPS + 2 : TAPS + 3, :]).astype(bf16)
        return carry

    chunks(count, scaled, 0)
    for quarter in range(QUARTERS):
        cols = slice(quarter * WIDE, (quarter + 1) * WIDE)
        hidden[...] = dot(z[...], w_up[:, cols])
        bias = small[TAPS + 5 + quarter : TAPS + 6 + quarter, :]

        def gelu(at, carry):
            h = hidden[at, :] + bias
            square = h * h
            tangent = jnp.tanh(h * (gelu_scale + (gelu_scale * gelu_cubic) * square))
            above = 0.5 + 0.5 * tangent
            active[at, cols] = (h * above).astype(bf16)
            slope[at, cols] = above + (0.5 * h) * (1.0 - tangent * tangent) * (
                gelu_scale + (3.0 * gelu_scale * gelu_cubic) * square
            )
            return carry

        chunks(count, gelu, 0)
    branch[...] = dot(active[...], w_down[...]) + small[TAPS + 3 : TAPS + 4, :]
    for row in range(ROWS_DEV):
        for tile in range(width // 8):
            start = tile * 8
            at = slice(row * width + start, row * width + start + 8)
            for half in range(2):
                value = pad[half, REACH + row, start + REACH : start + REACH + 8, :]
                gain = small[TAPS + 4 : TAPS + 5, lanes(half)]
                out[at, lanes(half)] = mask[at, :] * (value + gain * branch[at, lanes(half)])


def backward_cells(
    width, odd, small, own, own_row, upstream, w_up, w_down, normed, inverse, z, active, slope, branch, hidden, dm, dh, du, keep, send, sums
):
    count = ROWS_DEV * width
    zero = jnp.zeros((8, WIDE), f32)

    def first(at, carry):
        sum_dm, sum_em = carry
        e = upstream[at, :]
        inside = twice(own[at, :])
        grad = (e * small[TAPS + 4 : TAPS + 5, :]).astype(bf16)
        dm[at, :] = grad
        sum_dm = sum_dm + fold(grad.astype(f32) * inside)
        sum_em = sum_em + fold(e * branch[at, :] * inside)
        return sum_dm, sum_em

    sum_dm, sum_em = chunks(count, first, (zero, zero))
    for quarter in range(QUARTERS):
        cols = slice(quarter * WIDE, (quarter + 1) * WIDE)
        hidden[...] = dot(dm[...], w_down[cols, :], nt)

        def through(at, carry):
            dh[at, cols] = (hidden[at, :] * slope[at, cols]).astype(bf16)
            return carry

        chunks(count, through, 0)
    hidden[...] = dot(dh[...], w_up[...], nt)
    sum_dh = dot(own_row[...], dh[...])

    def norm(at, carry):
        sum_dzn, sum_dz, sum_du = carry
        dz = hidden[at, :]
        normal = normed[at, :]
        inside = twice(own[at, :])
        inner = dz * inside
        sum_dz = sum_dz + fold(inner)
        sum_dzn = sum_dzn + fold(inner * normal)
        dn = dz * small[TAPS + 1 : TAPS + 2, :]
        mean = jnp.sum(dn, axis=-1, keepdims=True) * (1.0 / WIDE)
        slant = jnp.sum(dn * normal, axis=-1, keepdims=True) * (1.0 / WIDE)
        grad = (twice(inverse[at, :]) * (dn - mean - normal * slant)).astype(bf16).astype(f32)
        du[at, :] = grad
        sum_du = sum_du + fold(grad * inside)
        dm[at, :] = (dm[at, :].astype(f32) * inside).astype(bf16)
        z[at, :] = (z[at, :].astype(f32) * inside).astype(bf16)
        return sum_dzn, sum_dz, sum_du

    sum_dzn, sum_dz, sum_du = chunks(count, norm, (zero, zero, zero))
    rows = [jnp.sum(value, axis=0, keepdims=True) for value in (sum_du, sum_dzn, sum_dz, sum_dm, sum_em)]
    rows += [sum_dh[0:1, quarter * WIDE : (quarter + 1) * WIDE] for quarter in range(QUARTERS)]
    for index, value in enumerate(rows):
        sums[index : index + 1, :] = value
    sums[len(rows) : 16, :] = jnp.zeros((16 - len(rows), WIDE), f32)

    def weights(up_ref, down_ref):
        for quarter in range(QUARTERS):
            cols = slice(quarter * WIDE, (quarter + 1) * WIDE)
            up_ref[cols, :] = dot(z[...], dh[:, cols], tn).astype(bf16)
            down_ref[cols, :] = dot(active[:, cols], dm[...], tn).astype(bf16)

    @pl.when(odd == 0)
    def _():
        weights(keep, send)

    @pl.when(odd == 1)
    def _():
        weights(send, keep)


def pick_weights(block, flags, own_up, own_down, got_up, got_down, other_up, other_down, w_up, w_down):
    odd, section = flags[0], flags[1]

    @pl.when(section == block)
    def _():
        w_up[...] = own_up[...]
        w_down[...] = own_down[...]

    @pl.when(section != block)
    def _():
        for ref, mine, other in ((w_up, got_up, other_up), (w_down, got_down, other_down)):
            half = mine.shape[0]
            ref[pl.ds(pl.multiple_of(odd * half, half), half), :] = mine[...]
            ref[pl.ds(pl.multiple_of((1 - odd) * half, half), half), :] = other[...]


def write_rows(source, width, out):
    for row in range(ROWS_DEV):
        out[row] = source[row * width : (row + 1) * width, :].astype(bf16)


def first_forward(
    flags, x, x_a, x_b, small, mask, own_up, own_down, got_up, got_down, other_up, other_down,
    y, send_a, send_b, normed, inverse, z, active, slope, branch, w_up, w_down,
    pad, taps, hidden, out,
):
    load_padded(pad, flags[0], x, x_a, x_b)
    pick_weights(0, flags, own_up, own_down, got_up, got_down, other_up, other_down, w_up, w_down)
    forward_cells(W_0, pad, taps, small, mask, w_up, w_down, normed, inverse, z, hidden, active, slope, branch, out)
    write_rows(out, W_0, y)
    send_rows(flags[0], y, send_a, send_b)


def second_block(
    flags, y, y_a, y_b, small, mask, own, own_row, upstream_in, own_up, own_down, got_up, got_down, other_up, other_down,
    final, du_out, send_a, send_b, keep, send, sums,
    pad, taps, hidden, out, normed, inverse, z, active, slope, branch, w_up, w_down, upstream, dm, dh, du,
):
    load_padded(pad, flags[0], y, y_a, y_b)
    pick_weights(1, flags, own_up, own_down, got_up, got_down, other_up, other_down, w_up, w_down)
    forward_cells(W_1, pad, taps, small, mask, w_up, w_down, normed, inverse, z, hidden, active, slope, branch, out)
    for row in range(ROWS_DEV):
        at = row * W_1 + SIDE_1
        final[row] = out[at : at + COLS_DEV, :].astype(bf16)
        upstream[row * W_1 : (row + 1) * W_1, :] = upstream_in[row].astype(f32)
    backward_cells(
        W_1, flags[0], small, own, own_row, upstream, w_up, w_down, normed, inverse, z, active, slope, branch, hidden, dm, dh, du, keep, send, sums
    )
    write_rows(du, W_1, du_out)
    send_rows(flags[0], du_out, send_a, send_b)


def first_backward(
    flags, du1, du1_a, du1_b, small1, small0, mask, own, own_row, upstream_in, normed, inverse, z_in, active, slope, branch, w_up, w_down,
    e_own, du_out, send_a, send_b, keep, send, sums,
    pad, taps, hidden, upstream, z, dm, dh, du,
):
    shift = SIDE_0 + REACH - SIDE_1
    pad[:, :, 0:8, :] = jnp.zeros((2, ROWS_DEV + 2 * REACH, 8, HALF), f32)
    pad[:, :, W_X - 16 : W_X, :] = jnp.zeros((2, ROWS_DEV + 2 * REACH, 16, HALF), f32)
    load_padded(pad, flags[0], du1, du1_a, du1_b, shift)
    load_taps(taps, small1)
    for row in range(ROWS_DEV):
        upstream[row * W_0 : (row + 1) * W_0, :] = upstream_in[row].astype(f32)
    for tile in range(W_0 // 8):
        start = tile * 8
        for half in range(2):
            spread = conv_tile(pad, taps, half, start, True)
            for row in range(ROWS_DEV):
                at = slice(row * W_0 + start, row * W_0 + start + 8)
                value = (upstream[at, lanes(half)] + spread[row]).astype(bf16).astype(f32)
                upstream[at, lanes(half)] = mask[at, :] * value
    for row in range(ROWS_DEV):
        at = row * W_0 + SIDE_0
        e_own[row] = upstream[at : at + W_OWN, :]
    z[...] = z_in[...]
    backward_cells(
        W_0, flags[0], small0, own, own_row, upstream, w_up, w_down, normed, inverse, z, active, slope, branch, hidden, dm, dh, du, keep, send, sums
    )
    write_rows(du, W_0, du_out)
    send_rows(flags[0], du_out, send_a, send_b)


def input_grad(flags, du, du_a, du_b, small, e_own, out, pad, taps, total):
    load_padded(pad, flags[0], du, du_a, du_b)
    load_taps(taps, small)
    for tile in range(W_OWN // 8):
        start = tile * 8
        for half in range(2):
            spread = conv_tile(pad, taps, half, start + SIDE_0 - REACH, True)
            for row in range(ROWS_DEV):
                at = slice(start, start + 8)
                total[row, at, lanes(half)] = e_own[row, at, lanes(half)] + spread[row]
    for row in range(ROWS_DEV):
        out[row] = total[row, 0:COLS_DEV, :].astype(bf16)


def tap_grads(width, flags, v, v_a, v_b, du, own, sums, out, pad, grads, total):
    load_padded(pad, flags[0], v, v_a, v_b)
    for row in range(ROWS_DEV):
        inside = own[row * width : (row + 1) * width, :]
        grads[row] = du[row].astype(f32) * twice(inside)
    total[...] = jnp.zeros((SMALL, WIDE), f32)
    for half in range(2):
        for col_off in range(KERNEL):
            partial = [None] * KERNEL
            for tile in range(width // 8):
                start = tile * 8
                grad = [grads[row, start : start + 8, lanes(half)] for row in range(ROWS_DEV)]
                for row in range(ROWS_DEV + KERNEL - 1):
                    window = pad[half, row, start + col_off : start + col_off + 8, :]
                    for out_row in range(ROWS_DEV):
                        row_off = row - out_row
                        if 0 <= row_off < KERNEL:
                            term = window * grad[out_row]
                            partial[row_off] = term if partial[row_off] is None else partial[row_off] + term
            for row_off in range(KERNEL):
                tap = row_off * KERNEL + col_off
                total[tap : tap + 1, lanes(half)] = jnp.sum(partial[row_off], axis=0, keepdims=True)
    total[TAPS : TAPS + 9, :] = sums[0:9, :]
    out[...] = total[...].astype(bf16)


def in_vmem():
    return pl.BlockSpec(memory_space=pltpu.VMEM)


def call(body, name, inputs, outputs, scratch, flops):
    return pl.pallas_call(
        body,
        name=name,
        out_shape=[jax.ShapeDtypeStruct(shape, dtype) for shape, dtype in outputs],
        in_specs=[pl.BlockSpec(memory_space=pltpu.SMEM)] + [in_vmem()] * (len(inputs) - 1),
        out_specs=[in_vmem()] * len(outputs),
        scratch_shapes=[pltpu.VMEM(shape, dtype) for shape, dtype in scratch],
        compiler_params=pltpu.CompilerParams(vmem_limit_bytes=56 << 20),
        cost_estimate=pl.CostEstimate(flops=flops, bytes_accessed=4 << 20, transcendentals=0),
    )(*inputs)


def swap_pairs(count, bit):
    return [(i, i ^ bit) for i in range(count)]


def on_device(
    window_input,
    output_cotangent,
    ocean_mask,
    dw_kernel,
    channel_params,
    up_weight,
    up_bias,
    down_weight,
):
    section = lax.axis_index("section")
    lat = lax.axis_index("lat")
    lon = lax.axis_index("lon")
    n_lat, n_lon = lax.axis_size("lat"), lax.axis_size("lon")
    odd = lat % 2
    flags = jnp.stack([odd, section]).astype(jnp.int32)
    channels = window_input.shape[-1]

    def over_section(value):
        return lax.ppermute(value, "section", [(0, 1), (1, 0)])

    def over_core(value):
        return lax.ppermute(value, "lat", swap_pairs(n_lat, 1))

    def lat_halo(send_a, send_b):
        pairs = [(i, i + 1) for i in range(1, n_lat - 1, 2)]
        pairs += [(j, i) for i, j in pairs]
        return over_core(send_a), lax.ppermute(send_b, "lat", pairs)

    def by_core(even, other):
        return jnp.where(odd == 0, even, other)

    small_own = jnp.concatenate(
        [dw_kernel[0], channel_params[0], up_bias[0].reshape(QUARTERS, WIDE), jnp.zeros((SMALL - TAPS - 9, WIDE), bf16)], axis=0
    )
    small_got = over_section(small_own)
    up, down = up_weight[0], down_weight[0]
    got_up = over_section(by_core(up[: channels // 2], up[channels // 2 :]))
    got_down = over_section(by_core(down[: HID // 2], down[HID // 2 :]))
    small_0 = jnp.where(section == 0, small_own, small_got).astype(f32)
    small_1 = jnp.where(section == 0, small_got, small_own).astype(f32)

    x = lax.dynamic_index_in_dim(window_input, section, 0, False)
    cot = lax.dynamic_index_in_dim(output_cotangent, section, 0, False)
    sea = ocean_mask.astype(bf16)

    def packed(x_part, cot_part, sea_part):
        sea_row = jnp.pad(sea_part, ((0, 0), (0, channels - sea_part.shape[1])))[:, None, :]
        return jnp.concatenate([x_part, cot_part, sea_row], axis=1)

    ring = [(i, (i + 1) % n_lon) for i in range(n_lon)]
    left = lax.ppermute(packed(x[:, -SIDE_X:], cot[:, -SIDE_1:], sea[:, -SIDE_0:]), "lon", ring)
    right = lax.ppermute(packed(x[:, :SIDE_X], cot[:, :SIDE_1], sea[:, :SIDE_0]), "lon", [(j, i) for i, j in ring])
    cot_at, sea_at = SIDE_X, SIDE_X + SIDE_1
    x_wide = jnp.concatenate([left[:, :SIDE_X], x, right[:, :SIDE_X], jnp.zeros((ROWS_DEV, W_X - COLS_DEV - 2 * SIDE_X, channels), bf16)], axis=1)
    x_a, x_b = lat_halo(by_core(x_wide[1:], x_wide[:REACH]), by_core(x_wide[:REACH], x_wide[1:]))
    mask_wide = jnp.concatenate(
        [left[:, sea_at, :SIDE_0], sea, right[:, sea_at, :SIDE_0], jnp.zeros((ROWS_DEV, W_0 - COLS_DEV - 2 * SIDE_0), bf16)], axis=1
    )
    before = SIDE_0 - SIDE_1
    cot_wide = jnp.concatenate(
        [
            jnp.zeros((ROWS_DEV, before, channels), bf16),
            left[:, cot_at:sea_at],
            cot,
            right[:, cot_at:sea_at],
            jnp.zeros((ROWS_DEV, W_0 - COLS_DEV - SIDE_1 - SIDE_0, channels), bf16),
        ],
        axis=1,
    )
    e_0 = cot_wide * mask_wide[:, :, None]
    e_1 = e_0[:, before : before + W_1]

    def spread_lanes(mask):
        flat = mask.astype(f32).reshape(-1, 1)
        return jnp.broadcast_to(flat, (flat.shape[0], HALF))

    mask_0, mask_1 = spread_lanes(mask_wide), spread_lanes(mask_wide[:, before : before + W_1])

    def own_cells(width, side):
        column = jnp.arange(width)
        inside = ((column >= side) & (column < side + COLS_DEV)).astype(f32)
        flat = jnp.tile(inside, ROWS_DEV)
        return jnp.broadcast_to(flat[:, None], (flat.shape[0], HALF)), jnp.broadcast_to(flat[None, :], (16, flat.shape[0])).astype(bf16)

    own_0, row_0 = own_cells(W_0, SIDE_0)
    own_1, row_1 = own_cells(W_1, SIDE_1)
    other_up, other_down = over_core(got_up), over_core(got_down)
    weights = (up, down, got_up, got_down, other_up, other_down)

    n_0, n_1 = ROWS_DEV * W_0, ROWS_DEV * W_1
    deep = ROWS_DEV + 2 * REACH
    taps_scratch = ((2, TAPS, 8, HALF), f32)

    y, y_send_a, y_send_b, normed, inverse, z, active, slope, branch, w_up, w_down = call(
        first_forward,
        "first_forward",
        (flags, x_wide, x_a, x_b, small_0, mask_0) + weights,
        [
            ((ROWS_DEV, W_0, WIDE), bf16), ((REACH, W_0, WIDE), bf16), ((REACH, W_0, WIDE), bf16),
            ((n_0, WIDE), f32), ((n_0, HALF), f32), ((n_0, WIDE), bf16), ((n_0, HID), bf16), ((n_0, HID), f32), ((n_0, WIDE), f32),
            ((WIDE, HID), bf16), ((HID, WIDE), bf16),
        ],
        [((2, deep, W_X, HALF), f32), taps_scratch, ((n_0, WIDE), f32), ((n_0, WIDE), f32)],
        2_000_000_000,
    )
    y_a, y_b = lat_halo(y_send_a, y_send_b)
    final, du1, du1_send_a, du1_send_b, keep_1, send_1, sums_1 = call(
        second_block,
        "second_block",
        (flags, y, y_a, y_b, small_1, mask_1, own_1, row_1, e_1) + weights,
        [
            ((ROWS_DEV, COLS_DEV, WIDE), bf16), ((ROWS_DEV, W_1, WIDE), bf16), ((REACH, W_1, WIDE), bf16), ((REACH, W_1, WIDE), bf16),
            ((HID, WIDE), bf16), ((HID, WIDE), bf16), ((16, WIDE), f32),
        ],
        [
            ((2, deep, W_0, HALF), f32), taps_scratch, ((n_1, WIDE), f32), ((n_1, WIDE), f32),
            ((n_1, WIDE), f32), ((n_1, HALF), f32), ((n_1, WIDE), bf16), ((n_1, HID), bf16), ((n_1, HID), f32), ((n_1, WIDE), f32),
            ((WIDE, HID), bf16), ((HID, WIDE), bf16), ((n_1, WIDE), f32), ((n_1, WIDE), bf16), ((n_1, HID), bf16), ((n_1, WIDE), f32),
        ],
        4_000_000_000,
    )
    du1_a, du1_b = lat_halo(du1_send_a, du1_send_b)
    e_own, du0, du0_send_a, du0_send_b, keep_0, send_0, sums_0 = call(
        first_backward,
        "first_backward",
        (flags, du1, du1_a, du1_b, small_1, small_0, mask_0, own_0, row_0, e_0, normed, inverse, z, active, slope, branch, w_up, w_down),
        [
            ((ROWS_DEV, W_OWN, WIDE), f32), ((ROWS_DEV, W_0, WIDE), bf16), ((REACH, W_0, WIDE), bf16), ((REACH, W_0, WIDE), bf16),
            ((HID, WIDE), bf16), ((HID, WIDE), bf16), ((16, WIDE), f32),
        ],
        [
            ((2, deep, W_X, HALF), f32), taps_scratch, ((n_0, WIDE), f32), ((n_0, WIDE), f32), ((n_0, WIDE), bf16),
            ((n_0, WIDE), bf16), ((n_0, HID), bf16), ((n_0, WIDE), f32),
        ],
        3_000_000_000,
    )
    du0_a, du0_b = lat_halo(du0_send_a, du0_send_b)
    (taps_1,) = call(
        functools.partial(tap_grads, W_1), "tap_grads_1", (flags, y, y_a, y_b, du1, own_1, sums_1), [((SMALL, WIDE), bf16)],
        [((2, deep, W_0, HALF), f32), ((ROWS_DEV, W_1, WIDE), f32), ((SMALL, WIDE), f32)], 2_000_000_000,
    )
    (taps_0,) = call(
        functools.partial(tap_grads, W_0), "tap_grads_0", (flags, x_wide, x_a, x_b, du0, own_0, sums_0), [((SMALL, WIDE), bf16)],
        [((2, deep, W_X, HALF), f32), ((ROWS_DEV, W_0, WIDE), f32), ((SMALL, WIDE), f32)], 2_000_000_000,
    )
    (start,) = call(
        input_grad, "input_grad", (flags, du0, du0_a, du0_b, small_0, e_own), [((ROWS_DEV, COLS_DEV, WIDE), bf16)],
        [((2, deep, W_0, HALF), f32), taps_scratch, ((ROWS_DEV, W_OWN, WIDE), f32)], 2_000_000_000,
    )

    bits = [("lat", 1 << i) for i in range(1, n_lat.bit_length() - 1)] + [("lon", 1 << i) for i in range(n_lon.bit_length() - 1)]
    orders = (bits, bits[1:] + bits[:1])

    def partner(place, step):
        row, col = place
        axis, bit = orders[row % 2][step]
        return (row ^ bit, col) if axis == "lat" else (row, col ^ bit)

    def exchange(value, step):
        pairs = []
        for row in range(n_lat):
            for col in range(n_lon):
                other = partner((row, col), step)
                pairs.append((row * n_lon + col, other[0] * n_lon + other[1]))
        return lax.ppermute(value, ("lat", "lon"), pairs)

    def side(step):
        def of(order):
            axis, bit = order[step]
            return ((lat if axis == "lat" else lon) // bit) % 2

        return jnp.where(odd == 0, of(orders[0]), of(orders[1]))

    def plus(first, second):
        return (first.astype(f32) + second.astype(f32)).astype(bf16)

    def reduce_scatter(keep, send):
        piece = plus(keep, over_core(send))
        for step in range(len(bits)):
            half = piece.shape[0] // 2
            low, high = piece[:half], piece[half:]
            which = side(step) == 0
            piece = plus(jnp.where(which, low, high), exchange(jnp.where(which, high, low), step))
        return piece

    piece_1 = reduce_scatter(keep_1, send_1)
    piece_0 = reduce_scatter(keep_0, send_0)
    to_first = section == 0
    cut = piece_0.shape[0]

    def both(piece, small):
        return jnp.concatenate([piece, small], axis=0)

    def chosen(first, second):
        return jnp.where(to_first, first, second)

    got = over_section(both(chosen(piece_1, piece_0), chosen(taps_1, taps_0)))
    piece = plus(chosen(piece_0, piece_1), got[:cut])
    small = plus(chosen(taps_0, taps_1), got[cut:])
    for step in reversed(range(len(bits))):
        got = exchange(both(piece, small), step)
        cut = piece.shape[0]
        small = plus(small, got[cut:])
        which = side(step) == 0
        piece = jnp.where(which, jnp.concatenate([piece, got[:cut]]), jnp.concatenate([got[:cut], piece]))
    got = over_core(both(piece, small))
    cut = piece.shape[0]
    factor = 1.0 / math.sqrt(BATCH * ROWS_DEV * COLS_DEV)
    small = (small.astype(f32) + got[cut:].astype(f32)) * factor
    grad_up = by_core(piece, got[:cut]).astype(f32) * factor
    grad_down = by_core(got[:cut], piece).astype(f32) * factor
    grad_up = jnp.concatenate([grad_up[quarter * WIDE : (quarter + 1) * WIDE] for quarter in range(QUARTERS)], axis=1)

    other_end = over_section(chosen(final, start))
    boundary = jnp.stack([chosen(start, other_end), chosen(other_end, final)])[None]
    return (
        boundary,
        small[None, :TAPS],
        small[None, TAPS : TAPS + 5],
        grad_up[None],
        small[TAPS + 5 : TAPS + 9].reshape(1, HID),
        grad_down[None],
    )


def solution(mesh):
    in_specs = (
        P(None, "lat", "lon", None),
        P(None, "lat", "lon", None),
        P("lat", "lon"),
        P("section", None, None),
        P("section", None, None),
        P("section", None, None),
        P("section", None),
        P("section", None, None),
    )
    out_specs = (
        P("section", None, "lat", "lon", None),
        P("section", None, None),
        P("section", None, None),
        P("section", None, None),
        P("section", None),
        P("section", None, None),
    )
    return jax.shard_map(
        on_device, mesh=mesh, in_specs=in_specs, out_specs=out_specs, check_vma=False
    )
```

time: 318 us -> 139 us (0.44)
  waiting for transfers between devices: 111 us -> 36.2 us
  blocking collectives: 54.4 us -> 0 us
  other arithmetic: 51.7 us -> 5.63 us
  Pallas kernels: 0 us -> 38.7 us
  matrix products: 23.5 us -> 0 us
  between operations: 17.3 us -> 1.39 us
  local copies, waits for them, and re-layouts: 15.5 us -> 12 us
    psum x1 -> x0, waiting for transfers between devices: 82.5 us -> none  [on_device(): lax.psum((owned[0], owned[1], owned[2], owned[3], owned[4]), ('lat', 'lon'))]
    psum x1 -> x0, blocking collectives: 54.4 us -> none  [on_device(): lax.psum((owned[0], owned[1], owned[2], owned[3], owned[4]), ('lat', 'lon'))]
    pallas_call x0 -> x6, Pallas kernels: none -> 38.7 us  [call(): pl.pallas_call(body, name=name, out_shape=[jax.ShapeDtypeStruct(shape, dt...]
    reduce_sum x13 -> x0, other arithmetic: 25.6 us -> none  [the longest x2 11.3 us: cell_forward(): average = jnp.mean(conv_out, axis=-1, keepdims=True)]
    dot_general x12 -> x0, matrix products: 23.5 us -> none  [the longest x2 7.83 us: cell_forward(): jnp.dot(flat_rows, w_up, preferred_element_type=jnp.float32)]
    convert_element_type x9 -> x17, other arithmetic: 10.6 us -> 1.4 us  [the longest x1 0.74 us: on_device(): small_1 = jnp.where(section == 0, small_got, small_own).astype(f32)]
    ppermute x18 -> x29, waiting for transfers between devices: 28.8 us -> 36.2 us  [the longest x5 15 us: over_section(): return lax.ppermute(value, 'section', [(0, 1), (1, 0)])]
    reshape x8 -> x0, local copies, waits for them, and re-layouts: 6.91 us -> none  [the longest x2 3.05 us: cell_forward(): branch = branch.reshape(conv_out.shape)]
  transfers between devices with their start and end apart: 19 -> 29, of which waited for: 11 -> 13; matrix products, arithmetic and copies ran while one was open for 7% -> 5% of each run, Pallas kernels for 0% -> 13%
where the time goes in v1:
time: 139 us; the launch traced here: 137 us
  starting transfers between devices  43.3 us (31%)
  Pallas kernels  38.7 us (28%)
  waiting for transfers between devices  36.2 us (26%)
  local copies, waits for them, and re-layouts  12 us (9%)
  other arithmetic  5.63 us (4%)
    pallas_call x6, Pallas kernels, call(): pl.pallas_call(body, name=name, out_shape=[jax.ShapeDtypeStruct(shape, dt...  38.7 us
    ppermute x5, waiting for transfers between devices, over_section(): return lax.ppermute(value, 'section', [(0, 1), (1, 0)])  15 us
    ppermute x9, waiting for transfers between devices, exchange(): return lax.ppermute(value, ('lat', 'lon'), pairs)  15 us
    ppermute x9, starting transfers between devices, over_core(): return lax.ppermute(value, 'lat', swap_pairs(n_lat, 1))  14.2 us
    ppermute x4, starting transfers between devices, lat_halo(): return (over_core(send_a), lax.ppermute(send_b, 'lat', pairs))  12.1 us
    ppermute x9, starting transfers between devices, exchange(): return lax.ppermute(value, ('lat', 'lon'), pairs)  7.31 us
    ppermute x4, waiting for transfers between devices, lat_halo(): return (over_core(send_a), lax.ppermute(send_b, 'lat', pairs))  6.17 us
    ppermute x5, starting transfers between devices, over_section(): return lax.ppermute(value, 'section', [(0, 1), (1, 0)])  5.43 us
  transfers between devices with their start and end apart: 29, of which 13 were waited for; matrix products, arithmetic and copies ran while one was open for 5% of the time, Pallas kernels for 13%

profile of v1, /device:TPU:1, one launch (start us, length us, event | category | flops | bytes accessed | tf_op | source)
XLA Modules:
  0.0 137.2 jit_solution(14484703374016324977)
XLA Ops:
  2.1 2.2 %collective-permute-start = (bf16[4,19,256]{2,1,0:T(8,128)(2,1)S(1)}, bf16[4,19,256]{2,1,0:T(8,128)(2,1)S(1)}, u32[]{:S(2)}, u32[]{:S(2)}) collective-permute-start(bf16[4,19,256]{2,1,0:T(8,128)(2,1)S(1)} %pad_maximum_fusion.5), channel_id=1, source_target_pairs={{0,1},{1,2},{2,3},{3,0},{4,5},{5,6},{6,7},{7,4},{8,9},{9,10},{10,1... | collective-permute-start | bytes 116744 | tf_op jit(solution)/shard_map/ppermute | solution.py:412
  4.3 2.1 %collective-permute-start.1 = (bf16[4,19,256]{2,1,0:T(8,128)(2,1)S(1)}, bf16[4,19,256]{2,1,0:T(8,128)(2,1)S(1)}, u32[]{:S(2)}, u32[]{:S(2)}) collective-permute-start(bf16[4,19,256]{2,1,0:T(8,128)(2,1)S(1)} %pad_maximum_fusion.6), channel_id=1, source_target_pairs={{1,0},{2,1},{3,2},{0,3},{5,4},{6,5},{7,6},{4,7},{9,8},{10,9},{11,1... | collective-permute-start | bytes 116744 | tf_op jit(solution)/shard_map/ppermute | solution.py:413
  6.4 1.3 collective-permute-start.5
  8.3 1.3 collective-permute-start.4
  10.5 9.2 %collective-permute-done.4 = bf16[64,256]{1,0:T(8,128)(2,1)S(1)} collective-permute-done((bf16[64,256]{1,0:T(8,128)(2,1)S(1)}, bf16[64,256]{1,0:T(8,128)(2,1)S(1)}, u32[]{:S(2)}, u32[]{:S(2)}) %collective-permute-start.4) | collective-permute-done | bytes 32800 | tf_op jit(solution)/shard_map/ppermute | solution.py:380
  20.6 1.9 %collective-permute-start.2 = (bf16[3,96,256]{2,1,0:T(8,128)(2,1)S(1)}, bf16[3,96,256]{2,1,0:T(8,128)(2,1)S(1)}, u32[]{:S(2)}, u32[]{:S(2)}) collective-permute-start(bf16[3,96,256]{2,1,0:T(8,128)(2,1)S(1)} %get-tuple-element.84), channel_id=1, source_target_pairs={{0,4},{4,0},{8,12},{12,8},{1,5},{5,1},{9,13},{13,9},{2,6},{6,2},{1... | collective-permute-start | bytes 442376 | tf_op jit(solution)/shard_map/ppermute | solution.py:383
  22.5 3.0 %collective-permute-start.3 = (bf16[3,96,256]{2,1,0:T(8,128)(2,1)S(1)}, bf16[3,96,256]{2,1,0:T(8,128)(2,1)S(1)}, u32[]{:S(2)}, u32[]{:S(2)}) collective-permute-start(bf16[3,96,256]{2,1,0:T(8,128)(2,1)S(1)} %get-tuple-element.83), channel_id=1, source_target_pairs={{4,8},{8,4},{5,9},{9,5},{6,10},{10,6},{7,11},{11,7},{20,24},{24,20... | collective-permute-start | bytes 442376 | tf_op jit(solution)/shard_map/ppermute | solution.py:388
  30.0 9.0 %first_forward.1 = (bf16[4,88,256]{2,1,0:T(8,128)(2,1)}, bf16[3,88,256]{2,1,0:T(8,128)(2,1)}, bf16[3,88,256]{2,1,0:T(8,128)(2,1)}, f32[352,256]{1,0:T(8,128)}, f...) custom-call(s32[2]{0:T(128)} %pad_add_fusion.flags, ...), custom_call_target="tpu_custom_call" | custom-call | flops 2000000000 | bytes 4194304 | tf_op jit(solution)/shard_map/first_forward/pallas_call | solution.py:345
  39.0 3.1 %collective-permute-start.10 = (bf16[3,88,256]{2,1,0:T(8,128)(2,1)}, bf16[3,88,256]{2,1,0:T(8,128)(2,1)S(1)}, u32[]{:S(2)}, u32[]{:S(2)}) collective-permute-start(bf16[3,88,256]{2,1,0:T(8,128)(2,1)} %get-tuple-element.33), channel_id=1, source_target_pairs={{4,8},{8,4},{5,9},{9,5},{6,10},{10,6},{7,11},{11,7},{20,24},{24,20... | collective-permute-start | bytes 405512 | tf_op jit(solution)/shard_map/ppermute | solution.py:388
  42.3 3.2 %collective-permute-done.10.y_b.v_b = bf16[3,88,256]{2,1,0:T(8,128)(2,1)S(1)} collective-permute-done((bf16[3,88,256]{2,1,0:T(8,128)(2,1)}, bf16[3,88,256]{2,1,0:T(8,128)(2,1)S(1)}, u32[]{:S(2)}, u32[]{:S(2)}) %collective-permute-start.10) | collective-permute-done | bytes 135200 | tf_op jit(solution)/shard_map/ppermute | solution.py:388
  47.7 11.3 %second_block.1 = (bf16[4,68,256]{2,1,0:T(8,128)(2,1)}, bf16[4,80,256]{2,1,0:T(8,128)(2,1)}, bf16[3,80,256]{2,1,0:T(8,128)(2,1)}, bf16[3,80,256]{2,1,0:T(8,128)(...) custom-call(s32[2]{0:T(128)} %pad_add_fusion.flags, ...), custom_call_target="tpu_custom_call" | custom-call | flops 4000000000 | bytes 4194304 | tf_op jit(solution)/shard_map/second_block/pallas_call | solution.py:345
  59.6 3.2 %collective-permute-start.12 = (bf16[3,80,256]{2,1,0:T(8,128)(2,1)}, bf16[3,80,256]{2,1,0:T(8,128)(2,1)S(1)}, u32[]{:S(2)}, u32[]{:S(2)}) collective-permute-start(bf16[3,80,256]{2,1,0:T(8,128)(2,1)} %get-tuple-element.36), channel_id=1, source_target_pairs={{4,8},{8,4},{5,9},{9,5},{6,10},{10,6},{7,11},{11,7},{20,24},{24,20... | collective-permute-start | bytes 368648 | tf_op jit(solution)/shard_map/ppermute | solution.py:388
  62.8 3.0 %tap_grads_1.1 = bf16[64,256]{1,0:T(8,128)(2,1)} custom-call(s32[2]{0:T(128)} %pad_add_fusion.flags, bf16[4,88,256]{2,1,0:T(8,128)(2,1)} %get-tuple-element.31.y.v, bf16[3,88,256]{2,1,0:T(8,128)(2,1)} %copy-done.23, bf16[3,88,256]{2,1,0:T(8,128)(2,1)} %copy-done.22, bf16[4,80,256]{2,1,0:T(8,128)(2,1)} %get-tuple-element.34.du1.du, ...), custom_call_target="tpu_custom_call" | custom-call | flops 2000000000 | bytes 4194304 | tf_op jit(solution)/shard_map/tap_grads_1/pallas_call | solution.py:345
  67.4 9.3 %first_backward.1 = (f32[4,72,256]{2,1,0:T(8,128)}, bf16[4,88,256]{2,1,0:T(8,128)(2,1)}, bf16[3,88,256]{2,1,0:T(8,128)(2,1)}, bf16[3,88,256]{2,1,0:T(8,128)(2,1)...) custom-call(s32[2]{0:T(128)} %pad_add_fusion.flags, ...), custom_call_target="tpu_custom_call" | custom-call | flops 3000000000 | bytes 4194304 | tf_op jit(solution)/shard_map/first_backward/pallas_call | solution.py:345
  76.7 3.2 %tap_grads_0.1 = bf16[64,256]{1,0:T(8,128)(2,1)} custom-call(s32[2]{0:T(128)} %pad_add_fusion.flags, bf16[4,96,256]{2,1,0:T(8,128)(2,1)} %copy-done, bf16[3,96,256]{2,1,0:T(8,128)(2,1)} %copy-done.18, bf16[3,96,256]{2,1,0:T(8,128)(2,1)} %copy-done.19, bf16[4,88,256]{2,1,0:T(8,128)(2,1)} %get-tuple-element.45.du, f32[352,128]{1,0:T(8,128)} %broadcast_in_dim.99.own, ...), custom_call_target="tpu_custom_call" | custom-call | flops 2000000000 | bytes 4194304 | tf_op jit(solution)/shard_map/tap_grads_0/pallas_call | solution.py:345
  81.9 3.8 %collective-permute-done.17 = bf16[512,256]{1,0:T(8,128)(2,1)S(1)} collective-permute-done((bf16[512,256]{1,0:T(8,128)(2,1)S(1)}, bf16[512,256]{1,0:T(8,128)(2,1)S(1)}, u32[]{:S(2)}, u32[]{:S(2)}) %collective-permute-start.17) | collective-permute-done | bytes 262176 | tf_op jit(solution)/shard_map/ppermute | solution.py:526
  86.3 2.2 %collective-permute-done.21 = bf16[512,256]{1,0:T(8,128)(2,1)S(1)} collective-permute-done((bf16[512,256]{1,0:T(8,128)(2,1)S(1)}, bf16[512,256]{1,0:T(8,128)(2,1)S(1)}, u32[]{:S(2)}, u32[]{:S(2)}) %collective-permute-start.21) | collective-permute-done | bytes 262176 | tf_op jit(solution)/shard_map/ppermute | solution.py:526
  89.2 2.7 %collective-permute-done.18 = bf16[256,256]{1,0:T(8,128)(2,1)S(1)} collective-permute-done((bf16[256,256]{1,0:T(8,128)(2,1)S(1)}, bf16[256,256]{1,0:T(8,128)(2,1)S(1)}, u32[]{:S(2)}, u32[]{:S(2)}) %collective-permute-start.18) | collective-permute-done | bytes 131104 | tf_op jit(solution)/shard_map/ppermute | solution.py:526
  91.9 1.3 collective-permute-start.19
  93.2 1.4 %collective-permute-done.22 = bf16[256,256]{1,0:T(8,128)(2,1)S(1)} collective-permute-done((bf16[256,256]{1,0:T(8,128)(2,1)S(1)}, bf16[256,256]{1,0:T(8,128)(2,1)S(1)}, u32[]{:S(2)}, u32[]{:S(2)}) %collective-permute-start.22) | collective-permute-done | bytes 131104 | tf_op jit(solution)/shard_map/ppermute | solution.py:526
  96.0 2.2 %collective-permute-done.23 = bf16[128,256]{1,0:T(8,128)(2,1)S(1)} collective-permute-done((bf16[128,256]{1,0:T(8,128)(2,1)S(1)}, bf16[128,256]{1,0:T(8,128)(2,1)S(1)}, u32[]{:S(2)}, u32[]{:S(2)}) %collective-permute-start.23) | collective-permute-done | bytes 65568 | tf_op jit(solution)/shard_map/ppermute | solution.py:526
  98.3 1.3 collective-permute-start.24
  99.6 2.2 %collective-permute-done.24 = bf16[192,256]{1,0:T(8,128)(2,1)S(1)} collective-permute-done((bf16[192,256]{1,0:T(8,128)(2,1)S(1)}, bf16[192,256]{1,0:T(8,128)(2,1)S(1)}, u32[]{:S(2)}, u32[]{:S(2)}) %collective-permute-start.24) | collective-permute-done | bytes 98336 | tf_op jit(solution)/shard_map/ppermute | solution.py:380
  103.0 2.7 %collective-permute-done.25 = bf16[192,256]{1,0:T(8,128)(2,1)S(1)} collective-permute-done((bf16[192,256]{1,0:T(8,128)(2,1)S(1)}, bf16[192,256]{1,0:T(8,128)(2,1)S(1)}, u32[]{:S(2)}, u32[]{:S(2)}) %collective-permute-start.25) | collective-permute-done | bytes 98336 | tf_op jit(solution)/shard_map/ppermute | solution.py:526
  105.9 8.5 %collective-permute-start.13 = (bf16[3,88,256]{2,1,0:T(8,128)(2,1)S(1)}, bf16[3,88,256]{2,1,0:T(8,128)(2,1)S(1)}, u32[]{:S(2)}, u32[]{:S(2)}) collective-permute-start(bf16[3,88,256]{2,1,0:T(8,128)(2,1)S(1)} %copy-done.21), channel_id=1, source_target_pairs={{0,4},{4,0},{8,12},{12,8},{1,5},{5,1},{9,13},{13,9},{2,6},{6,2},{1... | collective-permute-start | bytes 405512 | tf_op jit(solution)/shard_map/ppermute | solution.py:383
  114.4 2.7 %collective-permute-start.14 = (bf16[3,88,256]{2,1,0:T(8,128)(2,1)S(1)}, bf16[3,88,256]{2,1,0:T(8,128)(2,1)S(1)}, u32[]{:S(2)}, u32[]{:S(2)}) collective-permute-start(bf16[3,88,256]{2,1,0:T(8,128)(2,1)S(1)} %copy-done.20), channel_id=1, source_target_pairs={{4,8},{8,4},{5,9},{9,5},{6,10},{10,6},{7,11},{11,7},{20,24},{24,20... | collective-permute-start | bytes 405512 | tf_op jit(solution)/shard_map/ppermute | solution.py:388
  117.3 1.7 %collective-permute-start.27 = (bf16[576,256]{1,0:T(8,128)(2,1)S(1)}, bf16[576,256]{1,0:T(8,128)(2,1)S(1)}, u32[]{:S(2)}, u32[]{:S(2)}) collective-permute-start(bf16[576,256]{1,0:T(8,128)(2,1)S(1)} %pad_maximum_fusion.1), channel_id=1, source_target_pairs={{0,8},{1,9},{2,10},{3,11},{4,5},{5,4},{6,7},{7,6},{8,0},{9,1},{10,... | collective-permute-start | bytes 884744 | tf_op jit(solution)/shard_map/ppermute | solution.py:526
  119.0 1.7 %collective-permute-done.14.du_b = bf16[3,88,256]{2,1,0:T(8,128)(2,1)S(1)} collective-permute-done((bf16[3,88,256]{2,1,0:T(8,128)(2,1)S(1)}, bf16[3,88,256]{2,1,0:T(8,128)(2,1)S(1)}, u32[]{:S(2)}, u32[]{:S(2)}) %collective-permute-start.14) | collective-permute-done | bytes 135200 | tf_op jit(solution)/shard_map/ppermute | solution.py:388
  121.3 2.9 %input_grad.1 = bf16[4,68,256]{2,1,0:T(8,128)(2,1)} custom-call(s32[2]{0:T(128)} %pad_add_fusion.flags, bf16[4,88,256]{2,1,0:T(8,128)(2,1)} %get-tuple-element.45.du, bf16[3,88,256]{2,1,0:T(8,128)(2,1)} %copy-done.24, bf16[3,88,256]{2,1,0:T(8,128)(2,1)} %copy-done.25, f32[64,256]{1,0:T(8,128)} %get-tuple-element.92.small.small0, ...), custom_call_target="tpu_custom_call" | custom-call | flops 2000000000 | bytes 4194304 | tf_op jit(solution)/shard_map/input_grad/pallas_call | solution.py:345
  124.6 2.6 %collective-permute-start.28 = (bf16[1088,256]{1,0:T(8,128)(2,1)S(1)}, bf16[1088,256]{1,0:T(8,128)(2,1)S(1)}, u32[]{:S(2)}, u32[]{:S(2)}) collective-permute-start(bf16[1088,256]{1,0:T(8,128)(2,1)S(1)} %pad_maximum_fusion), channel_id=1, source_target_pairs={{0,4},{4,0},{8,12},{12,8},{1,5},{5,1},{9,13},{13,9},{2,6},{6,2},{1... | collective-permute-start | bytes 1671176 | tf_op jit(solution)/shard_map/ppermute | solution.py:383
  127.2 1.3 collective-permute-start.15
  128.5 3.6 %collective-permute-done.15 = bf16[4,68,256]{2,1,0:T(8,128)(2,1)S(1)} collective-permute-done((bf16[4,68,256]{2,1,0:T(8,128)(2,1)S(1)}, bf16[4,68,256]{2,1,0:T(8,128)(2,1)S(1)}, u32[]{:S(2)}, u32[]{:S(2)}) %collective-permute-start.15) | collective-permute-done | bytes 139296 | tf_op jit(solution)/shard_map/ppermute | solution.py:380
  (191 shorter events, 24.8 us)
Async XLA Ops:
  2.1 18.3 %collective-permute-start = (bf16[4,19,256]{2,1,0:T(8,128)(2,1)S(1)}, bf16[4,19,256]{2,1,0:T(8,128)(2,1)S(1)}, u32[]{:S(2)}, u32[]{:S(2)}) collective-permute-start(bf16[4,19,256]{2,1,0:T(8,128)(2,1)S(1)} %pad_maximum_fusion.5), channel_id=1, source_target_pairs={{0,1},{1,2},{2,3},{3,0},{4,5},{5,6},{6,7},{7,4},{8,9},{9,10},{10,1... | collective-permute-start | bytes 116744 | tf_op jit(solution)/shard_map/ppermute | solution.py:412
  4.3 16.1 %collective-permute-start.1 = (bf16[4,19,256]{2,1,0:T(8,128)(2,1)S(1)}, bf16[4,19,256]{2,1,0:T(8,128)(2,1)S(1)}, u32[]{:S(2)}, u32[]{:S(2)}) collective-permute-start(bf16[4,19,256]{2,1,0:T(8,128)(2,1)S(1)} %pad_maximum_fusion.6), channel_id=1, source_target_pairs={{1,0},{2,1},{3,2},{0,3},{5,4},{6,5},{7,6},{4,7},{9,8},{10,9},{11,1... | collective-permute-start | bytes 116744 | tf_op jit(solution)/shard_map/ppermute | solution.py:413
  6.4 19.8 %collective-permute-start.5 = (bf16[128,1024]{1,0:T(8,128)(2,1)S(1)}, bf16[128,1024]{1,0:T(8,128)(2,1)S(1)}, u32[]{:S(2)}, u32[]{:S(2)}) collective-permute-start(bf16[128,1024]{1,0:T(8,128)(2,1)S(1)} %select_bitcast_fusion.1), channel_id=1, source_target_pairs={{0,16},{16,0},{1,17},{17,1},{2,18},{18,2},{3,19},{19,3},{4,20},{20... | collective-permute-start | bytes 786440 | tf_op jit(solution)/shard_map/ppermute | solution.py:380
  7.8 18.6 %collective-permute-start.6 = (bf16[512,256]{1,0:T(8,128)(2,1)S(1)}, bf16[512,256]{1,0:T(8,128)(2,1)S(1)}, u32[]{:S(2)}, u32[]{:S(2)}) collective-permute-start(bf16[512,256]{1,0:T(8,128)(2,1)S(1)} %select_bitcast_fusion), channel_id=1, source_target_pairs={{0,16},{16,0},{1,17},{17,1},{2,18},{18,2},{3,19},{19,3},{4,20},{20... | collective-permute-start | bytes 786440 | tf_op jit(solution)/shard_map/ppermute | solution.py:380
  8.3 11.4 %collective-permute-start.4 = (bf16[64,256]{1,0:T(8,128)(2,1)S(1)}, bf16[64,256]{1,0:T(8,128)(2,1)S(1)}, u32[]{:S(2)}, u32[]{:S(2)}) collective-permute-start(bf16[64,256]{1,0:T(8,128)(2,1)S(1)} %maximum_maximum_fusion.1), channel_id=1, source_target_pairs={{0,16},{16,0},{1,17},{17,1},{2,18},{18,2},{3,19},{19,3},{4,20},{20... | collective-permute-start | bytes 98312 | tf_op jit(solution)/shard_map/ppermute | solution.py:380
  20.6 7.3 %collective-permute-start.2 = (bf16[3,96,256]{2,1,0:T(8,128)(2,1)S(1)}, bf16[3,96,256]{2,1,0:T(8,128)(2,1)S(1)}, u32[]{:S(2)}, u32[]{:S(2)}) collective-permute-start(bf16[3,96,256]{2,1,0:T(8,128)(2,1)S(1)} %get-tuple-element.84), channel_id=1, source_target_pairs={{0,4},{4,0},{8,12},{12,8},{1,5},{5,1},{9,13},{13,9},{2,6},{6,2},{1... | collective-permute-start | bytes 442376 | tf_op jit(solution)/shard_map/ppermute | solution.py:383
  22.5 6.5 %collective-permute-start.3 = (bf16[3,96,256]{2,1,0:T(8,128)(2,1)S(1)}, bf16[3,96,256]{2,1,0:T(8,128)(2,1)S(1)}, u32[]{:S(2)}, u32[]{:S(2)}) collective-permute-start(bf16[3,96,256]{2,1,0:T(8,128)(2,1)S(1)} %get-tuple-element.83), channel_id=1, source_target_pairs={{4,8},{8,4},{5,9},{9,5},{6,10},{10,6},{7,11},{11,7},{20,24},{24,20... | collective-permute-start | bytes 442376 | tf_op jit(solution)/shard_map/ppermute | solution.py:388
  26.3 2.7 %collective-permute-start.7 = (bf16[128,1024]{1,0:T(8,128)(2,1)S(1)}, bf16[128,1024]{1,0:T(8,128)(2,1)S(1)}, u32[]{:S(2)}, u32[]{:S(2)}) collective-permute-start(bf16[128,1024]{1,0:T(8,128)(2,1)S(1)} %collective-permute-done.5.got_up), channel_id=1, source_target_pairs={{0,4},{4,0},{8,12},{12,8},{1,5},{5,1},{9,13},{13,9},{2,6},{6,2},{1... | collective-permute-start | bytes 786440 | tf_op jit(solution)/shard_map/ppermute | solution.py:383
  26.4 2.6 %collective-permute-start.8 = (bf16[512,256]{1,0:T(8,128)(2,1)S(1)}, bf16[512,256]{1,0:T(8,128)(2,1)S(1)}, u32[]{:S(2)}, u32[]{:S(2)}) collective-permute-start(bf16[512,256]{1,0:T(8,128)(2,1)S(1)} %collective-permute-done.6.got_down), channel_id=1, source_target_pairs={{0,4},{4,0},{8,12},{12,8},{1,5},{5,1},{9,13},{13,9},{2,6},{6,2},{1... | collective-permute-start | bytes 786440 | tf_op jit(solution)/shard_map/ppermute | solution.py:383
  26.9 12.0 %copy-start.1 = (bf16[4,88,256]{2,1,0:T(8,128)(2,1)}, bf16[4,88,256]{2,1,0:T(8,128)(2,1)S(1)}, u32[]{:S(2)}) copy-start(bf16[4,88,256]{2,1,0:T(8,128)(2,1)S(1)} %broadcast_multiply_fusion.upstream_in) | copy-start | bytes 540676
  39.0 6.5 %collective-permute-start.10 = (bf16[3,88,256]{2,1,0:T(8,128)(2,1)}, bf16[3,88,256]{2,1,0:T(8,128)(2,1)S(1)}, u32[]{:S(2)}, u32[]{:S(2)}) collective-permute-start(bf16[3,88,256]{2,1,0:T(8,128)(2,1)} %get-tuple-element.33), channel_id=1, source_target_pairs={{4,8},{8,4},{5,9},{9,5},{6,10},{10,6},{7,11},{11,7},{20,24},{24,20... | collective-permute-start | bytes 405512 | tf_op jit(solution)/shard_map/ppermute | solution.py:388
  42.0 3.5 %collective-permute-start.9 = (bf16[3,88,256]{2,1,0:T(8,128)(2,1)}, bf16[3,88,256]{2,1,0:T(8,128)(2,1)S(1)}, u32[]{:S(2)}, u32[]{:S(2)}) collective-permute-start(bf16[3,88,256]{2,1,0:T(8,128)(2,1)} %get-tuple-element.32), channel_id=1, source_target_pairs={{0,4},{4,0},{8,12},{12,8},{1,5},{5,1},{9,13},{13,9},{2,6},{6,2},{1... | collective-permute-start | bytes 405512 | tf_op jit(solution)/shard_map/ppermute | solution.py:383
  59.0 20.9 %collective-permute-start.16 = (bf16[1024,256]{1,0:T(8,128)(2,1)}, bf16[1024,256]{1,0:T(8,128)(2,1)S(1)}, u32[]{:S(2)}, u32[]{:S(2)}) collective-permute-start(bf16[1024,256]{1,0:T(8,128)(2,1)} %get-tuple-element.53), channel_id=1, source_target_pairs={{0,4},{4,0},{8,12},{12,8},{1,5},{5,1},{9,13},{13,9},{2,6},{6,2},{1... | collective-permute-start | bytes 1572872 | tf_op jit(solution)/shard_map/ppermute | solution.py:383
  59.1 6.8 %collective-permute-start.11 = (bf16[3,80,256]{2,1,0:T(8,128)(2,1)}, bf16[3,80,256]{2,1,0:T(8,128)(2,1)S(1)}, u32[]{:S(2)}, u32[]{:S(2)}) collective-permute-start(bf16[3,80,256]{2,1,0:T(8,128)(2,1)} %get-tuple-element.35), channel_id=1, source_target_pairs={{0,4},{4,0},{8,12},{12,8},{1,5},{5,1},{9,13},{13,9},{2,6},{6,2},{1... | collective-permute-start | bytes 368648 | tf_op jit(solution)/shard_map/ppermute | solution.py:383
  59.6 6.4 %collective-permute-start.12 = (bf16[3,80,256]{2,1,0:T(8,128)(2,1)}, bf16[3,80,256]{2,1,0:T(8,128)(2,1)S(1)}, u32[]{:S(2)}, u32[]{:S(2)}) collective-permute-start(bf16[3,80,256]{2,1,0:T(8,128)(2,1)} %get-tuple-element.36), channel_id=1, source_target_pairs={{4,8},{8,4},{5,9},{9,5},{6,10},{10,6},{7,11},{11,7},{20,24},{24,20... | collective-permute-start | bytes 368648 | tf_op jit(solution)/shard_map/ppermute | solution.py:388
  76.6 3.6 %collective-permute-start.20 = (bf16[1024,256]{1,0:T(8,128)(2,1)}, bf16[1024,256]{1,0:T(8,128)(2,1)S(1)}, u32[]{:S(2)}, u32[]{:S(2)}) collective-permute-start(bf16[1024,256]{1,0:T(8,128)(2,1)} %get-tuple-element.55), channel_id=1, source_target_pairs={{0,4},{4,0},{8,12},{12,8},{1,5},{5,1},{9,13},{13,9},{2,6},{6,2},{1... | collective-permute-start | bytes 1572872 | tf_op jit(solution)/shard_map/ppermute | solution.py:383
  80.1 5.6 %collective-permute-start.17 = (bf16[512,256]{1,0:T(8,128)(2,1)S(1)}, bf16[512,256]{1,0:T(8,128)(2,1)S(1)}, u32[]{:S(2)}, u32[]{:S(2)}) collective-permute-start(bf16[512,256]{1,0:T(8,128)(2,1)S(1)} %broadcast_select_fusion.1), channel_id=1, source_target_pairs={{0,8},{1,9},{2,10},{3,11},{4,5},{5,4},{6,7},{7,6},{8,0},{9,1},{10,... | collective-permute-start | bytes 786440 | tf_op jit(solution)/shard_map/ppermute | solution.py:526
  81.2 7.4 %collective-permute-start.21 = (bf16[512,256]{1,0:T(8,128)(2,1)S(1)}, bf16[512,256]{1,0:T(8,128)(2,1)S(1)}, u32[]{:S(2)}, u32[]{:S(2)}) collective-permute-start(bf16[512,256]{1,0:T(8,128)(2,1)S(1)} %broadcast_select_fusion), channel_id=1, source_target_pairs={{0,8},{1,9},{2,10},{3,11},{4,5},{5,4},{6,7},{7,6},{8,0},{9,1},{10,... | collective-permute-start | bytes 786440 | tf_op jit(solution)/shard_map/ppermute | solution.py:526
  85.8 6.0 %collective-permute-start.18 = (bf16[256,256]{1,0:T(8,128)(2,1)S(1)}, bf16[256,256]{1,0:T(8,128)(2,1)S(1)}, u32[]{:S(2)}, u32[]{:S(2)}) collective-permute-start(bf16[256,256]{1,0:T(8,128)(2,1)S(1)} %broadcast_select_fusion.6), channel_id=1, source_target_pairs={{0,1},{1,0},{2,3},{3,2},{4,6},{5,7},{6,4},{7,5},{8,9},{9,8},{10,11... | collective-permute-start | bytes 393224 | tf_op jit(solution)/shard_map/ppermute | solution.py:526
  88.7 6.0 %collective-permute-start.22 = (bf16[256,256]{1,0:T(8,128)(2,1)S(1)}, bf16[256,256]{1,0:T(8,128)(2,1)S(1)}, u32[]{:S(2)}, u32[]{:S(2)}) collective-permute-start(bf16[256,256]{1,0:T(8,128)(2,1)S(1)} %broadcast_select_fusion.5), channel_id=1, source_target_pairs={{0,1},{1,0},{2,3},{3,2},{4,6},{5,7},{6,4},{7,5},{8,9},{9,8},{10,11... | collective-permute-start | bytes 393224 | tf_op jit(solution)/shard_map/ppermute | solution.py:526
  91.9 4.1 %collective-permute-start.19 = (bf16[128,256]{1,0:T(8,128)(2,1)S(1)}, bf16[128,256]{1,0:T(8,128)(2,1)S(1)}, u32[]{:S(2)}, u32[]{:S(2)}) collective-permute-start(bf16[128,256]{1,0:T(8,128)(2,1)S(1)} %broadcast_select_fusion.8), channel_id=1, source_target_pairs={{0,2},{1,3},{2,0},{3,1},{4,12},{5,13},{6,14},{7,15},{8,10},{9,11},... | collective-permute-start | bytes 196616 | tf_op jit(solution)/shard_map/ppermute | solution.py:526
  94.7 3.5 %collective-permute-start.23 = (bf16[128,256]{1,0:T(8,128)(2,1)S(1)}, bf16[128,256]{1,0:T(8,128)(2,1)S(1)}, u32[]{:S(2)}, u32[]{:S(2)}) collective-permute-start(bf16[128,256]{1,0:T(8,128)(2,1)S(1)} %broadcast_select_fusion.7), channel_id=1, source_target_pairs={{0,2},{1,3},{2,0},{3,1},{4,12},{5,13},{6,14},{7,15},{8,10},{9,11},... | collective-permute-start | bytes 196616 | tf_op jit(solution)/shard_map/ppermute | solution.py:526
  96.0 9.9 %copy-start.21 = (bf16[3,88,256]{2,1,0:T(8,128)(2,1)S(1)}, bf16[3,88,256]{2,1,0:T(8,128)(2,1)}, u32[]{:S(2)}) copy-start(bf16[3,88,256]{2,1,0:T(8,128)(2,1)} %get-tuple-element.46) | copy-start | bytes 405508
  96.0 18.4 %copy-start.20 = (bf16[3,88,256]{2,1,0:T(8,128)(2,1)S(1)}, bf16[3,88,256]{2,1,0:T(8,128)(2,1)}, u32[]{:S(2)}) copy-start(bf16[3,88,256]{2,1,0:T(8,128)(2,1)} %get-tuple-element.47) | copy-start | bytes 405508
  98.3 3.5 %collective-permute-start.24 = (bf16[192,256]{1,0:T(8,128)(2,1)S(1)}, bf16[192,256]{1,0:T(8,128)(2,1)S(1)}, u32[]{:S(2)}, u32[]{:S(2)}) collective-permute-start(bf16[192,256]{1,0:T(8,128)(2,1)S(1)} %pad_maximum_fusion.3), channel_id=1, source_target_pairs={{0,16},{16,0},{1,17},{17,1},{2,18},{18,2},{3,19},{19,3},{4,20},{20... | collective-permute-start | bytes 294920 | tf_op jit(solution)/shard_map/ppermute | solution.py:380
  101.9 3.8 %collective-permute-start.25 = (bf16[192,256]{1,0:T(8,128)(2,1)S(1)}, bf16[192,256]{1,0:T(8,128)(2,1)S(1)}, u32[]{:S(2)}, u32[]{:S(2)}) collective-permute-start(bf16[192,256]{1,0:T(8,128)(2,1)S(1)} %pad_maximum_fusion.4), channel_id=1, source_target_pairs={{0,2},{1,3},{2,0},{3,1},{4,12},{5,13},{6,14},{7,15},{8,10},{9,11},... | collective-permute-start | bytes 294920 | tf_op jit(solution)/shard_map/ppermute | solution.py:526
  105.8 11.3 %collective-permute-start.26 = (bf16[320,256]{1,0:T(8,128)(2,1)S(1)}, bf16[320,256]{1,0:T(8,128)(2,1)S(1)}, u32[]{:S(2)}, u32[]{:S(2)}) collective-permute-start(bf16[320,256]{1,0:T(8,128)(2,1)S(1)} %pad_maximum_fusion.2), channel_id=1, source_target_pairs={{0,1},{1,0},{2,3},{3,2},{4,6},{5,7},{6,4},{7,5},{8,9},{9,8},{10,11... | collective-permute-start | bytes 491528 | tf_op jit(solution)/shard_map/ppermute | solution.py:526
  105.9 13.1 %collective-permute-start.13 = (bf16[3,88,256]{2,1,0:T(8,128)(2,1)S(1)}, bf16[3,88,256]{2,1,0:T(8,128)(2,1)S(1)}, u32[]{:S(2)}, u32[]{:S(2)}) collective-permute-start(bf16[3,88,256]{2,1,0:T(8,128)(2,1)S(1)} %copy-done.21), channel_id=1, source_target_pairs={{0,4},{4,0},{8,12},{12,8},{1,5},{5,1},{9,13},{13,9},{2,6},{6,2},{1... | collective-permute-start | bytes 405512 | tf_op jit(solution)/shard_map/ppermute | solution.py:383
  114.4 6.3 %collective-permute-start.14 = (bf16[3,88,256]{2,1,0:T(8,128)(2,1)S(1)}, bf16[3,88,256]{2,1,0:T(8,128)(2,1)S(1)}, u32[]{:S(2)}, u32[]{:S(2)}) collective-permute-start(bf16[3,88,256]{2,1,0:T(8,128)(2,1)S(1)} %copy-done.20), channel_id=1, source_target_pairs={{4,8},{8,4},{5,9},{9,5},{6,10},{10,6},{7,11},{11,7},{20,24},{24,20... | collective-permute-start | bytes 405512 | tf_op jit(solution)/shard_map/ppermute | solution.py:388
  117.3 7.0 %collective-permute-start.27 = (bf16[576,256]{1,0:T(8,128)(2,1)S(1)}, bf16[576,256]{1,0:T(8,128)(2,1)S(1)}, u32[]{:S(2)}, u32[]{:S(2)}) collective-permute-start(bf16[576,256]{1,0:T(8,128)(2,1)S(1)} %pad_maximum_fusion.1), channel_id=1, source_target_pairs={{0,8},{1,9},{2,10},{3,11},{4,5},{5,4},{6,7},{7,6},{8,0},{9,1},{10,... | collective-permute-start | bytes 884744 | tf_op jit(solution)/shard_map/ppermute | solution.py:526
  124.6 8.3 %collective-permute-start.28 = (bf16[1088,256]{1,0:T(8,128)(2,1)S(1)}, bf16[1088,256]{1,0:T(8,128)(2,1)S(1)}, u32[]{:S(2)}, u32[]{:S(2)}) collective-permute-start(bf16[1088,256]{1,0:T(8,128)(2,1)S(1)} %pad_maximum_fusion), channel_id=1, source_target_pairs={{0,4},{4,0},{8,12},{12,8},{1,5},{5,1},{9,13},{13,9},{2,6},{6,2},{1... | collective-permute-start | bytes 1671176 | tf_op jit(solution)/shard_map/ppermute | solution.py:383
  127.2 4.9 %collective-permute-start.15 = (bf16[4,68,256]{2,1,0:T(8,128)(2,1)S(1)}, bf16[4,68,256]{2,1,0:T(8,128)(2,1)S(1)}, u32[]{:S(2)}, u32[]{:S(2)}) collective-permute-start(bf16[4,68,256]{2,1,0:T(8,128)(2,1)S(1)} %broadcast_select_fusion.4), channel_id=1, source_target_pairs={{0,16},{16,0},{1,17},{17,1},{2,18},{18,2},{3,19},{19,3},{4,20},{20... | collective-permute-start | bytes 417800 | tf_op jit(solution)/shard_map/ppermute | solution.py:380
  (25 other events, 88.9 us)

commit v2 on v1

v2 whole, which is shorter than its diff:
```python
import math

import jax
import jax.numpy as jnp
from jax import lax
from jax.experimental import pallas as pl
from jax.experimental.pallas import tpu as pltpu
from jax.sharding import PartitionSpec as P

KERNEL = 7
TAPS = KERNEL * KERNEL
REACH = KERNEL // 2
ROWS_DEV = 4
COLS_DEV = 68
BATCH = 2
HALF = 128
WIDE = 256
HID = 1024
QUARTERS = HID // WIDE
SIDE_X, SIDE_0, SIDE_1 = 12, 9, 6
W_X, W_0, W_1, W_OWN = 96, 88, 80, 72
CHUNK = 32
SMALL = 64
N_0, N_1 = ROWS_DEV * W_0, ROWS_DEV * W_1
AT_NORMED, AT_BASE, AT_INVERSE, AT_E_0, AT_E_1 = 0, N_0, 2 * N_0, 3 * N_0, 4 * N_0
KEPT_ROWS = 40960

norm_eps = 1e-06
gelu_scale = 0.7978845608028654
gelu_cubic = 0.044715
f32, bf16 = jnp.float32, jnp.bfloat16

nn = (((1,), (0,)), ((), ()))
nt = (((1,), (1,)), ((), ()))
tn = (((0,), (0,)), ((), ()))


def dot(left, right, dims=nn):
    return lax.dot_general(left, right, dims, preferred_element_type=f32)


def lanes(half):
    return slice(half * HALF, (half + 1) * HALF)


def load_padded(pad, odd, center, first, second, offset=0):
    width = center.shape[1]

    def put(row, value):
        value = value.astype(f32)
        for half in range(2):
            pad[half, row, offset : offset + width, :] = value[:, lanes(half)]

    at_first = jnp.where(odd == 1, 0, REACH + ROWS_DEV)
    at_second = jnp.where(odd == 1, REACH + ROWS_DEV, 0)
    for row in range(ROWS_DEV):
        put(REACH + row, center[row])
    for row in range(REACH):
        put(at_first + row, first[row])
        put(at_second + row, second[row])


def load_taps(taps, small):
    for half in range(2):
        taps[half] = jnp.broadcast_to(small[0:TAPS, lanes(half)][:, None, :], (TAPS, 8, HALF))


def groups(width, most):
    tiles = width // 8
    count = -(-tiles // most)
    bounds = [tiles * i // count for i in range(count + 1)]
    return [range(first, last) for first, last in zip(bounds, bounds[1:])]


def conv_tiles(pad, taps, half, starts, reverse):
    sums = [[None] * ROWS_DEV for _ in starts]
    for col_off in range(KERNEL):
        column = [taps[half, TAPS - 1 - tap if reverse else tap] for tap in range(col_off, TAPS, KERNEL)]
        for row in range(ROWS_DEV + KERNEL - 1):
            for index, start in enumerate(starts):
                window = pad[half, row, start + col_off : start + col_off + 8, :]
                for out_row in range(ROWS_DEV):
                    row_off = row - out_row
                    if 0 <= row_off < KERNEL:
                        term = window * column[row_off]
                        held = sums[index][out_row]
                        sums[index][out_row] = term if held is None else held + term
    return sums


def chunks(count, body, carry=0):
    for i in range(count // CHUNK):
        carry = body(slice(i * CHUNK, (i + 1) * CHUNK), carry)
    return carry


def fold(value):
    return jnp.sum(value.reshape(CHUNK // 8, 8, value.shape[-1]), axis=0)


def twice(value):
    return jnp.concatenate([value, value], axis=1)


def send_rows(odd, source, send_first, send_second):
    first, second = jnp.where(odd == 1, 0, 1), jnp.where(odd == 1, 1, 0)
    send_first[...] = source[pl.ds(first, REACH)]
    send_second[...] = source[pl.ds(second, REACH)]


def forward_conv(width, pad, taps, small, normed, inverse, z, base):
    count = ROWS_DEV * width
    load_taps(taps, small)
    for group in groups(width, 4):
        starts = [tile * 8 for tile in group]
        halves = [conv_tiles(pad, taps, half, starts, False) for half in range(2)]
        for index, row in [(index, row) for index in range(len(starts)) for row in range(ROWS_DEV)]:
            start = starts[index]
            u = [halves[half][index][row] + small[TAPS : TAPS + 1, lanes(half)] for half in range(2)]
            mean = jnp.sum(u[0] + u[1], axis=-1, keepdims=True) * (1.0 / WIDE)
            u = [value - mean for value in u]
            spread = jnp.sum(u[0] * u[0] + u[1] * u[1], axis=-1, keepdims=True) * (1.0 / WIDE)
            scale = lax.rsqrt(spread + norm_eps)
            at = slice(row * width + start, row * width + start + 8)
            inverse[at, :] = jnp.broadcast_to(scale, (8, HALF))
            for half in range(2):
                normed[at, lanes(half)] = u[half] * scale
                base[at, lanes(half)] = pad[half, REACH + row, start + REACH : start + REACH + 8, :]
    scale_cells(count, small, normed, z)


def scale_cells(count, small, normed, z):
    def scaled(at, carry):
        z[at, :] = (normed[at, :] * small[TAPS + 1 : TAPS + 2, :] + small[TAPS + 2 : TAPS + 3, :]).astype(bf16)
        return carry

    chunks(count, scaled, 0)


def forward_mlp(width, small, mask, w_up, w_down, z, base, hidden, active, slope, branch, out):
    count = ROWS_DEV * width
    for quarter in range(QUARTERS):
        cols = slice(quarter * WIDE, (quarter + 1) * WIDE)
        held = hidden.at[quarter % 2]
        held[...] = dot(z[...], w_up[:, cols])
        bias = small[TAPS + 5 + quarter : TAPS + 6 + quarter, :]

        def gelu(at, carry, held=held, cols=cols, bias=bias):
            h = held[at, :] + bias
            square = h * h
            tangent = jnp.tanh(h * (gelu_scale + (gelu_scale * gelu_cubic) * square))
            above = 0.5 + 0.5 * tangent
            active[at, cols] = (h * above).astype(bf16)
            slope[at, cols] = above + (0.5 * h) * (1.0 - tangent * tangent) * (
                gelu_scale + (3.0 * gelu_scale * gelu_cubic) * square
            )
            return carry

        chunks(count, gelu, 0)
    branch[...] = dot(active[...], w_down[...]) + small[TAPS + 3 : TAPS + 4, :]
    if out is None:
        return

    def residual(at, carry):
        out[at, :] = twice(mask[at, :]) * (base[at, :] + small[TAPS + 4 : TAPS + 5, :] * branch[at, :])
        return carry

    chunks(count, residual, 0)


def backward_cells(
    width, odd, small, own, own_row, upstream, w_up, w_down, normed, inverse, z, active, slope, branch, hidden, dm, dh, du, keep, send, sums
):
    count = ROWS_DEV * width
    zero = jnp.zeros((8, WIDE), f32)

    def first(at, carry):
        sum_dm, sum_em = carry
        e = upstream[at, :]
        inside = twice(own[at, :])
        grad = (e * small[TAPS + 4 : TAPS + 5, :]).astype(bf16)
        dm[at, :] = grad
        sum_dm = sum_dm + fold(grad.astype(f32) * inside)
        sum_em = sum_em + fold(e * branch[at, :] * inside)
        return sum_dm, sum_em

    sum_dm, sum_em = chunks(count, first, (zero, zero))
    for quarter in range(QUARTERS):
        cols = slice(quarter * WIDE, (quarter + 1) * WIDE)
        held = hidden.at[quarter % 2]
        held[...] = dot(dm[...], w_down[cols, :], nt)

        def through(at, carry, held=held, cols=cols):
            dh[at, cols] = (held[at, :] * slope[at, cols]).astype(bf16)
            return carry

        chunks(count, through, 0)
    hidden[0] = dot(dh[...], w_up[...], nt)
    sum_dh = dot(own_row[...], dh[...])

    def norm(at, carry):
        sum_dzn, sum_dz, sum_du = carry
        dz = hidden[0, at, :]
        normal = normed[at, :]
        inside = twice(own[at, :])
        inner = dz * inside
        sum_dz = sum_dz + fold(inner)
        sum_dzn = sum_dzn + fold(inner * normal)
        dn = dz * small[TAPS + 1 : TAPS + 2, :]
        mean = jnp.sum(dn, axis=-1, keepdims=True) * (1.0 / WIDE)
        slant = jnp.sum(dn * normal, axis=-1, keepdims=True) * (1.0 / WIDE)
        grad = (twice(inverse[at, :]) * (dn - mean - normal * slant)).astype(bf16).astype(f32)
        du[at, :] = grad
        sum_du = sum_du + fold(grad * inside)
        dm[at, :] = (dm[at, :].astype(f32) * inside).astype(bf16)
        z[at, :] = (z[at, :].astype(f32) * inside).astype(bf16)
        return sum_dzn, sum_dz, sum_du

    sum_dzn, sum_dz, sum_du = chunks(count, norm, (zero, zero, zero))
    rows = [jnp.sum(value, axis=0, keepdims=True) for value in (sum_du, sum_dzn, sum_dz, sum_dm, sum_em)]
    rows += [sum_dh[0:1, quarter * WIDE : (quarter + 1) * WIDE] for quarter in range(QUARTERS)]
    for index, value in enumerate(rows):
        sums[index : index + 1, :] = value
    sums[len(rows) : 16, :] = jnp.zeros((16 - len(rows), WIDE), f32)

    def weights(up_ref, down_ref):
        for quarter in range(QUARTERS):
            cols = slice(quarter * WIDE, (quarter + 1) * WIDE)
            up_ref[cols, :] = dot(z[...], dh[:, cols], tn).astype(bf16)
            down_ref[cols, :] = dot(active[:, cols], dm[...], tn).astype(bf16)

    @pl.when(odd == 0)
    def _():
        weights(keep, send)

    @pl.when(odd == 1)
    def _():
        weights(send, keep)


def weight_copies(block, flags, parts, w_up, w_down, sems, act):
    odd, section = flags[0], flags[1]
    own_up, own_down, got_up, got_down, other_up, other_down = parts

    @pl.when(section == block)
    def _():
        act(pltpu.make_async_copy(own_up, w_up, sems.at[0]))
        act(pltpu.make_async_copy(own_down, w_down, sems.at[1]))

    @pl.when(section != block)
    def _():
        for index, (ref, mine, other) in enumerate(((w_up, got_up, other_up), (w_down, got_down, other_down))):
            half = mine.shape[0]
            for place, part in enumerate((mine, other)):
                first = odd if place == 0 else 1 - odd
                rows = pl.ds(pl.multiple_of(first * half, half), half)
                act(pltpu.make_async_copy(part, ref.at[rows, :], sems.at[2 + 2 * index + place]))


def start_copy(copy):
    copy.start()


def wait_copy(copy):
    copy.wait()


def write_rows(source, width, out):
    for row in range(ROWS_DEV):
        out[row] = source[row * width : (row + 1) * width, :].astype(bf16)


def kept_copies(kept, sems, places, out):
    copies = []
    for index, (ref, first) in enumerate(places):
        rows = kept.at[first : first + ref.shape[0], 0 : ref.shape[1]]
        copies.append(pltpu.make_async_copy(ref, rows, sems.at[index]) if out else pltpu.make_async_copy(rows, ref, sems.at[index]))
    return copies


def first_conv(
    flags, x, x_a, x_b, small, mask, cot, left, right, kept, pad, taps, wide, normed, inverse, z, base, e_1, sems
):
    places = [(wide, AT_E_0), (e_1, AT_E_1), (normed, AT_NORMED), (base, AT_BASE), (inverse, AT_INVERSE)]
    copies = kept_copies(kept, sems, places, True)
    before = SIDE_0 - SIDE_1
    wide[...] = jnp.zeros((N_0, WIDE), f32)
    for row in range(ROWS_DEV):
        at = row * W_0 + before
        wide[at : at + SIDE_1, :] = left[row].astype(f32)[SIDE_X : SIDE_X + SIDE_1]
        wide[at + SIDE_1 : at + SIDE_1 + COLS_DEV, :] = cot[row].astype(f32)
        wide[at + SIDE_1 + COLS_DEV : at + W_1, :] = right[row].astype(f32)[SIDE_X : SIDE_X + SIDE_1]
    wide[...] = wide[...] * twice(mask[...])
    for row in range(ROWS_DEV):
        at = row * W_0 + before
        e_1[row * W_1 : (row + 1) * W_1, :] = wide[at : at + W_1, :]
    for copy in copies[:2]:
        copy.start()
    load_padded(pad, flags[0], x, x_a, x_b)
    forward_conv(W_0, pad, taps, small, normed, inverse, z, base)
    for copy in copies[2:]:
        copy.start()
    for copy in copies:
        copy.wait()


def first_forward(flags, small, mask, kept, *refs):
    parts, refs = refs[:6], refs[6:]
    y, send_a, send_b, normed, z, base, hidden, out, active, slope, branch, w_up, w_down, weight_sems, sems = refs
    copies = kept_copies(kept, sems, [(normed, AT_NORMED), (base, AT_BASE)], False)
    for copy in copies:
        copy.start()
    weight_copies(0, flags, parts, w_up, w_down, weight_sems, start_copy)
    for copy in copies:
        copy.wait()
    scale_cells(N_0, small, normed, z)
    weight_copies(0, flags, parts, w_up, w_down, weight_sems, wait_copy)
    forward_mlp(W_0, small, mask, w_up, w_down, z, base, hidden, active, slope, branch, out)
    write_rows(out, W_0, y)
    send_rows(flags[0], y, send_a, send_b)


def first_again(flags, small, kept, *refs):
    parts, refs = refs[:6], refs[6:]
    active, slope, branch, w_up, w_down, normed, z, hidden, weight_sems, sems = refs
    (copy,) = kept_copies(kept, sems, [(normed, AT_NORMED)], False)
    copy.start()
    weight_copies(0, flags, parts, w_up, w_down, weight_sems, start_copy)
    copy.wait()
    scale_cells(N_0, small, normed, z)
    weight_copies(0, flags, parts, w_up, w_down, weight_sems, wait_copy)
    forward_mlp(W_0, small, None, w_up, w_down, z, None, hidden, active, slope, branch, None)


def second_block(flags, y, y_a, y_b, small, mask, own, own_row, kept, *refs):
    parts, refs = refs[:6], refs[6:]
    final, du_out, send_a, send_b, keep, send, sums, pad = refs[:8]
    taps, hidden, out, normed, inverse, z, base, active, slope, branch, w_up, w_down, upstream, dm, dh, du, weight_sems, sems = refs[8:]
    (copy,) = kept_copies(kept, sems, [(upstream, AT_E_1)], False)
    copy.start()
    weight_copies(1, flags, parts, w_up, w_down, weight_sems, start_copy)
    load_padded(pad, flags[0], y, y_a, y_b)
    forward_conv(W_1, pad, taps, small, normed, inverse, z, base)
    weight_copies(1, flags, parts, w_up, w_down, weight_sems, wait_copy)
    copy.wait()
    forward_mlp(W_1, small, mask, w_up, w_down, z, base, hidden, active, slope, branch, out)
    for row in range(ROWS_DEV):
        at = row * W_1 + SIDE_1
        final[row] = out[at : at + COLS_DEV, :].astype(bf16)
    backward_cells(
        W_1, flags[0], small, own, own_row, upstream, w_up, w_down, normed, inverse, z, active, slope, branch, hidden, dm, dh, du, keep, send, sums
    )
    write_rows(du, W_1, du_out)
    send_rows(flags[0], du_out, send_a, send_b)


def first_backward(
    flags, du1, du1_a, du1_b, small1, small0, mask, own, own_row, active, slope, branch, w_up, w_down, kept,
    e_own, du_out, send_a, send_b, keep, send, sums,
    pad, taps, hidden, upstream, z, dm, dh, du, normed, inverse, sems,
):
    copies = kept_copies(kept, sems, [(upstream, AT_E_0), (normed, AT_NORMED), (inverse, AT_INVERSE)], False)
    for copy in copies:
        copy.start()
    shift = SIDE_0 + REACH - SIDE_1
    pad[:, :, 0:8, :] = jnp.zeros((2, ROWS_DEV + 2 * REACH, 8, HALF), f32)
    pad[:, :, W_X - 16 : W_X, :] = jnp.zeros((2, ROWS_DEV + 2 * REACH, 16, HALF), f32)
    load_padded(pad, flags[0], du1, du1_a, du1_b, shift)
    load_taps(taps, small1)
    for copy in copies:
        copy.wait()
    for group in groups(W_0, 4):
        starts = [tile * 8 for tile in group]
        for half in range(2):
            spread = conv_tiles(pad, taps, half, starts, True)
            for index, start in enumerate(starts):
                for row in range(ROWS_DEV):
                    at = slice(row * W_0 + start, row * W_0 + start + 8)
                    value = (upstream[at, lanes(half)] + spread[index][row]).astype(bf16).astype(f32)
                    upstream[at, lanes(half)] = mask[at, :] * value
    for row in range(ROWS_DEV):
        at = row * W_0 + SIDE_0
        e_own[row] = upstream[at : at + W_OWN, :]
    scale_cells(N_0, small0, normed, z)
    backward_cells(
        W_0, flags[0], small0, own, own_row, upstream, w_up, w_down, normed, inverse, z, active, slope, branch, hidden, dm, dh, du, keep, send, sums
    )
    write_rows(du, W_0, du_out)
    send_rows(flags[0], du_out, send_a, send_b)


def input_grad(flags, du, du_a, du_b, small, e_own, out, pad, taps, total):
    load_padded(pad, flags[0], du, du_a, du_b)
    load_taps(taps, small)
    for group in groups(W_OWN, 5):
        starts = [tile * 8 for tile in group]
        for half in range(2):
            spread = conv_tiles(pad, taps, half, [start + SIDE_0 - REACH for start in starts], True)
            for index, start in enumerate(starts):
                for row in range(ROWS_DEV):
                    at = slice(start, start + 8)
                    total[row, at, lanes(half)] = e_own[row, at, lanes(half)] + spread[index][row]
    for row in range(ROWS_DEV):
        out[row] = total[row, 0:COLS_DEV, :].astype(bf16)


def tap_grads_1(flags, pad, du, own, sums, out, grads, total):
    tap_sums(W_1, pad, du, own, sums, out, grads, total)


def tap_grads_0(flags, v, v_a, v_b, du, own, sums, out, pad, grads, total):
    load_padded(pad, flags[0], v, v_a, v_b)
    tap_sums(W_0, pad, du, own, sums, out, grads, total)


def tap_sums(width, pad, du, own, sums, out, grads, total):
    for row in range(ROWS_DEV):
        inside = own[row * width : (row + 1) * width, :]
        grads[row] = du[row].astype(f32) * twice(inside)
    total[...] = jnp.zeros((SMALL, WIDE), f32)
    for half in range(2):
        for offsets in (range(0, 4), range(4, KERNEL)):
            partial = [[None] * KERNEL for _ in offsets]
            for tile in range(width // 8):
                start = tile * 8
                grad = [grads[row, start : start + 8, lanes(half)] for row in range(ROWS_DEV)]
                for row in range(ROWS_DEV + KERNEL - 1):
                    for index, col_off in enumerate(offsets):
                        window = pad[half, row, start + col_off : start + col_off + 8, :]
                        for out_row in range(ROWS_DEV):
                            row_off = row - out_row
                            if 0 <= row_off < KERNEL:
                                term = window * grad[out_row]
                                held = partial[index][row_off]
                                partial[index][row_off] = term if held is None else held + term
            for index, col_off in enumerate(offsets):
                for row_off in range(KERNEL):
                    tap = row_off * KERNEL + col_off
                    total[tap : tap + 1, lanes(half)] = jnp.sum(partial[index][row_off], axis=0, keepdims=True)
    total[TAPS : TAPS + 9, :] = sums[0:9, :]
    out[...] = total[...].astype(bf16)


def finish(flags, piece, small, got, up, down, taps, channels, bias, up_vmem, down_vmem, sems):
    factor = 1.0 / math.sqrt(BATCH * ROWS_DEV * COLS_DEV)

    def copies(quarter):
        cols = slice(quarter * WIDE, (quarter + 1) * WIDE)
        return (
            pltpu.make_async_copy(up_vmem.at[:, cols], up.at[0, :, cols], sems.at[0, quarter]),
            pltpu.make_async_copy(down_vmem.at[cols, :], down.at[0, cols, :], sems.at[1, quarter]),
        )

    def write(up_rows, down_rows):
        for quarter in range(QUARTERS):
            cols = slice(quarter * WIDE, (quarter + 1) * WIDE)
            up_vmem[:, cols] = up_rows[cols, :].astype(f32) * factor
            down_vmem[cols, :] = down_rows[cols, :].astype(f32) * factor
            for copy in copies(quarter):
                copy.start()

    @pl.when(flags[0] == 0)
    def _():
        write(piece, got)

    @pl.when(flags[0] == 1)
    def _():
        write(got, piece)

    sums = (small[...].astype(f32) + got[HID:, :].astype(f32)) * factor
    taps[0] = sums[:TAPS]
    channels[0] = sums[TAPS : TAPS + 5]
    for quarter in range(QUARTERS):
        bias[:, quarter * WIDE : (quarter + 1) * WIDE] = sums[TAPS + 5 + quarter : TAPS + 6 + quarter]
    for quarter in range(QUARTERS):
        for copy in copies(quarter):
            copy.wait()


def in_vmem():
    return pl.BlockSpec(memory_space=pltpu.VMEM)


def call(body, name, inputs, outputs, scratch, flops, hbm_in=0, hbm_out=0, sems=()):
    in_hbm = pl.BlockSpec(memory_space=pltpu.HBM)
    return pl.pallas_call(
        body,
        name=name,
        out_shape=[jax.ShapeDtypeStruct(shape, dtype) for shape, dtype in outputs],
        in_specs=[pl.BlockSpec(memory_space=pltpu.SMEM)] + [in_vmem()] * (len(inputs) - 1 - hbm_in) + [in_hbm] * hbm_in,
        out_specs=[in_hbm] * hbm_out + [in_vmem()] * (len(outputs) - hbm_out),
        scratch_shapes=[pltpu.VMEM(shape, dtype) for shape, dtype in scratch] + [pltpu.SemaphoreType.DMA(shape) for shape in sems],
        compiler_params=pltpu.CompilerParams(vmem_limit_bytes=28 << 20),
        cost_estimate=pl.CostEstimate(flops=10 * flops, bytes_accessed=4 << 20, transcendentals=0),
    )(*inputs)


def swap_pairs(count, bit):
    return [(i, i ^ bit) for i in range(count)]


def on_device(
    window_input,
    output_cotangent,
    ocean_mask,
    dw_kernel,
    channel_params,
    up_weight,
    up_bias,
    down_weight,
):
    section = lax.axis_index("section")
    lat = lax.axis_index("lat")
    lon = lax.axis_index("lon")
    n_lat, n_lon = lax.axis_size("lat"), lax.axis_size("lon")
    odd = lat % 2
    flags = jnp.stack([odd, section]).astype(jnp.int32)
    channels = window_input.shape[-1]

    def over_section(value):
        return lax.ppermute(value, "section", [(0, 1), (1, 0)])

    def over_core(value):
        return lax.ppermute(value, "lat", swap_pairs(n_lat, 1))

    def lat_halo(send_a, send_b):
        pairs = [(i, i + 1) for i in range(1, n_lat - 1, 2)]
        pairs += [(j, i) for i, j in pairs]
        return over_core(send_a), lax.ppermute(send_b, "lat", pairs)

    def by_core(even, other):
        return jnp.where(odd == 0, even, other)

    x = lax.dynamic_index_in_dim(window_input, section, 0, False)
    cot = lax.dynamic_index_in_dim(output_cotangent, section, 0, False)
    sea = ocean_mask.astype(bf16)

    def packed(x_part, cot_part, sea_part):
        sea_row = jnp.pad(sea_part, ((0, 0), (0, channels - sea_part.shape[1])))[:, None, :]
        return jnp.concatenate([x_part, cot_part, sea_row], axis=1)

    ring = [(i, (i + 1) % n_lon) for i in range(n_lon)]
    left = lax.ppermute(packed(x[:, -SIDE_X:], cot[:, -SIDE_1:], sea[:, -SIDE_0:]), "lon", ring)
    right = lax.ppermute(packed(x[:, :SIDE_X], cot[:, :SIDE_1], sea[:, :SIDE_0]), "lon", [(j, i) for i, j in ring])
    small_own = jnp.concatenate(
        [dw_kernel[0], channel_params[0], up_bias[0].reshape(QUARTERS, WIDE), jnp.zeros((SMALL - TAPS - 9, WIDE), bf16)], axis=0
    )
    up, down = up_weight[0], down_weight[0]
    cut = channels // 2
    small_got = over_section(small_own)
    send_up = by_core(up[:cut], up[cut:])
    send_down = by_core(down[: HID // 2], down[HID // 2 :])
    send_up, send_down, left, right, small_got = lax.optimization_barrier((send_up, send_down, left, right, small_got))
    got_up, got_down = over_section(send_up), over_section(send_down)
    small_0 = jnp.where(section == 0, small_own, small_got).astype(f32)
    small_1 = jnp.where(section == 0, small_got, small_own).astype(f32)

    before = SIDE_0 - SIDE_1
    sea_at = SIDE_X + SIDE_1
    x_wide = jnp.concatenate([left[:, :SIDE_X], x, right[:, :SIDE_X], jnp.zeros((ROWS_DEV, W_X - COLS_DEV - 2 * SIDE_X, channels), bf16)], axis=1)
    x_a, x_b = lat_halo(by_core(x_wide[1:], x_wide[:REACH]), by_core(x_wide[:REACH], x_wide[1:]))
    mask_wide = jnp.concatenate(
        [left[:, sea_at, :SIDE_0], sea, right[:, sea_at, :SIDE_0], jnp.zeros((ROWS_DEV, W_0 - COLS_DEV - 2 * SIDE_0), bf16)], axis=1
    )
    before = SIDE_0 - SIDE_1
    def spread_lanes(mask):
        flat = mask.astype(f32).reshape(-1, 1)
        return jnp.broadcast_to(flat, (flat.shape[0], HALF))

    mask_0, mask_1 = spread_lanes(mask_wide), spread_lanes(mask_wide[:, before : before + W_1])

    def own_cells(width, side):
        column = jnp.arange(width)
        inside = ((column >= side) & (column < side + COLS_DEV)).astype(f32)
        flat = jnp.tile(inside, ROWS_DEV)
        return jnp.broadcast_to(flat[:, None], (flat.shape[0], HALF)), jnp.broadcast_to(flat[None, :], (16, flat.shape[0])).astype(bf16)

    owN_0, row_0 = own_cells(W_0, SIDE_0)
    owN_1, row_1 = own_cells(W_1, SIDE_1)

    deep = ROWS_DEV + 2 * REACH
    taps_scratch = ((2, TAPS, 8, HALF), f32)

    (kept,) = call(
        first_conv,
        "first_conv",
        (flags, x_wide, x_a, x_b, small_0, mask_0, cot, left, right),
        [((KEPT_ROWS, WIDE), f32)],
        [
            ((2, deep, W_X, HALF), f32), taps_scratch, ((N_0, WIDE), f32), ((N_0, WIDE), f32), ((N_0, HALF), f32),
            ((N_0, WIDE), bf16), ((N_0, WIDE), f32), ((N_1, WIDE), f32),
        ],
        2_000_000_000,
        hbm_out=1,
        sems=((5,),),
    )
    got_up, got_down, kept = lax.optimization_barrier((got_up, got_down, kept))
    other_up, other_down = over_core(got_up), over_core(got_down)
    weights = (up, down, got_up, got_down, other_up, other_down)
    y, y_send_a, y_send_b = call(
        first_forward,
        "first_forward",
        (flags, small_0, mask_0, kept) + weights,
        [((ROWS_DEV, W_0, WIDE), bf16), ((REACH, W_0, WIDE), bf16), ((REACH, W_0, WIDE), bf16)],
        [
            ((N_0, WIDE), f32), ((N_0, WIDE), bf16), ((N_0, WIDE), f32), ((2, N_0, WIDE), f32), ((N_0, WIDE), f32),
            ((N_0, HID), bf16), ((N_0, HID), f32), ((N_0, WIDE), f32), ((WIDE, HID), bf16), ((HID, WIDE), bf16),
        ],
        2_000_000_000,
        hbm_in=7,
        sems=((6,), (2,)),
    )
    y_a, y_b = lat_halo(y_send_a, y_send_b)
    final, du1, du1_send_a, du1_send_b, keep_1, send_1, sums_1, pad_1 = call(
        second_block,
        "second_block",
        (flags, y, y_a, y_b, small_1, mask_1, owN_1, row_1, kept) + weights,
        [
            ((ROWS_DEV, COLS_DEV, WIDE), bf16), ((ROWS_DEV, W_1, WIDE), bf16), ((REACH, W_1, WIDE), bf16), ((REACH, W_1, WIDE), bf16),
            ((HID, WIDE), bf16), ((HID, WIDE), bf16), ((16, WIDE), f32), ((2, deep, W_0, HALF), f32),
        ],
        [
            taps_scratch, ((2, N_1, WIDE), f32), ((N_1, WIDE), f32),
            ((N_1, WIDE), f32), ((N_1, HALF), f32), ((N_1, WIDE), bf16), ((N_1, WIDE), f32), ((N_1, HID), bf16), ((N_1, HID), f32), ((N_1, WIDE), f32),
            ((WIDE, HID), bf16), ((HID, WIDE), bf16), ((N_1, WIDE), f32), ((N_1, WIDE), bf16), ((N_1, HID), bf16), ((N_1, WIDE), f32),
        ],
        4_000_000_000,
        hbm_in=7,
        sems=((6,), (1,)),
    )
    du1_a, du1_b = lat_halo(du1_send_a, du1_send_b)
    small_again, _ = lax.optimization_barrier((small_0, du1_send_a))
    active, slope, branch, w_up, w_down = call(
        first_again,
        "first_again",
        (flags, small_again, kept) + weights,
        [((N_0, HID), bf16), ((N_0, HID), f32), ((N_0, WIDE), f32), ((WIDE, HID), bf16), ((HID, WIDE), bf16)],
        [((N_0, WIDE), f32), ((N_0, WIDE), bf16), ((2, N_0, WIDE), f32)],
        2_000_000_000,
        hbm_in=7,
        sems=((6,), (1,)),
    )
    send_1, du1_a, du1_b, active = lax.optimization_barrier((send_1, du1_a, du1_b, active))
    e_own, du0, du0_send_a, du0_send_b, keep_0, send_0, sums_0 = call(
        first_backward,
        "first_backward",
        (flags, du1, du1_a, du1_b, small_1, small_0, mask_0, owN_0, row_0, active, slope, branch, w_up, w_down, kept),
        [
            ((ROWS_DEV, W_OWN, WIDE), f32), ((ROWS_DEV, W_0, WIDE), bf16), ((REACH, W_0, WIDE), bf16), ((REACH, W_0, WIDE), bf16),
            ((HID, WIDE), bf16), ((HID, WIDE), bf16), ((16, WIDE), f32),
        ],
        [
            ((2, deep, W_X, HALF), f32), taps_scratch, ((2, N_0, WIDE), f32), ((N_0, WIDE), f32), ((N_0, WIDE), bf16),
            ((N_0, WIDE), bf16), ((N_0, HID), bf16), ((N_0, WIDE), f32),
            ((N_0, WIDE), f32), ((N_0, HALF), f32),
        ],
        3_000_000_000,
        hbm_in=1,
        sems=((3,),),
    )
    bits = [("lat", 1 << i) for i in range(1, n_lat.bit_length() - 1)] + [("lon", 1 << i) for i in range(n_lon.bit_length() - 1)]
    orders = (bits, bits[1:] + bits[:1])

    def partner(place, step):
        row, col = place
        axis, bit = orders[row % 2][step]
        return (row ^ bit, col) if axis == "lat" else (row, col ^ bit)

    def exchange(value, step):
        pairs = []
        for row in range(n_lat):
            for col in range(n_lon):
                other = partner((row, col), step)
                pairs.append((row * n_lon + col, other[0] * n_lon + other[1]))
        return lax.ppermute(value, ("lat", "lon"), pairs)

    def side(step):
        def of(order):
            axis, bit = order[step]
            return ((lat if axis == "lat" else lon) // bit) % 2

        return jnp.where(odd == 0, of(orders[0]), of(orders[1]))

    def plus(first, second):
        return (first.astype(f32) + second.astype(f32)).astype(bf16)

    def reduce_scatter(keep, send):
        piece = plus(keep, over_core(send))
        for step in range(len(bits)):
            half = piece.shape[0] // 2
            low, high = piece[:half], piece[half:]
            which = side(step) == 0
            piece = plus(jnp.where(which, low, high), exchange(jnp.where(which, high, low), step))
        return piece

    def reduce_step(piece, step):
        half = piece.shape[0] // 2
        low, high = piece[:half], piece[half:]
        which = side(step) == 0
        return plus(jnp.where(which, low, high), exchange(jnp.where(which, high, low), step))

    to_first = section == 0

    def chosen(first, second):
        return jnp.where(to_first, first, second)

    core_1 = over_core(send_1)
    core_0 = over_core(send_0)
    piece_1 = plus(keep_1, core_1)
    du0_a, du0_b = lat_halo(du0_send_a, du0_send_b)
    (taps_1,) = call(
        tap_grads_1, "tap_grads_1", (flags, pad_1, du1, owN_1, sums_1), [((SMALL, WIDE), bf16)],
        [((ROWS_DEV, W_1, WIDE), f32), ((SMALL, WIDE), f32)], 2_000_000_000,
    )
    (taps_0,) = call(
        tap_grads_0, "tap_grads_0", (flags, x_wide, x_a, x_b, du0, owN_0, sums_0), [((SMALL, WIDE), bf16)],
        [((2, deep, W_X, HALF), f32), ((ROWS_DEV, W_0, WIDE), f32), ((SMALL, WIDE), f32)], 2_000_000_000,
    )
    piece_0, taps_0, taps_1 = lax.optimization_barrier((plus(keep_0, core_0), taps_0, taps_1))
    steps = len(bits)
    for step in range(steps):
        piece_1, piece_0 = reduce_step(piece_1, step), reduce_step(piece_0, step)
        if step == 0:
            (start,) = call(
                input_grad, "input_grad", (flags, du0, du0_a, du0_b, small_0, e_own), [((ROWS_DEV, COLS_DEV, WIDE), bf16)],
                [((2, deep, W_0, HALF), f32), taps_scratch, ((ROWS_DEV, W_OWN, WIDE), f32)], 2_000_000_000,
            )
            other_end = over_section(chosen(final, start))
            piece_0, start = lax.optimization_barrier((piece_0, start))
    cut = piece_0.shape[0]
    piece_0, other_end = lax.optimization_barrier((piece_0, other_end))
    boundary = jnp.stack([chosen(start, other_end), chosen(other_end, final)])[None]

    def both(piece, small):
        return jnp.concatenate([piece, small], axis=0)

    got = over_section(both(chosen(piece_1, piece_0), chosen(taps_1, taps_0)))
    got, boundary = lax.optimization_barrier((got, boundary))
    piece = plus(chosen(piece_0, piece_1), got[:cut])
    small = plus(chosen(taps_0, taps_1), got[cut:])
    for step in reversed(range(len(bits))):
        got = exchange(both(piece, small), step)
        cut = piece.shape[0]
        small = plus(small, got[cut:])
        which = side(step) == 0
        piece = jnp.where(which, jnp.concatenate([piece, got[:cut]]), jnp.concatenate([got[:cut], piece]))
    got = over_core(both(piece, small))
    grad_up, grad_down, grad_taps, grad_channels, grad_bias = call(
        finish,
        "finish",
        (flags, piece, small, got),
        [((1, WIDE, HID), f32), ((1, HID, WIDE), f32), ((1, TAPS, WIDE), f32), ((1, 5, WIDE), f32), ((1, HID), f32)],
        [((WIDE, HID), f32), ((HID, WIDE), f32)],
        10_000_000,
        hbm_out=2,
        sems=((2, QUARTERS),),
    )
    return (
        boundary,
        grad_taps,
        grad_channels,
        grad_up,
        grad_bias,
        grad_down,
    )


def solution(mesh):
    in_specs = (
        P(None, "lat", "lon", None),
        P(None, "lat", "lon", None),
        P("lat", "lon"),
        P("section", None, None),
        P("section", None, None),
        P("section", None, None),
        P("section", None),
        P("section", None, None),
    )
    out_specs = (
        P("section", None, "lat", "lon", None),
        P("section", None, None),
        P("section", None, None),
        P("section", None, None),
        P("section", None),
        P("section", None, None),
    )
    return jax.shard_map(
        on_device, mesh=mesh, in_specs=in_specs, out_specs=out_specs, check_vma=False
    )
```

time: 139 us -> 123 us (0.88); the launches traced: 137 us -> 123 us
  Pallas kernels: 38.7 us -> 29 us
  local copies, waits for them, and re-layouts: 12 us -> 6.01 us
  waiting for transfers between devices: 36.2 us -> 41.3 us
  starting transfers between devices: 43.3 us -> 40.6 us
    ppermute x9, waiting for transfers between devices: 15 us -> 28.9 us  [exchange(): return lax.ppermute(value, ('lat', 'lon'), pairs)]
    ppermute x5, waiting for transfers between devices: 15 us -> 2.19 us  [over_section(): return lax.ppermute(value, 'section', [(0, 1), (1, 0)])]
    pallas_call x6 -> x9, Pallas kernels: 38.7 us -> 29 us  [call(): pl.pallas_call(body, name=name, out_shape=[jax.ShapeDtypeStruct(shape, dt...]
    ppermute x9, starting transfers between devices: 14.2 us -> 8.53 us  [over_core(): return lax.ppermute(value, 'lat', swap_pairs(n_lat, 1))]
    ppermute x4, starting transfers between devices: 12.1 us -> 15.3 us  [lat_halo(): return (over_core(send_a), lax.ppermute(send_b, 'lat', pairs))]
    broadcast_in_dim x2 -> x0, other arithmetic: 2.27 us -> none  [the longest x1 1.18 us: on_device(): grad_down[None]]
    ppermute x9, waiting for transfers between devices: 0.02 us -> 1.9 us  [over_core(): return lax.ppermute(value, 'lat', swap_pairs(n_lat, 1))]
    broadcast_in_dim x3, local copies, waits for them, and re-layouts: 1.79 us -> 0.29 us  [spread_lanes(): return jnp.broadcast_to(flat, (flat.shape[0], HALF))]
  transfers between devices with their start and end apart: 29 -> 29, of which waited for: 13 -> 16; matrix products, arithmetic and copies ran while one was open for 5% -> 4% of each run, Pallas kernels for 13% -> 10%
where the time goes in v2:
time: 123 us
  waiting for transfers between devices  41.3 us (34%)
  starting transfers between devices  40.6 us (33%)
  Pallas kernels  29 us (24%)
  local copies, waits for them, and re-layouts  6.01 us (5%)
  other arithmetic  4.37 us (4%)
  between operations  1.31 us (1%)
    pallas_call x9, Pallas kernels, call(): pl.pallas_call(body, name=name, out_shape=[jax.ShapeDtypeStruct(shape, dt...  29 us
    ppermute x9, waiting for transfers between devices, exchange(): return lax.ppermute(value, ('lat', 'lon'), pairs)  28.9 us
    ppermute x4, starting transfers between devices, lat_halo(): return (over_core(send_a), lax.ppermute(send_b, 'lat', pairs))  15.3 us
    ppermute x9, starting transfers between devices, over_core(): return lax.ppermute(value, 'lat', swap_pairs(n_lat, 1))  8.53 us
    ppermute x9, starting transfers between devices, exchange(): return lax.ppermute(value, ('lat', 'lon'), pairs)  8.24 us
    ppermute x4, waiting for transfers between devices, lat_halo(): return (over_core(send_a), lax.ppermute(send_b, 'lat', pairs))  7.19 us
    ppermute x5, starting transfers between devices, over_section(): return lax.ppermute(value, 'section', [(0, 1), (1, 0)])  5.17 us
    unnamed x21, local copies, waits for them, and re-layouts  3.72 us
  transfers between devices with their start and end apart: 29, of which 16 were waited for; matrix products, arithmetic and copies ran while one was open for 4% of the time, Pallas kernels for 10%

profile of v2, /device:TPU:1, one launch (start us, length us, event | category | flops | bytes accessed | tf_op | source)
XLA Modules:
  0.0 122.6 jit_solution(4694565886568586341)
XLA Ops:
  2.4 2.1 %collective-permute-start.2 = (bf16[64,256]{1,0:T(8,128)(2,1)S(1)}, bf16[64,256]{1,0:T(8,128)(2,1)S(1)}, u32[]{:S(2)}, u32[]{:S(2)}) collective-permute-start(bf16[64,256]{1,0:T(8,128)(2,1)S(1)} %maximum_maximum_fusion.1), channel_id=1, source_target_pairs={{0,16},{16,0},{1,17},{17,1},{2,18},{18,2},{3,19},{19,3},{4,20},{20... | collective-permute-start | bytes 98312 | tf_op jit(solution)/shard_map/ppermute | solution.py:521
  6.5 1.3 %collective-permute-start = (bf16[4,19,256]{2,1,0:T(8,128)(2,1)S(1)}, bf16[4,19,256]{2,1,0:T(8,128)(2,1)S(1)}, u32[]{:S(2)}, u32[]{:S(2)}) collective-permute-start(bf16[4,19,256]{2,1,0:T(8,128)(2,1)S(1)} %pad_maximum_fusion.5), channel_id=1, source_target_pairs={{0,1},{1,2},{2,3},{3,0},{4,5},{5,6},{6,7},{7,4},{8,9},{9,10},{10,1... | collective-permute-start | bytes 116744 | tf_op jit(solution)/shard_map/ppermute | solution.py:543
  7.9 2.1 %collective-permute-start.1 = (bf16[4,19,256]{2,1,0:T(8,128)(2,1)S(1)}, bf16[4,19,256]{2,1,0:T(8,128)(2,1)S(1)}, u32[]{:S(2)}, u32[]{:S(2)}) collective-permute-start(bf16[4,19,256]{2,1,0:T(8,128)(2,1)S(1)} %pad_maximum_fusion.6), channel_id=1, source_target_pairs={{1,0},{2,1},{3,2},{0,3},{5,4},{6,5},{7,6},{4,7},{9,8},{10,9},{11,1... | collective-permute-start | bytes 116744 | tf_op jit(solution)/shard_map/ppermute | solution.py:544
  11.9 1.2 collective-permute-start.4
  13.2 6.0 %collective-permute-start.6 = (bf16[3,96,256]{2,1,0:T(8,128)(2,1)S(1)}, bf16[3,96,256]{2,1,0:T(8,128)(2,1)S(1)}, u32[]{:S(2)}, u32[]{:S(2)}) collective-permute-start(bf16[3,96,256]{2,1,0:T(8,128)(2,1)S(1)} %get-tuple-element.126), channel_id=1, source_target_pairs={{4,8},{8,4},{5,9},{9,5},{6,10},{10,6},{7,11},{11,7},{20,24},{24,20... | collective-permute-start | bytes 442376 | tf_op jit(solution)/shard_map/ppermute | solution.py:529
  19.4 2.9 %collective-permute-done.6.x_b.v_b = bf16[3,96,256]{2,1,0:T(8,128)(2,1)S(1)} collective-permute-done((bf16[3,96,256]{2,1,0:T(8,128)(2,1)S(1)}, bf16[3,96,256]{2,1,0:T(8,128)(2,1)S(1)}, u32[]{:S(2)}, u32[]{:S(2)}) %collective-permute-start.6) | collective-permute-done | bytes 147488 | tf_op jit(solution)/shard_map/ppermute | solution.py:529
  22.4 4.5 %first_conv.1.kept = f32[40960,256]{1,0:T(8,128)} custom-call(s32[2]{0:T(128)S(1)} %pad_add_fusion.flags, bf16[4,96,256]{2,1,0:T(8,128)(2,1)S(1)} %maximum_maximum_fusion.x.v, bf16[3,96,256]{2,1,0:T(8,128)(2,1)S(1)} %collective-permute-done.5.x_a.v_a, bf16[3,96,256]{2,1,0:T(8,128)(2,1)S(1)} %collective-permute-done.6.x_b.v_b, ...), custom_call_target="tpu_custom_call" | custom-call | flops 20000000000 | bytes 4194304 | tf_op jit(solution)/shard_map/first_conv/pallas_call | solution.py:486
  29.0 3.2 %first_forward.1 = (bf16[4,88,256]{2,1,0:T(8,128)(2,1)S(1)}, bf16[3,88,256]{2,1,0:T(8,128)(2,1)}, bf16[3,88,256]{2,1,0:T(8,128)(2,1)S(1)}) custom-call(s32[2]{0:T(128)S(1)} %pad_add_fusion.flags, f32[64,256]{1,0:T(8,128)S(1)} %get-tuple-element.71.small.small0, f32[352,128]{1,0:T(8,128)S(1)} %broadcast_in_dim.69.mask, f32[40960,256]{1,0:T(8,128)} %first_conv.1.kept, ...), custom_call_target="tpu_custom_call" | custom-call | flops 20000000000 | bytes 4194304 | tf_op jit(solution)/shard_map/first_forward/pallas_call | solution.py:486
  33.0 3.3 %collective-permute-start.10 = (bf16[3,88,256]{2,1,0:T(8,128)(2,1)S(1)}, bf16[3,88,256]{2,1,0:T(8,128)(2,1)S(1)}, u32[]{:S(2)}, u32[]{:S(2)}) collective-permute-start(bf16[3,88,256]{2,1,0:T(8,128)(2,1)S(1)} %get-tuple-element.66), channel_id=1, source_target_pairs={{4,8},{8,4},{5,9},{9,5},{6,10},{10,6},{7,11},{11,7},{20,24},{24,20... | collective-permute-start | bytes 405512 | tf_op jit(solution)/shard_map/ppermute | solution.py:529
  36.5 2.8 %collective-permute-done.10.y_b = bf16[3,88,256]{2,1,0:T(8,128)(2,1)S(1)} collective-permute-done((bf16[3,88,256]{2,1,0:T(8,128)(2,1)S(1)}, bf16[3,88,256]{2,1,0:T(8,128)(2,1)S(1)}, u32[]{:S(2)}, u32[]{:S(2)}) %collective-permute-start.10) | collective-permute-done | bytes 135200 | tf_op jit(solution)/shard_map/ppermute | solution.py:529
  40.4 5.6 %second_block.1 = (bf16[4,68,256]{2,1,0:T(8,128)(2,1)S(1)}, bf16[4,80,256]{2,1,0:T(8,128)(2,1)S(1)}, bf16[3,80,256]{2,1,0:T(8,128)(2,1)S(1)}, bf16[3,80,256]{2,1...) custom-call(s32[2]{0:T(128)S(1)} %pad_add_fusion.flags, ...), custom_call_target="tpu_custom_call" | custom-call | flops 40000000000 | bytes 4194304 | tf_op jit(solution)/shard_map/second_block/pallas_call | solution.py:486
  46.1 3.5 %collective-permute-start.12 = (bf16[3,80,256]{2,1,0:T(8,128)(2,1)S(1)}, bf16[3,80,256]{2,1,0:T(8,128)(2,1)S(1)}, u32[]{:S(2)}, u32[]{:S(2)}) collective-permute-start(bf16[3,80,256]{2,1,0:T(8,128)(2,1)S(1)} %get-tuple-element.70), channel_id=1, source_target_pairs={{4,8},{8,4},{5,9},{9,5},{6,10},{10,6},{7,11},{11,7},{20,24},{24,20... | collective-permute-start | bytes 368648 | tf_op jit(solution)/shard_map/ppermute | solution.py:529
  49.6 1.7 %tap_grads_1.1 = bf16[64,256]{1,0:T(8,128)(2,1)S(1)} custom-call(s32[2]{0:T(128)S(1)} %pad_add_fusion.flags, f32[2,10,88,128]{3,2,1,0:T(8,128)S(1)} %get-tuple-element.86.pad, bf16[4,80,256]{2,1,0:T(8,128)(2,1)S(1)} %get-tuple-element.74.du1.du, f32[320,128]{1,0:T(8,128)S(1)} %broadcast_in_dim.75.own, f32[16,256]{1,0:T(8,128)S(1)} %get-tuple-element.87.sums), custom_call_target="tpu_custom_call" | custom-call | flops 20000000000 | bytes 4194304 | tf_op jit(solution)/shard_map/tap_grads_1/pallas_call | solution.py:486
  51.3 2.8 %first_again.1 = (bf16[352,1024]{1,0:T(8,128)(2,1)S(1)}, f32[352,1024]{1,0:T(8,128)S(1)}, f32[352,256]{1,0:T(8,128)S(1)}, bf16[256,1024]{1,0:T(8,128)(2,1)S(1)}, bf16[1024,256]{1,0:T(8,128)(2,1)S(1)}) custom-call(s32[2]{0:T(128)S(1)} %pad_add_fusion.flags, f32[64,256]{1,0:T(8,128)S(1)} %get-tuple-element.71.small.small0, f32[40960,256]{1,0:T(8,128)} %first_conv.1.kept, ...), custom_call_target="tpu_custom_call" | custom-call | flops 20000000000 | bytes 4194304 | tf_op jit(solution)/shard_map/first_again/pallas_call | solution.py:486
  54.2 5.3 %first_backward.1 = (f32[4,72,256]{2,1,0:T(8,128)S(1)}, bf16[4,88,256]{2,1,0:T(8,128)(2,1)S(1)}, bf16[3,88,256]{2,1,0:T(8,128)(2,1)S(1)}, bf16[3,88,256]{2,1,0:T...) custom-call(s32[2]{0:T(128)S(1)} %pad_add_fusion.flags, ...), custom_call_target="tpu_custom_call" | custom-call | flops 30000001024 | bytes 4194304 | tf_op jit(solution)/shard_map/first_backward/pallas_call | solution.py:486
  59.6 2.4 %collective-permute-start.20 = (bf16[3,88,256]{2,1,0:T(8,128)(2,1)S(1)}, bf16[3,88,256]{2,1,0:T(8,128)(2,1)S(1)}, u32[]{:S(2)}, u32[]{:S(2)}) collective-permute-start(bf16[3,88,256]{2,1,0:T(8,128)(2,1)S(1)} %get-tuple-element.90), channel_id=1, source_target_pairs={{4,8},{8,4},{5,9},{9,5},{6,10},{10,6},{7,11},{11,7},{20,24},{24,20... | collective-permute-start | bytes 405512 | tf_op jit(solution)/shard_map/ppermute | solution.py:529
  62.7 1.8 %tap_grads_0.1 = bf16[64,256]{1,0:T(8,128)(2,1)S(1)} custom-call(s32[2]{0:T(128)S(1)} %pad_add_fusion.flags, bf16[4,96,256]{2,1,0:T(8,128)(2,1)S(1)} %maximum_maximum_fusion.x.v, bf16[3,96,256]{2,1,0:T(8,128)(2,1)S(1)} %collective-permute-done.5.x_a.v_a, bf16[3,96,256]{2,1,0:T(8,128)(2,1)S(1)} %collective-permute-done.6.x_b.v_b, ...), custom_call_target="tpu_custom_call" | custom-call | flops 20000000000 | bytes 4194304 | tf_op jit(solution)/shard_map/tap_grads_0/pallas_call | solution.py:486
  64.5 1.4 %collective-permute-done.20.du_b = bf16[3,88,256]{2,1,0:T(8,128)(2,1)S(1)} collective-permute-done((bf16[3,88,256]{2,1,0:T(8,128)(2,1)S(1)}, bf16[3,88,256]{2,1,0:T(8,128)(2,1)S(1)}, u32[]{:S(2)}, u32[]{:S(2)}) %collective-permute-start.20) | collective-permute-done | bytes 135200 | tf_op jit(solution)/shard_map/ppermute | solution.py:529
  66.0 1.6 %input_grad.1 = bf16[4,68,256]{2,1,0:T(8,128)(2,1)S(1)} custom-call(s32[2]{0:T(128)S(1)} %pad_add_fusion.flags, bf16[4,88,256]{2,1,0:T(8,128)(2,1)S(1)} %get-tuple-element.84.du, bf16[3,88,256]{2,1,0:T(8,128)(2,1)S(1)} %collective-permute-done.19.du_a, bf16[3,88,256]{2,1,0:T(8,128)(2,1)S(1)} %collective-permute-done.20.du_b, ...), custom_call_target="tpu_custom_call" | custom-call | flops 20000000000 | bytes 4194304 | tf_op jit(solution)/shard_map/input_grad/pallas_call | solution.py:486
  69.9 3.8 %collective-permute-done.18 = bf16[512,256]{1,0:T(8,128)(2,1)S(1)} collective-permute-done((bf16[512,256]{1,0:T(8,128)(2,1)S(1)}, bf16[512,256]{1,0:T(8,128)(2,1)S(1)}, u32[]{:S(2)}, u32[]{:S(2)}) %collective-permute-start.18) | collective-permute-done | bytes 262176 | tf_op jit(solution)/shard_map/ppermute | solution.py:675
  73.8 2.1 %collective-permute-start.21 = (bf16[256,256]{1,0:T(8,128)(2,1)S(1)}, bf16[256,256]{1,0:T(8,128)(2,1)S(1)}, u32[]{:S(2)}, u32[]{:S(2)}) collective-permute-start(bf16[256,256]{1,0:T(8,128)(2,1)S(1)} %broadcast_select_fusion.5), channel_id=1, source_target_pairs={{0,1},{1,0},{2,3},{3,2},{4,6},{5,7},{6,4},{7,5},{8,9},{9,8},{10,11... | collective-permute-start | bytes 393224 | tf_op jit(solution)/shard_map/ppermute | solution.py:675
  76.3 2.1 %collective-permute-start.15 = (bf16[256,256]{1,0:T(8,128)(2,1)S(1)}, bf16[256,256]{1,0:T(8,128)(2,1)S(1)}, u32[]{:S(2)}, u32[]{:S(2)}) collective-permute-start(bf16[256,256]{1,0:T(8,128)(2,1)S(1)} %broadcast_select_fusion.6), channel_id=1, source_target_pairs={{0,1},{1,0},{2,3},{3,2},{4,6},{5,7},{6,4},{7,5},{8,9},{9,8},{10,11... | collective-permute-start | bytes 393224 | tf_op jit(solution)/shard_map/ppermute | solution.py:675
  79.9 2.6 %collective-permute-done.15 = bf16[256,256]{1,0:T(8,128)(2,1)S(1)} collective-permute-done((bf16[256,256]{1,0:T(8,128)(2,1)S(1)}, bf16[256,256]{1,0:T(8,128)(2,1)S(1)}, u32[]{:S(2)}, u32[]{:S(2)}) %collective-permute-start.15) | collective-permute-done | bytes 131104 | tf_op jit(solution)/shard_map/ppermute | solution.py:675
  82.8 3.0 %collective-permute-done.16 = bf16[128,256]{1,0:T(8,128)(2,1)S(1)} collective-permute-done((bf16[128,256]{1,0:T(8,128)(2,1)S(1)}, bf16[128,256]{1,0:T(8,128)(2,1)S(1)}, u32[]{:S(2)}, u32[]{:S(2)}) %collective-permute-start.16) | collective-permute-done | bytes 65568 | tf_op jit(solution)/shard_map/ppermute | solution.py:675
  85.9 1.3 %collective-permute-start.24 = (bf16[192,256]{1,0:T(8,128)(2,1)S(1)}, bf16[192,256]{1,0:T(8,128)(2,1)S(1)}, u32[]{:S(2)}, u32[]{:S(2)}) collective-permute-start(bf16[192,256]{1,0:T(8,128)(2,1)S(1)} %pad_maximum_fusion.3), channel_id=1, source_target_pairs={{0,16},{16,0},{1,17},{17,1},{2,18},{18,2},{3,19},{19,3},{4,20},{20... | collective-permute-start | bytes 294920 | tf_op jit(solution)/shard_map/ppermute | solution.py:521
  87.2 2.2 %collective-permute-done.24 = bf16[192,256]{1,0:T(8,128)(2,1)S(1)} collective-permute-done((bf16[192,256]{1,0:T(8,128)(2,1)S(1)}, bf16[192,256]{1,0:T(8,128)(2,1)S(1)}, u32[]{:S(2)}, u32[]{:S(2)}) %collective-permute-start.24) | collective-permute-done | bytes 98336 | tf_op jit(solution)/shard_map/ppermute | solution.py:521
  89.6 3.5 %collective-permute-done.25 = bf16[192,256]{1,0:T(8,128)(2,1)S(1)} collective-permute-done((bf16[192,256]{1,0:T(8,128)(2,1)S(1)}, bf16[192,256]{1,0:T(8,128)(2,1)S(1)}, u32[]{:S(2)}, u32[]{:S(2)}) %collective-permute-start.25) | collective-permute-done | bytes 98336 | tf_op jit(solution)/shard_map/ppermute | solution.py:675
  93.1 1.4 %collective-permute-start.26 = (bf16[320,256]{1,0:T(8,128)(2,1)S(1)}, bf16[320,256]{1,0:T(8,128)(2,1)S(1)}, u32[]{:S(2)}, u32[]{:S(2)}) collective-permute-start(bf16[320,256]{1,0:T(8,128)(2,1)S(1)} %pad_maximum_fusion.2), channel_id=1, source_target_pairs={{0,1},{1,0},{2,3},{3,2},{4,6},{5,7},{6,4},{7,5},{8,9},{9,8},{10,11... | collective-permute-start | bytes 491528 | tf_op jit(solution)/shard_map/ppermute | solution.py:675
  94.5 7.7 %collective-permute-done.26 = bf16[320,256]{1,0:T(8,128)(2,1)S(1)} collective-permute-done((bf16[320,256]{1,0:T(8,128)(2,1)S(1)}, bf16[320,256]{1,0:T(8,128)(2,1)S(1)}, u32[]{:S(2)}, u32[]{:S(2)}) %collective-permute-start.26) | collective-permute-done | bytes 163872 | tf_op jit(solution)/shard_map/ppermute | solution.py:675
  102.5 7.3 %collective-permute-done.27 = bf16[576,256]{1,0:T(8,128)(2,1)S(1)} collective-permute-done((bf16[576,256]{1,0:T(8,128)(2,1)S(1)}, bf16[576,256]{1,0:T(8,128)(2,1)S(1)}, u32[]{:S(2)}, u32[]{:S(2)}) %collective-permute-start.27) | collective-permute-done | bytes 294944 | tf_op jit(solution)/shard_map/ppermute | solution.py:675
  110.2 7.0 %collective-permute-start.28 = (bf16[1088,256]{1,0:T(8,128)(2,1)S(1)}, bf16[1088,256]{1,0:T(8,128)(2,1)S(1)}, u32[]{:S(2)}, u32[]{:S(2)}) collective-permute-start(bf16[1088,256]{1,0:T(8,128)(2,1)S(1)} %pad_maximum_fusion), channel_id=1, source_target_pairs={{0,4},{4,0},{8,12},{12,8},{1,5},{5,1},{9,13},{13,9},{2,6},{6,2},{1... | collective-permute-start | bytes 1671176 | tf_op jit(solution)/shard_map/ppermute | solution.py:524
  118.8 2.5 %finish.1 = (f32[1,256,1024]{2,1,0:T(8,128)}, f32[1,1024,256]{2,1,0:T(8,128)}, f32[1,49,256]{2,1,0:T(8,128)S(1)}, f32[1,5,256]{2,1,0:T(8,128)S(1)}, f32[1,1024]{1,0:T(1,128)}) custom-call(s32[2]{0:T(128)S(1)} %pad_add_fusion.flags, bf16[1024,256]{1,0:T(8,128)(2,1)S(1)} %maximum_select_fusion.piece, bf16[64,256]{1,0:T(8,128)(2,1)S(1)} %add_convert_fusion.9.small, ...), custom_call_target="tpu_custom_call" | custom-call | flops 100000000 | bytes 4194304 | tf_op jit(solution)/shard_map/finish/pallas_call | solution.py:486
  (141 shorter events, 18.9 us)
Async XLA Ops:
  0.6 9.3 %copy-start.2 = (bf16[1,256,1024]{2,1,0:T(8,128)(2,1)S(1)}, bf16[1,256,1024]{2,1,0:T(8,128)(2,1)}, u32[]{:S(2)}) copy-start(bf16[1,256,1024]{2,1,0:T(8,128)(2,1)} %param.13) | copy-start | bytes 1572868
  2.4 7.9 %collective-permute-start.2 = (bf16[64,256]{1,0:T(8,128)(2,1)S(1)}, bf16[64,256]{1,0:T(8,128)(2,1)S(1)}, u32[]{:S(2)}, u32[]{:S(2)}) collective-permute-start(bf16[64,256]{1,0:T(8,128)(2,1)S(1)} %maximum_maximum_fusion.1), channel_id=1, source_target_pairs={{0,16},{16,0},{1,17},{17,1},{2,18},{18,2},{3,19},{19,3},{4,20},{20... | collective-permute-start | bytes 98312 | tf_op jit(solution)/shard_map/ppermute | solution.py:521
  6.5 4.9 %collective-permute-start = (bf16[4,19,256]{2,1,0:T(8,128)(2,1)S(1)}, bf16[4,19,256]{2,1,0:T(8,128)(2,1)S(1)}, u32[]{:S(2)}, u32[]{:S(2)}) collective-permute-start(bf16[4,19,256]{2,1,0:T(8,128)(2,1)S(1)} %pad_maximum_fusion.5), channel_id=1, source_target_pairs={{0,1},{1,2},{2,3},{3,0},{4,5},{5,6},{6,7},{7,4},{8,9},{9,10},{10,1... | collective-permute-start | bytes 116744 | tf_op jit(solution)/shard_map/ppermute | solution.py:543
  7.9 3.5 %collective-permute-start.1 = (bf16[4,19,256]{2,1,0:T(8,128)(2,1)S(1)}, bf16[4,19,256]{2,1,0:T(8,128)(2,1)S(1)}, u32[]{:S(2)}, u32[]{:S(2)}) collective-permute-start(bf16[4,19,256]{2,1,0:T(8,128)(2,1)S(1)} %pad_maximum_fusion.6), channel_id=1, source_target_pairs={{1,0},{2,1},{3,2},{0,3},{5,4},{6,5},{7,6},{4,7},{9,8},{10,9},{11,1... | collective-permute-start | bytes 116744 | tf_op jit(solution)/shard_map/ppermute | solution.py:544
  10.0 9.3 %copy-start.6 = (bf16[1,49,256]{2,1,0:T(8,128)(2,1)S(1)}, bf16[1,49,256]{2,1,0:T(8,128)(2,1)}, u32[]{:S(2)}) copy-start(bf16[1,49,256]{2,1,0:T(8,128)(2,1)} %param.11) | copy-start | bytes 75268
  11.6 15.4 %collective-permute-start.3 = (bf16[128,1024]{1,0:T(8,128)(2,1)S(1)}, bf16[128,1024]{1,0:T(8,128)(2,1)S(1)}, u32[]{:S(2)}, u32[]{:S(2)}) collective-permute-start(bf16[128,1024]{1,0:T(8,128)(2,1)S(1)} %select_bitcast_fusion.1), channel_id=1, source_target_pairs={{0,16},{16,0},{1,17},{17,1},{2,18},{18,2},{3,19},{19,3},{4,20},{20... | collective-permute-start | bytes 786440 | tf_op jit(solution)/shard_map/ppermute | solution.py:521
  11.9 15.1 %collective-permute-start.4 = (bf16[512,256]{1,0:T(8,128)(2,1)S(1)}, bf16[512,256]{1,0:T(8,128)(2,1)S(1)}, u32[]{:S(2)}, u32[]{:S(2)}) collective-permute-start(bf16[512,256]{1,0:T(8,128)(2,1)S(1)} %select_bitcast_fusion), channel_id=1, source_target_pairs={{0,16},{16,0},{1,17},{17,1},{2,18},{18,2},{3,19},{19,3},{4,20},{20... | collective-permute-start | bytes 786440 | tf_op jit(solution)/shard_map/ppermute | solution.py:521
  13.2 9.1 %collective-permute-start.6 = (bf16[3,96,256]{2,1,0:T(8,128)(2,1)S(1)}, bf16[3,96,256]{2,1,0:T(8,128)(2,1)S(1)}, u32[]{:S(2)}, u32[]{:S(2)}) collective-permute-start(bf16[3,96,256]{2,1,0:T(8,128)(2,1)S(1)} %get-tuple-element.126), channel_id=1, source_target_pairs={{4,8},{8,4},{5,9},{9,5},{6,10},{10,6},{7,11},{11,7},{20,24},{24,20... | collective-permute-start | bytes 442376 | tf_op jit(solution)/shard_map/ppermute | solution.py:529
  19.2 3.1 %collective-permute-start.5 = (bf16[3,96,256]{2,1,0:T(8,128)(2,1)S(1)}, bf16[3,96,256]{2,1,0:T(8,128)(2,1)S(1)}, u32[]{:S(2)}, u32[]{:S(2)}) collective-permute-start(bf16[3,96,256]{2,1,0:T(8,128)(2,1)S(1)} %get-tuple-element.127), channel_id=1, source_target_pairs={{0,4},{4,0},{8,12},{12,8},{1,5},{5,1},{9,13},{13,9},{2,6},{6,2},{1... | collective-permute-start | bytes 442376 | tf_op jit(solution)/shard_map/ppermute | solution.py:524
  27.0 1.6 %collective-permute-start.7 = (bf16[128,1024]{1,0:T(8,128)(2,1)S(1)}, bf16[128,1024]{1,0:T(8,128)(2,1)S(1)}, u32[]{:S(2)}, u32[]{:S(2)}) collective-permute-start(bf16[128,1024]{1,0:T(8,128)(2,1)S(1)} %collective-permute-done.3.refs_2_), channel_id=1, source_target_pairs={{0,4},{4,0},{8,12},{12,8},{1,5},{5,1},{9,13},{13,9},{2,6},{6,2},{1... | collective-permute-start | bytes 786440 | tf_op jit(solution)/shard_map/ppermute | solution.py:524
  27.1 1.9 %collective-permute-start.8 = (bf16[512,256]{1,0:T(8,128)(2,1)S(1)}, bf16[512,256]{1,0:T(8,128)(2,1)S(1)}, u32[]{:S(2)}, u32[]{:S(2)}) collective-permute-start(bf16[512,256]{1,0:T(8,128)(2,1)S(1)} %collective-permute-done.4.refs_3_), channel_id=1, source_target_pairs={{0,4},{4,0},{8,12},{12,8},{1,5},{5,1},{9,13},{13,9},{2,6},{6,2},{1... | collective-permute-start | bytes 786440 | tf_op jit(solution)/shard_map/ppermute | solution.py:524
  32.8 3.6 %collective-permute-start.9 = (bf16[3,88,256]{2,1,0:T(8,128)(2,1)}, bf16[3,88,256]{2,1,0:T(8,128)(2,1)S(1)}, u32[]{:S(2)}, u32[]{:S(2)}) collective-permute-start(bf16[3,88,256]{2,1,0:T(8,128)(2,1)} %get-tuple-element.65), channel_id=1, source_target_pairs={{0,4},{4,0},{8,12},{12,8},{1,5},{5,1},{9,13},{13,9},{2,6},{6,2},{1... | collective-permute-start | bytes 405512 | tf_op jit(solution)/shard_map/ppermute | solution.py:524
  33.0 6.3 %collective-permute-start.10 = (bf16[3,88,256]{2,1,0:T(8,128)(2,1)S(1)}, bf16[3,88,256]{2,1,0:T(8,128)(2,1)S(1)}, u32[]{:S(2)}, u32[]{:S(2)}) collective-permute-start(bf16[3,88,256]{2,1,0:T(8,128)(2,1)S(1)} %get-tuple-element.66), channel_id=1, source_target_pairs={{4,8},{8,4},{5,9},{9,5},{6,10},{10,6},{7,11},{11,7},{20,24},{24,20... | collective-permute-start | bytes 405512 | tf_op jit(solution)/shard_map/ppermute | solution.py:529
  46.0 8.1 %collective-permute-start.11 = (bf16[3,80,256]{2,1,0:T(8,128)(2,1)S(1)}, bf16[3,80,256]{2,1,0:T(8,128)(2,1)S(1)}, u32[]{:S(2)}, u32[]{:S(2)}) collective-permute-start(bf16[3,80,256]{2,1,0:T(8,128)(2,1)S(1)} %get-tuple-element.69), channel_id=1, source_target_pairs={{0,4},{4,0},{8,12},{12,8},{1,5},{5,1},{9,13},{13,9},{2,6},{6,2},{1... | collective-permute-start | bytes 368648 | tf_op jit(solution)/shard_map/ppermute | solution.py:524
  46.1 8.0 %collective-permute-start.12 = (bf16[3,80,256]{2,1,0:T(8,128)(2,1)S(1)}, bf16[3,80,256]{2,1,0:T(8,128)(2,1)S(1)}, u32[]{:S(2)}, u32[]{:S(2)}) collective-permute-start(bf16[3,80,256]{2,1,0:T(8,128)(2,1)S(1)} %get-tuple-element.70), channel_id=1, source_target_pairs={{4,8},{8,4},{5,9},{9,5},{6,10},{10,6},{7,11},{11,7},{20,24},{24,20... | collective-permute-start | bytes 368648 | tf_op jit(solution)/shard_map/ppermute | solution.py:529
  59.6 5.0 %collective-permute-start.19 = (bf16[3,88,256]{2,1,0:T(8,128)(2,1)S(1)}, bf16[3,88,256]{2,1,0:T(8,128)(2,1)S(1)}, u32[]{:S(2)}, u32[]{:S(2)}) collective-permute-start(bf16[3,88,256]{2,1,0:T(8,128)(2,1)S(1)} %get-tuple-element.89), channel_id=1, source_target_pairs={{0,4},{4,0},{8,12},{12,8},{1,5},{5,1},{9,13},{13,9},{2,6},{6,2},{1... | collective-permute-start | bytes 405512 | tf_op jit(solution)/shard_map/ppermute | solution.py:524
  59.6 6.3 %collective-permute-start.20 = (bf16[3,88,256]{2,1,0:T(8,128)(2,1)S(1)}, bf16[3,88,256]{2,1,0:T(8,128)(2,1)S(1)}, u32[]{:S(2)}, u32[]{:S(2)}) collective-permute-start(bf16[3,88,256]{2,1,0:T(8,128)(2,1)S(1)} %get-tuple-element.90), channel_id=1, source_target_pairs={{4,8},{8,4},{5,9},{9,5},{6,10},{10,6},{7,11},{11,7},{20,24},{24,20... | collective-permute-start | bytes 405512 | tf_op jit(solution)/shard_map/ppermute | solution.py:529
  62.1 5.8 %collective-permute-start.17 = (bf16[1024,256]{1,0:T(8,128)(2,1)S(1)}, bf16[1024,256]{1,0:T(8,128)(2,1)S(1)}, u32[]{:S(2)}, u32[]{:S(2)}) collective-permute-start(bf16[1024,256]{1,0:T(8,128)(2,1)S(1)} %get-tuple-element.83), channel_id=1, source_target_pairs={{0,4},{4,0},{8,12},{12,8},{1,5},{5,1},{9,13},{13,9},{2,6},{6,2},{1... | collective-permute-start | bytes 1572872 | tf_op jit(solution)/shard_map/ppermute | solution.py:524
  62.2 6.8 %collective-permute-start.13 = (bf16[1024,256]{1,0:T(8,128)(2,1)S(1)}, bf16[1024,256]{1,0:T(8,128)(2,1)S(1)}, u32[]{:S(2)}, u32[]{:S(2)}) collective-permute-start(bf16[1024,256]{1,0:T(8,128)(2,1)S(1)} %get-tuple-element.73), channel_id=1, source_target_pairs={{0,4},{4,0},{8,12},{12,8},{1,5},{5,1},{9,13},{13,9},{2,6},{6,2},{1... | collective-permute-start | bytes 1572872 | tf_op jit(solution)/shard_map/ppermute | solution.py:524
  67.6 15.2 %collective-permute-start.23 = (bf16[4,68,256]{2,1,0:T(8,128)(2,1)S(1)}, bf16[4,68,256]{2,1,0:T(8,128)(2,1)S(1)}, u32[]{:S(2)}, u32[]{:S(2)}) collective-permute-start(bf16[4,68,256]{2,1,0:T(8,128)(2,1)S(1)} %broadcast_select_fusion.2), channel_id=1, source_target_pairs={{0,16},{16,0},{1,17},{17,1},{2,18},{18,2},{3,19},{19,3},{4,20},{20... | collective-permute-start | bytes 417800 | tf_op jit(solution)/shard_map/ppermute | solution.py:521
  68.1 5.6 %collective-permute-start.18 = (bf16[512,256]{1,0:T(8,128)(2,1)S(1)}, bf16[512,256]{1,0:T(8,128)(2,1)S(1)}, u32[]{:S(2)}, u32[]{:S(2)}) collective-permute-start(bf16[512,256]{1,0:T(8,128)(2,1)S(1)} %broadcast_select_fusion), channel_id=1, source_target_pairs={{0,8},{1,9},{2,10},{3,11},{4,5},{5,4},{6,7},{7,6},{8,0},{9,1},{10,... | collective-permute-start | bytes 786440 | tf_op jit(solution)/shard_map/ppermute | solution.py:675
  69.1 7.1 %collective-permute-start.14 = (bf16[512,256]{1,0:T(8,128)(2,1)S(1)}, bf16[512,256]{1,0:T(8,128)(2,1)S(1)}, u32[]{:S(2)}, u32[]{:S(2)}) collective-permute-start(bf16[512,256]{1,0:T(8,128)(2,1)S(1)} %broadcast_select_fusion.1), channel_id=1, source_target_pairs={{0,8},{1,9},{2,10},{3,11},{4,5},{5,4},{6,7},{7,6},{8,0},{9,1},{10,... | collective-permute-start | bytes 786440 | tf_op jit(solution)/shard_map/ppermute | solution.py:675
  73.8 5.3 %collective-permute-start.21 = (bf16[256,256]{1,0:T(8,128)(2,1)S(1)}, bf16[256,256]{1,0:T(8,128)(2,1)S(1)}, u32[]{:S(2)}, u32[]{:S(2)}) collective-permute-start(bf16[256,256]{1,0:T(8,128)(2,1)S(1)} %broadcast_select_fusion.5), channel_id=1, source_target_pairs={{0,1},{1,0},{2,3},{3,2},{4,6},{5,7},{6,4},{7,5},{8,9},{9,8},{10,11... | collective-permute-start | bytes 393224 | tf_op jit(solution)/shard_map/ppermute | solution.py:675
  76.3 6.2 %collective-permute-start.15 = (bf16[256,256]{1,0:T(8,128)(2,1)S(1)}, bf16[256,256]{1,0:T(8,128)(2,1)S(1)}, u32[]{:S(2)}, u32[]{:S(2)}) collective-permute-start(bf16[256,256]{1,0:T(8,128)(2,1)S(1)} %broadcast_select_fusion.6), channel_id=1, source_target_pairs={{0,1},{1,0},{2,3},{3,2},{4,6},{5,7},{6,4},{7,5},{8,9},{9,8},{10,11... | collective-permute-start | bytes 393224 | tf_op jit(solution)/shard_map/ppermute | solution.py:675
  79.2 3.5 %collective-permute-start.22 = (bf16[128,256]{1,0:T(8,128)(2,1)S(1)}, bf16[128,256]{1,0:T(8,128)(2,1)S(1)}, u32[]{:S(2)}, u32[]{:S(2)}) collective-permute-start(bf16[128,256]{1,0:T(8,128)(2,1)S(1)} %broadcast_select_fusion.7), channel_id=1, source_target_pairs={{0,2},{1,3},{2,0},{3,1},{4,12},{5,13},{6,14},{7,15},{8,10},{9,11},... | collective-permute-start | bytes 196616 | tf_op jit(solution)/shard_map/ppermute | solution.py:675
  82.6 3.2 %collective-permute-start.16 = (bf16[128,256]{1,0:T(8,128)(2,1)S(1)}, bf16[128,256]{1,0:T(8,128)(2,1)S(1)}, u32[]{:S(2)}, u32[]{:S(2)}) collective-permute-start(bf16[128,256]{1,0:T(8,128)(2,1)S(1)} %broadcast_select_fusion.8), channel_id=1, source_target_pairs={{0,2},{1,3},{2,0},{3,1},{4,12},{5,13},{6,14},{7,15},{8,10},{9,11},... | collective-permute-start | bytes 196616 | tf_op jit(solution)/shard_map/ppermute | solution.py:675
  85.9 3.5 %collective-permute-start.24 = (bf16[192,256]{1,0:T(8,128)(2,1)S(1)}, bf16[192,256]{1,0:T(8,128)(2,1)S(1)}, u32[]{:S(2)}, u32[]{:S(2)}) collective-permute-start(bf16[192,256]{1,0:T(8,128)(2,1)S(1)} %pad_maximum_fusion.3), channel_id=1, source_target_pairs={{0,16},{16,0},{1,17},{17,1},{2,18},{18,2},{3,19},{19,3},{4,20},{20... | collective-permute-start | bytes 294920 | tf_op jit(solution)/shard_map/ppermute | solution.py:521
  89.5 3.5 %collective-permute-start.25 = (bf16[192,256]{1,0:T(8,128)(2,1)S(1)}, bf16[192,256]{1,0:T(8,128)(2,1)S(1)}, u32[]{:S(2)}, u32[]{:S(2)}) collective-permute-start(bf16[192,256]{1,0:T(8,128)(2,1)S(1)} %pad_maximum_fusion.4), channel_id=1, source_target_pairs={{0,2},{1,3},{2,0},{3,1},{4,12},{5,13},{6,14},{7,15},{8,10},{9,11},... | collective-permute-start | bytes 294920 | tf_op jit(solution)/shard_map/ppermute | solution.py:675
  93.1 9.2 %collective-permute-start.26 = (bf16[320,256]{1,0:T(8,128)(2,1)S(1)}, bf16[320,256]{1,0:T(8,128)(2,1)S(1)}, u32[]{:S(2)}, u32[]{:S(2)}) collective-permute-start(bf16[320,256]{1,0:T(8,128)(2,1)S(1)} %pad_maximum_fusion.2), channel_id=1, source_target_pairs={{0,1},{1,0},{2,3},{3,2},{4,6},{5,7},{6,4},{7,5},{8,9},{9,8},{10,11... | collective-permute-start | bytes 491528 | tf_op jit(solution)/shard_map/ppermute | solution.py:675
  102.5 7.4 %collective-permute-start.27 = (bf16[576,256]{1,0:T(8,128)(2,1)S(1)}, bf16[576,256]{1,0:T(8,128)(2,1)S(1)}, u32[]{:S(2)}, u32[]{:S(2)}) collective-permute-start(bf16[576,256]{1,0:T(8,128)(2,1)S(1)} %pad_maximum_fusion.1), channel_id=1, source_target_pairs={{0,8},{1,9},{2,10},{3,11},{4,5},{5,4},{6,7},{7,6},{8,0},{9,1},{10,... | collective-permute-start | bytes 884744 | tf_op jit(solution)/shard_map/ppermute | solution.py:675
  110.1 12.5 %copy-start.1 = (bf16[2,4,68,256]{3,1,2,0:T(4,128)(2,1)S(1)}, bf16[2,4,68,256]{3,1,2,0:T(4,128)(2,1)}, u32[]{:S(2)}) copy-start(bf16[2,4,68,256]{3,1,2,0:T(4,128)(2,1)} %param.8) | copy-start | bytes 835588
  110.2 8.6 %collective-permute-start.28 = (bf16[1088,256]{1,0:T(8,128)(2,1)S(1)}, bf16[1088,256]{1,0:T(8,128)(2,1)S(1)}, u32[]{:S(2)}, u32[]{:S(2)}) collective-permute-start(bf16[1088,256]{1,0:T(8,128)(2,1)S(1)} %pad_maximum_fusion), channel_id=1, source_target_pairs={{0,4},{4,0},{8,12},{12,8},{1,5},{5,1},{9,13},{13,9},{2,6},{6,2},{1... | collective-permute-start | bytes 1671176 | tf_op jit(solution)/shard_map/ppermute | solution.py:524
  (5 other events, 20.2 us)

commit v3 on v2

--- a/solution.py
+++ b/solution.py
@@ -367,8 +367,7 @@
     pad[:, :, W_X - 16 : W_X, :] = jnp.zeros((2, ROWS_DEV + 2 * REACH, 16, HALF), f32)
     load_padded(pad, flags[0], du1, du1_a, du1_b, shift)
     load_taps(taps, small1)
-    for copy in copies:
-        copy.wait()
+    copies[0].wait()
     for group in groups(W_0, 4):
         starts = [tile * 8 for tile in group]
         for half in range(2):
@@ -381,6 +380,8 @@
     for row in range(ROWS_DEV):
         at = row * W_0 + SIDE_0
         e_own[row] = upstream[at : at + W_OWN, :]
+    for copy in copies[1:]:
+        copy.wait()
     scale_cells(N_0, small0, normed, z)
     backward_cells(
         W_0, flags[0], small0, own, own_row, upstream, w_up, w_down, normed, inverse, z, active, slope, branch, hidden, dm, dh, du, keep, send, sums
@@ -441,47 +442,59 @@
     out[...] = total[...].astype(bf16)
 
 
-def finish(flags, piece, small, got, up, down, taps, channels, bias, up_vmem, down_vmem, sems):
-    factor = 1.0 / math.sqrt(BATCH * ROWS_DEV * COLS_DEV)
-
-    def copies(quarter):
-        cols = slice(quarter * WIDE, (quarter + 1) * WIDE)
-        return (
-            pltpu.make_async_copy(up_vmem.at[:, cols], up.at[0, :, cols], sems.at[0, quarter]),
-            pltpu.make_async_copy(down_vmem.at[cols, :], down.at[0, cols, :], sems.at[1, quarter]),
-        )
-
-    def write(up_rows, down_rows):
+factor = 1.0 / math.sqrt(BATCH * ROWS_DEV * COLS_DEV)
+
+
+def write_weights(is_up, rows, up, down, up_vmem, down_vmem, sems, beside=None):
+    def send(copies, fill):
         for quarter in range(QUARTERS):
-            cols = slice(quarter * WIDE, (quarter + 1) * WIDE)
-            up_vmem[:, cols] = up_rows[cols, :].astype(f32) * factor
-            down_vmem[cols, :] = down_rows[cols, :].astype(f32) * factor
-            for copy in copies(quarter):
-                copy.start()
-
-    @pl.when(flags[0] == 0)
+            fill(quarter, rows[quarter * WIDE : (quarter + 1) * WIDE, :].astype(f32) * factor)
+            copies[quarter].start()
+        if beside:
+            beside()
+        for copy in copies:
+            copy.wait()
+
+    def cols(quarter):
+        return slice(quarter * WIDE, (quarter + 1) * WIDE)
+
+    @pl.when(is_up)
     def _():
-        write(piece, got)
-
-    @pl.when(flags[0] == 1)
+        def fill(quarter, value):
+            up_vmem[:, cols(quarter)] = value
+
+        send([pltpu.make_async_copy(up_vmem.at[:, cols(q)], up.at[0, :, cols(q)], sems.at[0, q]) for q in range(QUARTERS)], fill)
+
+    @pl.when(jnp.logical_not(is_up))
     def _():
-        write(got, piece)
-
-    sums = (small[...].astype(f32) + got[HID:, :].astype(f32)) * factor
-    taps[0] = sums[:TAPS]
-    channels[0] = sums[TAPS : TAPS + 5]
-    for quarter in range(QUARTERS):
-        bias[:, quarter * WIDE : (quarter + 1) * WIDE] = sums[TAPS + 5 + quarter : TAPS + 6 + quarter]
-    for quarter in range(QUARTERS):
-        for copy in copies(quarter):
-            copy.wait()
+        def fill(quarter, value):
+            down_vmem[cols(quarter), :] = value
+
+        send([pltpu.make_async_copy(down_vmem.at[cols(q), :], down.at[0, cols(q), :], sems.at[1, q]) for q in range(QUARTERS)], fill)
+
+
+def finish_own(flags, piece, up, down, up_vmem, down_vmem, sems):
+    write_weights(flags[0] == 0, piece, up, down, up_vmem, down_vmem, sems)
+
+
+def finish_got(flags, small, got, up_in, down_in, up, down, taps, channels, bias, up_vmem, down_vmem, sems):
+    def rest():
+        sums = (small[...].astype(f32) + got[HID:, :].astype(f32)) * factor
+        for tap in range(TAPS):
+            taps[tap] = sums[tap : tap + 1]
+        for index in range(5):
+            channels[index] = sums[TAPS + index : TAPS + index + 1]
+        for quarter in range(QUARTERS):
+            bias[:, quarter * WIDE : (quarter + 1) * WIDE] = sums[TAPS + 5 + quarter : TAPS + 6 + quarter]
+
+    write_weights(flags[0] == 1, got, up, down, up_vmem, down_vmem, sems, rest)
 
 
 def in_vmem():
     return pl.BlockSpec(memory_space=pltpu.VMEM)
 
 
-def call(body, name, inputs, outputs, scratch, flops, hbm_in=0, hbm_out=0, sems=()):
+def call(body, name, inputs, outputs, scratch, flops, hbm_in=0, hbm_out=0, sems=(), aliases=None):
     in_hbm = pl.BlockSpec(memory_space=pltpu.HBM)
     return pl.pallas_call(
         body,
@@ -489,6 +502,7 @@
         out_shape=[jax.ShapeDtypeStruct(shape, dtype) for shape, dtype in outputs],
         in_specs=[pl.BlockSpec(memory_space=pltpu.SMEM)] + [in_vmem()] * (len(inputs) - 1 - hbm_in) + [in_hbm] * hbm_in,
         out_specs=[in_hbm] * hbm_out + [in_vmem()] * (len(outputs) - hbm_out),
+        input_output_aliases=aliases or {},
         scratch_shapes=[pltpu.VMEM(shape, dtype) for shape, dtype in scratch] + [pltpu.SemaphoreType.DMA(shape) for shape in sems],
         compiler_params=pltpu.CompilerParams(vmem_limit_bytes=28 << 20),
         cost_estimate=pl.CostEstimate(flops=10 * flops, bytes_accessed=4 << 20, transcendentals=0),
@@ -526,7 +540,9 @@
     def lat_halo(send_a, send_b):
         pairs = [(i, i + 1) for i in range(1, n_lat - 1, 2)]
         pairs += [(j, i) for i, j in pairs]
-        return over_core(send_a), lax.ppermute(send_b, "lat", pairs)
+        got_b = lax.ppermute(send_b, "lat", pairs)
+        beside = jnp.where(odd == 1, lat < n_lat - 1, lat > 0)
+        return over_core(send_a), jnp.where(beside, got_b, jnp.zeros_like(got_b))
 
     def by_core(even, other):
         return jnp.where(odd == 0, even, other)
@@ -540,8 +556,11 @@
         return jnp.concatenate([x_part, cot_part, sea_row], axis=1)
 
     ring = [(i, (i + 1) % n_lon) for i in range(n_lon)]
-    left = lax.ppermute(packed(x[:, -SIDE_X:], cot[:, -SIDE_1:], sea[:, -SIDE_0:]), "lon", ring)
-    right = lax.ppermute(packed(x[:, :SIDE_X], cot[:, :SIDE_1], sea[:, :SIDE_0]), "lon", [(j, i) for i, j in ring])
+    to_right = packed(x[:, -SIDE_X:], cot[:, -SIDE_1:], sea[:, -SIDE_0:])
+    to_left = packed(x[:, :SIDE_X], cot[:, :SIDE_1], sea[:, :SIDE_0])
+    to_right, to_left, dw_kernel = lax.optimization_barrier((to_right, to_left, dw_kernel))
+    left = lax.ppermute(to_right, "lon", ring)
+    right = lax.ppermute(to_left, "lon", [(j, i) for i, j in ring])
     small_own = jnp.concatenate(
         [dw_kernel[0], channel_params[0], up_bias[0].reshape(QUARTERS, WIDE), jnp.zeros((SMALL - TAPS - 9, WIDE), bf16)], axis=0
     )
@@ -550,7 +569,7 @@
     small_got = over_section(small_own)
     send_up = by_core(up[:cut], up[cut:])
     send_down = by_core(down[: HID // 2], down[HID // 2 :])
-    send_up, send_down, left, right, small_got = lax.optimization_barrier((send_up, send_down, left, right, small_got))
+    send_up, send_down, small_got = lax.optimization_barrier((send_up, send_down, small_got))
     got_up, got_down = over_section(send_up), over_section(send_down)
     small_0 = jnp.where(section == 0, small_own, small_got).astype(f32)
     small_1 = jnp.where(section == 0, small_got, small_own).astype(f32)
@@ -575,8 +594,8 @@
         flat = jnp.tile(inside, ROWS_DEV)
         return jnp.broadcast_to(flat[:, None], (flat.shape[0], HALF)), jnp.broadcast_to(flat[None, :], (16, flat.shape[0])).astype(bf16)
 
-    owN_0, row_0 = own_cells(W_0, SIDE_0)
-    owN_1, row_1 = own_cells(W_1, SIDE_1)
+    own_0, row_0 = own_cells(W_0, SIDE_0)
+    own_1, row_1 = own_cells(W_1, SIDE_1)
 
     deep = ROWS_DEV + 2 * REACH
     taps_scratch = ((2, TAPS, 8, HALF), f32)
@@ -614,7 +633,7 @@
     final, du1, du1_send_a, du1_send_b, keep_1, send_1, sums_1, pad_1 = call(
         second_block,
         "second_block",
-        (flags, y, y_a, y_b, small_1, mask_1, owN_1, row_1, kept) + weights,
+        (flags, y, y_a, y_b, small_1, mask_1, own_1, row_1, kept) + weights,
         [
             ((ROWS_DEV, COLS_DEV, WIDE), bf16), ((ROWS_DEV, W_1, WIDE), bf16), ((REACH, W_1, WIDE), bf16), ((REACH, W_1, WIDE), bf16),
             ((HID, WIDE), bf16), ((HID, WIDE), bf16), ((16, WIDE), f32), ((2, deep, W_0, HALF), f32),
@@ -644,7 +663,7 @@
     e_own, du0, du0_send_a, du0_send_b, keep_0, send_0, sums_0 = call(
         first_backward,
         "first_backward",
-        (flags, du1, du1_a, du1_b, small_1, small_0, mask_0, owN_0, row_0, active, slope, branch, w_up, w_down, kept),
+        (flags, du1, du1_a, du1_b, small_1, small_0, mask_0, own_0, row_0, active, slope, branch, w_up, w_down, kept),
         [
             ((ROWS_DEV, W_OWN, WIDE), f32), ((ROWS_DEV, W_0, WIDE), bf16), ((REACH, W_0, WIDE), bf16), ((REACH, W_0, WIDE), bf16),
             ((HID, WIDE), bf16), ((HID, WIDE), bf16), ((16, WIDE), f32),
@@ -659,7 +678,7 @@
         sems=((3,),),
     )
     bits = [("lat", 1 << i) for i in range(1, n_lat.bit_length() - 1)] + [("lon", 1 << i) for i in range(n_lon.bit_length() - 1)]
-    orders = (bits, bits[1:] + bits[:1])
+    orders = (bits, bits[1:2] + bits[:1] + bits[2:])
 
     def partner(place, step):
         row, col = place
@@ -693,9 +712,9 @@
             piece = plus(jnp.where(which, low, high), exchange(jnp.where(which, high, low), step))
         return piece
 
-    def reduce_step(piece, step):
-        half = piece.shape[0] // 2
-        low, high = piece[:half], piece[half:]
+    def reduce_step(pieces, step):
+        half = pieces.shape[1] // 2
+        low, high = pieces[:, :half], pieces[:, half:]
         which = side(step) == 0
         return plus(jnp.where(which, low, high), exchange(jnp.where(which, high, low), step))
 
@@ -706,55 +725,66 @@
 
     core_1 = over_core(send_1)
     core_0 = over_core(send_0)
-    piece_1 = plus(keep_1, core_1)
+    (taps_0,) = call(
+        tap_grads_0, "tap_grads_0", (flags, x_wide, x_a, x_b, du0, own_0, sums_0), [((SMALL, WIDE), bf16)],
+        [((2, deep, W_X, HALF), f32), ((ROWS_DEV, W_0, WIDE), f32), ((SMALL, WIDE), f32)], 2_000_000_000,
+    )
+    core_0, taps_0, pad_1 = lax.optimization_barrier((core_0, taps_0, pad_1))
+    pieces = jnp.stack([plus(keep_0, core_0), plus(keep_1, core_1)])
+    (taps_1,) = call(
+        tap_grads_1, "tap_grads_1", (flags, pad_1, du1, own_1, sums_1), [((SMALL, WIDE), bf16)],
+        [((ROWS_DEV, W_1, WIDE), f32), ((SMALL, WIDE), f32)], 2_000_000_000,
+    )
+    pieces = reduce_step(pieces, 0)
+    pieces, taps_1, du0_send_a, du0_send_b = lax.optimization_barrier((pieces, taps_1, du0_send_a, du0_send_b))
     du0_a, du0_b = lat_halo(du0_send_a, du0_send_b)
-    (taps_1,) = call(
-        tap_grads_1, "tap_grads_1", (flags, pad_1, du1, owN_1, sums_1), [((SMALL, WIDE), bf16)],
-        [((ROWS_DEV, W_1, WIDE), f32), ((SMALL, WIDE), f32)], 2_000_000_000,
-    )
-    (taps_0,) = call(
-        tap_grads_0, "tap_grads_0", (flags, x_wide, x_a, x_b, du0, owN_0, sums_0), [((SMALL, WIDE), bf16)],
-        [((2, deep, W_X, HALF), f32), ((ROWS_DEV, W_0, WIDE), f32), ((SMALL, WIDE), f32)], 2_000_000_000,
-    )
-    piece_0, taps_0, taps_1 = lax.optimization_barrier((plus(keep_0, core_0), taps_0, taps_1))
-    steps = len(bits)
-    for step in range(steps):
-        piece_1, piece_0 = reduce_step(piece_1, step), reduce_step(piece_0, step)
-        if step == 0:
-            (start,) = call(
-                input_grad, "input_grad", (flags, du0, du0_a, du0_b, small_0, e_own), [((ROWS_DEV, COLS_DEV, WIDE), bf16)],
-                [((2, deep, W_0, HALF), f32), taps_scratch, ((ROWS_DEV, W_OWN, WIDE), f32)], 2_000_000_000,
-            )
-            other_end = over_section(chosen(final, start))
-            piece_0, start = lax.optimization_barrier((piece_0, start))
+    pieces = reduce_step(pieces, 1)
+    pieces, du0_a, du0_b = lax.optimization_barrier((pieces, du0_a, du0_b))
+    (start,) = call(
+        input_grad, "input_grad", (flags, du0, du0_a, du0_b, small_0, e_own), [((ROWS_DEV, COLS_DEV, WIDE), bf16)],
+        [((2, deep, W_0, HALF), f32), taps_scratch, ((ROWS_DEV, W_OWN, WIDE), f32)], 2_000_000_000,
+    )
+    for step in range(2, len(bits)):
+        pieces = reduce_step(pieces, step)
+    pieces, start = lax.optimization_barrier((pieces, start))
+    other_end = over_section(chosen(final, start))
+    piece_0, piece_1 = pieces[0], pieces[1]
     cut = piece_0.shape[0]
-    piece_0, other_end = lax.optimization_barrier((piece_0, other_end))
     boundary = jnp.stack([chosen(start, other_end), chosen(other_end, final)])[None]
 
     def both(piece, small):
         return jnp.concatenate([piece, small], axis=0)
 
     got = over_section(both(chosen(piece_1, piece_0), chosen(taps_1, taps_0)))
-    got, boundary = lax.optimization_barrier((got, boundary))
     piece = plus(chosen(piece_0, piece_1), got[:cut])
     small = plus(chosen(taps_0, taps_1), got[cut:])
     for step in reversed(range(len(bits))):
+        if step == 0:
+            piece, boundary = lax.optimization_barrier((piece, boundary))
         got = exchange(both(piece, small), step)
         cut = piece.shape[0]
         small = plus(small, got[cut:])
         which = side(step) == 0
         piece = jnp.where(which, jnp.concatenate([piece, got[:cut]]), jnp.concatenate([got[:cut], piece]))
     got = over_core(both(piece, small))
+    weight_outs = [((1, WIDE, HID), f32), ((1, HID, WIDE), f32)]
+    weight_scratch = [((WIDE, HID), f32), ((HID, WIDE), f32)]
+    halves = call(
+        finish_own, "finish_own", (flags, piece), weight_outs, weight_scratch, 1_000_000, hbm_out=2, sems=((2, QUARTERS),)
+    )
     grad_up, grad_down, grad_taps, grad_channels, grad_bias = call(
-        finish,
-        "finish",
-        (flags, piece, small, got),
-        [((1, WIDE, HID), f32), ((1, HID, WIDE), f32), ((1, TAPS, WIDE), f32), ((1, 5, WIDE), f32), ((1, HID), f32)],
-        [((WIDE, HID), f32), ((HID, WIDE), f32)],
-        10_000_000,
+        finish_got,
+        "finish_got",
+        (flags, small, got, *halves),
+        weight_outs + [((TAPS, 1, WIDE), f32), ((5, 1, WIDE), f32), ((1, HID), f32)],
+        weight_scratch,
+        1_000_000,
+        hbm_in=2,
         hbm_out=2,
         sems=((2, QUARTERS),),
-    )
+        aliases={3: 0, 4: 1},
+    )
+    grad_taps, grad_channels = jnp.swapaxes(grad_taps, 0, 1), jnp.swapaxes(grad_channels, 0, 1)
     return (
         boundary,
         grad_taps,

time: 123 us -> 114 us (0.927)
  starting transfers between devices: 40.6 us -> 31 us
  waiting for transfers between devices: 41.3 us -> 43.5 us
    ppermute x9 -> x6, starting transfers between devices: 8.24 us -> 2.72 us  [exchange(): return lax.ppermute(value, ('lat', 'lon'), pairs)]
    ppermute x6, waiting for transfers between devices: 8.26 us -> 11.7 us  [the longest x4 8.88 us: lat_halo(): got_b = lax.ppermute(send_b, 'lat', pairs)]
    ppermute x9, starting transfers between devices: 8.53 us -> 5.45 us  [over_core(): return lax.ppermute(value, 'lat', swap_pairs(n_lat, 1))]
    ppermute x9 -> x6, waiting for transfers between devices: 28.9 us -> 27 us  [exchange(): return lax.ppermute(value, ('lat', 'lon'), pairs)]
    ppermute x5, waiting for transfers between devices: 2.19 us -> 3.71 us  [over_section(): return lax.ppermute(value, 'section', [(0, 1), (1, 0)])]
    unnamed x21 -> x15, local copies, waits for them, and re-layouts: 3.72 us -> 2.42 us
    pallas_call x9 -> x10, Pallas kernels: 29 us -> 28.8 us  [call(): pl.pallas_call(body, name=name, out_shape=[jax.ShapeDtypeStruct(shape, dt...]
  transfers between devices with their start and end apart: 29 -> 26, of which waited for: 16 -> 12; matrix products, arithmetic and copies ran while one was open for 4% -> 2% of each run, Pallas kernels for 10% -> 16%
where the time goes in v3:
time: 114 us; the launch traced here: 113 us
  waiting for transfers between devices  43.5 us (38%)
  starting transfers between devices  31 us (27%)
  Pallas kernels  28.8 us (25%)
  local copies, waits for them, and re-layouts  4.78 us (4%)
  other arithmetic  3.71 us (3%)
  between operations  1.46 us (1%)
    pallas_call x10, Pallas kernels, call(): pl.pallas_call(body, name=name, out_shape=[jax.ShapeDtypeStruct(shape, dt...  28.8 us
    ppermute x6, waiting for transfers between devices, exchange(): return lax.ppermute(value, ('lat', 'lon'), pairs)  27 us
    ppermute x4, starting transfers between devices, lat_halo(): got_b = lax.ppermute(send_b, 'lat', pairs)  15.3 us
    ppermute x4, waiting for transfers between devices, lat_halo(): got_b = lax.ppermute(send_b, 'lat', pairs)  8.88 us
    ppermute x9, starting transfers between devices, over_core(): return lax.ppermute(value, 'lat', swap_pairs(n_lat, 1))  5.45 us
    ppermute x5, starting transfers between devices, over_section(): return lax.ppermute(value, 'section', [(0, 1), (1, 0)])  4.21 us
    ppermute x5, waiting for transfers between devices, over_section(): return lax.ppermute(value, 'section', [(0, 1), (1, 0)])  3.71 us
    ppermute x1, starting transfers between devices, on_device(): right = lax.ppermute(to_left, 'lon', [(j, i) for i, j in ring])  3.32 us
  transfers between devices with their start and end apart: 26, of which 12 were waited for; matrix products, arithmetic and copies ran while one was open for 2% of the time, Pallas kernels for 16%

profile of v3, /device:TPU:1, one launch (start us, length us, event | category | flops | bytes accessed | tf_op | source)
XLA Modules:
  0.0 113.3 jit_solution(3635660955994135174)
XLA Ops:
  2.2 1.1 %constant_dynamic-slice_fusion = (bf16[1,4,68,256]{3,1,2,0:T(4,128)(2,1)S(1)}, bf16[1,4,68,256]{3,1,2,0:T(4,128)(2,1)S(1)}) fusion(bf16[2,4,68,256]{3,1,2,0:T(4,128)(2,1)} %param.9, s32[]{:T(128)S(6)} %select_n.261, bf16[2,4,68,256]{3,1,2,0:T(4,128)(2,1)} %param.8), kind=kLoop, calls=%fused_computation.60 | loop fusion | bytes 557060 | tf_op jit(solution)/shard_map/jit(dynamic_index_in_dim)/dynamic_slice | solution.py:551
  3.7 2.1 %collective-permute-start = (bf16[64,256]{1,0:T(8,128)(2,1)S(1)}, bf16[64,256]{1,0:T(8,128)(2,1)S(1)}, u32[]{:S(2)}, u32[]{:S(2)}) collective-permute-start(bf16[64,256]{1,0:T(8,128)(2,1)S(1)} %maximum_maximum_fusion.1), channel_id=1, source_target_pairs={{0,16},{16,0},{1,17},{17,1},{2,18},{18,2},{3,19},{19,3},{4,20},{20... | collective-permute-start | bytes 98312 | tf_op jit(solution)/shard_map/ppermute | solution.py:535
  5.8 3.3 %collective-permute-start.2 = (bf16[4,19,256]{2,1,0:T(8,128)(2,1)S(1)}, bf16[4,19,256]{2,1,0:T(8,128)(2,1)S(1)}, u32[]{:S(2)}, u32[]{:S(2)}) collective-permute-start(bf16[4,19,256]{2,1,0:T(8,128)(2,1)S(1)} %pad_maximum_fusion.7), channel_id=1, source_target_pairs={{1,0},{2,1},{3,2},{0,3},{5,4},{6,5},{7,6},{4,7},{9,8},{10,9},{11,1... | collective-permute-start | bytes 116744 | tf_op jit(solution)/shard_map/ppermute | solution.py:563
  9.7 1.2 %collective-permute-start.4 = (bf16[512,256]{1,0:T(8,128)(2,1)S(1)}, bf16[512,256]{1,0:T(8,128)(2,1)S(1)}, u32[]{:S(2)}, u32[]{:S(2)}) collective-permute-start(bf16[512,256]{1,0:T(8,128)(2,1)S(1)} %select_bitcast_fusion), channel_id=1, source_target_pairs={{0,16},{16,0},{1,17},{17,1},{2,18},{18,2},{3,19},{19,3},{4,20},{20... | collective-permute-start | bytes 786440 | tf_op jit(solution)/shard_map/ppermute | solution.py:535
  11.1 2.8 %collective-permute-done.1.left = bf16[4,19,256]{2,1,0:T(8,128)(2,1)S(1)} collective-permute-done((bf16[4,19,256]{2,1,0:T(8,128)(2,1)S(1)}, bf16[4,19,256]{2,1,0:T(8,128)(2,1)S(1)}, u32[]{:S(2)}, u32[]{:S(2)}) %collective-permute-start.1) | collective-permute-done | bytes 38944 | tf_op jit(solution)/shard_map/ppermute | solution.py:562
  14.0 5.4 %collective-permute-start.6 = (bf16[3,96,256]{2,1,0:T(8,128)(2,1)S(1)}, bf16[3,96,256]{2,1,0:T(8,128)(2,1)S(1)}, u32[]{:S(2)}, u32[]{:S(2)}) collective-permute-start(bf16[3,96,256]{2,1,0:T(8,128)(2,1)S(1)} %get-tuple-element.140), channel_id=1, source_target_pairs={{4,8},{8,4},{5,9},{9,5},{6,10},{10,6},{7,11},{11,7},{20,24},{24,20... | collective-permute-start | bytes 442376 | tf_op jit(solution)/shard_map/ppermute | solution.py:543
  19.6 2.9 %collective-permute-done.6 = bf16[3,96,256]{2,1,0:T(8,128)(2,1)S(1)} collective-permute-done((bf16[3,96,256]{2,1,0:T(8,128)(2,1)S(1)}, bf16[3,96,256]{2,1,0:T(8,128)(2,1)S(1)}, u32[]{:S(2)}, u32[]{:S(2)}) %collective-permute-start.6) | collective-permute-done | bytes 147488 | tf_op jit(solution)/shard_map/ppermute | solution.py:543
  22.7 4.5 %first_conv.1.kept = f32[40960,256]{1,0:T(8,128)} custom-call(s32[2]{0:T(128)S(1)} %pad_add_fusion.flags, bf16[4,96,256]{2,1,0:T(8,128)(2,1)S(1)} %maximum_maximum_fusion.x.v, bf16[3,96,256]{2,1,0:T(8,128)(2,1)S(1)} %collective-permute-done.5.x_a.v_a, bf16[3,96,256]{2,1,0:T(8,128)(2,1)S(1)} %broadcast_select_fusion.3.x_b.v_b, ...), custom_call_target="tpu_custom_call" | custom-call | flops 20000000000 | bytes 4194304 | tf_op jit(solution)/shard_map/first_conv/pallas_call | solution.py:499
  29.2 2.5 %first_forward.1 = (bf16[4,88,256]{2,1,0:T(8,128)(2,1)S(1)}, bf16[3,88,256]{2,1,0:T(8,128)(2,1)S(1)}, bf16[3,88,256]{2,1,0:T(8,128)(2,1)S(1)}) custom-call(s32[2]{0:T(128)S(1)} %pad_add_fusion.flags, f32[64,256]{1,0:T(8,128)S(1)} %get-tuple-element.80.small.small0, f32[352,128]{1,0:T(8,128)S(1)} %broadcast_in_dim.75.mask, f32[40960,256]{1,0:T(8,128)} %first_conv.1.kept, ...), custom_call_target="tpu_custom_call" | custom-call | flops 20000000000 | bytes 4194304 | tf_op jit(solution)/shard_map/first_forward/pallas_call | solution.py:499
  32.5 3.3 %collective-permute-start.10 = (bf16[3,88,256]{2,1,0:T(8,128)(2,1)S(1)}, bf16[3,88,256]{2,1,0:T(8,128)(2,1)S(1)}, u32[]{:S(2)}, u32[]{:S(2)}) collective-permute-start(bf16[3,88,256]{2,1,0:T(8,128)(2,1)S(1)} %get-tuple-element.75), channel_id=1, source_target_pairs={{4,8},{8,4},{5,9},{9,5},{6,10},{10,6},{7,11},{11,7},{20,24},{24,20... | collective-permute-start | bytes 405512 | tf_op jit(solution)/shard_map/ppermute | solution.py:543
  36.0 2.8 %collective-permute-done.10 = bf16[3,88,256]{2,1,0:T(8,128)(2,1)S(1)} collective-permute-done((bf16[3,88,256]{2,1,0:T(8,128)(2,1)S(1)}, bf16[3,88,256]{2,1,0:T(8,128)(2,1)S(1)}, u32[]{:S(2)}, u32[]{:S(2)}) %collective-permute-start.10) | collective-permute-done | bytes 135200 | tf_op jit(solution)/shard_map/ppermute | solution.py:543
  39.0 0.9 copy-done.3
  40.0 5.6 %second_block.1 = (bf16[4,68,256]{2,1,0:T(8,128)(2,1)S(1)}, bf16[4,80,256]{2,1,0:T(8,128)(2,1)S(1)}, bf16[3,80,256]{2,1,0:T(8,128)(2,1)S(1)}, bf16[3,80,256]{2,1...) custom-call(s32[2]{0:T(128)S(1)} %pad_add_fusion.flags, ...), custom_call_target="tpu_custom_call" | custom-call | flops 40000000000 | bytes 4194304 | tf_op jit(solution)/shard_map/second_block/pallas_call | solution.py:499
  45.6 3.4 %collective-permute-start.12 = (bf16[3,80,256]{2,1,0:T(8,128)(2,1)S(1)}, bf16[3,80,256]{2,1,0:T(8,128)(2,1)S(1)}, u32[]{:S(2)}, u32[]{:S(2)}) collective-permute-start(bf16[3,80,256]{2,1,0:T(8,128)(2,1)S(1)} %get-tuple-element.79), channel_id=1, source_target_pairs={{4,8},{8,4},{5,9},{9,5},{6,10},{10,6},{7,11},{11,7},{20,24},{24,20... | collective-permute-start | bytes 368648 | tf_op jit(solution)/shard_map/ppermute | solution.py:543
  49.0 2.8 %first_again.1 = (bf16[352,1024]{1,0:T(8,128)(2,1)S(1)}, f32[352,1024]{1,0:T(8,128)S(1)}, f32[352,256]{1,0:T(8,128)S(1)}, bf16[256,1024]{1,0:T(8,128)(2,1)S(1)}, bf16[1024,256]{1,0:T(8,128)(2,1)S(1)}) custom-call(s32[2]{0:T(128)S(1)} %pad_add_fusion.flags, f32[64,256]{1,0:T(8,128)S(1)} %get-tuple-element.80.small.small0, f32[40960,256]{1,0:T(8,128)} %first_conv.1.kept, ...), custom_call_target="tpu_custom_call" | custom-call | flops 20000000000 | bytes 4194304 | tf_op jit(solution)/shard_map/first_again/pallas_call | solution.py:499
  52.0 4.5 %first_backward.1 = (f32[4,72,256]{2,1,0:T(8,128)S(1)}, bf16[4,88,256]{2,1,0:T(8,128)(2,1)S(1)}, bf16[3,88,256]{2,1,0:T(8,128)(2,1)S(1)}, bf16[3,88,256]{2,1,0:T...) custom-call(s32[2]{0:T(128)S(1)} %pad_add_fusion.flags, ...), custom_call_target="tpu_custom_call" | custom-call | flops 30000001024 | bytes 4194304 | tf_op jit(solution)/shard_map/first_backward/pallas_call | solution.py:499
  57.0 1.8 %tap_grads_0.1 = bf16[64,256]{1,0:T(8,128)(2,1)S(1)} custom-call(s32[2]{0:T(128)S(1)} %pad_add_fusion.flags, bf16[4,96,256]{2,1,0:T(8,128)(2,1)S(1)} %maximum_maximum_fusion.x.v, bf16[3,96,256]{2,1,0:T(8,128)(2,1)S(1)} %collective-permute-done.5.x_a.v_a, bf16[3,96,256]{2,1,0:T(8,128)(2,1)S(1)} %broadcast_select_fusion.3.x_b.v_b, ...), custom_call_target="tpu_custom_call" | custom-call | flops 20000000000 | bytes 4194304 | tf_op jit(solution)/shard_map/tap_grads_0/pallas_call | solution.py:499
  59.4 1.7 %tap_grads_1.1 = bf16[64,256]{1,0:T(8,128)(2,1)S(1)} custom-call(s32[2]{0:T(128)S(1)} %pad_add_fusion.flags, f32[2,10,88,128]{3,2,1,0:T(8,128)S(1)} %get-tuple-element.97.pad, bf16[4,80,256]{2,1,0:T(8,128)(2,1)S(1)} %get-tuple-element.76.du1.du, f32[320,128]{1,0:T(8,128)S(1)} %broadcast_in_dim.82.own, f32[16,256]{1,0:T(8,128)S(1)} %get-tuple-element.98.sums), custom_call_target="tpu_custom_call" | custom-call | flops 20000000000 | bytes 4194304 | tf_op jit(solution)/shard_map/tap_grads_1/pallas_call | solution.py:499
  61.1 6.6 %collective-permute-done.15 = bf16[2,512,256]{2,1,0:T(8,128)(2,1)S(1)} collective-permute-done((bf16[2,512,256]{2,1,0:T(8,128)(2,1)S(1)}, bf16[2,512,256]{2,1,0:T(8,128)(2,1)S(1)}, u32[]{:S(2)}, u32[]{:S(2)}) %collective-permute-start.15) | collective-permute-done | bytes 524320 | tf_op jit(solution)/shard_map/ppermute | solution.py:694
  68.0 1.2 %collective-permute-start.16 = (bf16[2,256,256]{2,1,0:T(8,128)(2,1)S(1)}, bf16[2,256,256]{2,1,0:T(8,128)(2,1)S(1)}, u32[]{:S(2)}, u32[]{:S(2)}) collective-permute-start(bf16[2,256,256]{2,1,0:T(8,128)(2,1)S(1)} %broadcast_select_fusion.1), channel_id=1, source_target_pairs={{0,1},{1,0},{2,3},{3,2},{4,12},{5,13},{6,14},{7,15},{8,9},{9,8},{1... | collective-permute-start | bytes 786440 | tf_op jit(solution)/shard_map/ppermute | solution.py:694
  69.2 3.2 %collective-permute-start.18 = (bf16[3,88,256]{2,1,0:T(8,128)(2,1)S(1)}, bf16[3,88,256]{2,1,0:T(8,128)(2,1)S(1)}, u32[]{:S(2)}, u32[]{:S(2)}) collective-permute-start(bf16[3,88,256]{2,1,0:T(8,128)(2,1)S(1)} %get-tuple-element.103), channel_id=1, source_target_pairs={{4,8},{8,4},{5,9},{9,5},{6,10},{10,6},{7,11},{11,7},{20,24},{24,20... | collective-permute-start | bytes 405512 | tf_op jit(solution)/shard_map/ppermute | solution.py:543
  72.4 3.1 %collective-permute-done.18 = bf16[3,88,256]{2,1,0:T(8,128)(2,1)S(1)} collective-permute-done((bf16[3,88,256]{2,1,0:T(8,128)(2,1)S(1)}, bf16[3,88,256]{2,1,0:T(8,128)(2,1)S(1)}, u32[]{:S(2)}, u32[]{:S(2)}) %collective-permute-start.18) | collective-permute-done | bytes 135200 | tf_op jit(solution)/shard_map/ppermute | solution.py:543
  76.3 1.6 %input_grad.1 = bf16[4,68,256]{2,1,0:T(8,128)(2,1)S(1)} custom-call(s32[2]{0:T(128)S(1)} %pad_add_fusion.flags, bf16[4,88,256]{2,1,0:T(8,128)(2,1)S(1)} %get-tuple-element.91.du, bf16[3,88,256]{2,1,0:T(8,128)(2,1)S(1)} %collective-permute-done.17.du_a, bf16[3,88,256]{2,1,0:T(8,128)(2,1)S(1)} %broadcast_select_fusion.6.du_b, ...), custom_call_target="tpu_custom_call" | custom-call | flops 20000000000 | bytes 4194304 | tf_op jit(solution)/shard_map/input_grad/pallas_call | solution.py:499
  77.8 6.8 %collective-permute-done.19 = bf16[2,128,256]{2,1,0:T(8,128)(2,1)S(1)} collective-permute-done((bf16[2,128,256]{2,1,0:T(8,128)(2,1)S(1)}, bf16[2,128,256]{2,1,0:T(8,128)(2,1)S(1)}, u32[]{:S(2)}, u32[]{:S(2)}) %collective-permute-start.19) | collective-permute-done | bytes 131104 | tf_op jit(solution)/shard_map/ppermute | solution.py:694
  85.0 3.7 %collective-permute-done.20 = bf16[192,256]{1,0:T(8,128)(2,1)S(1)} collective-permute-done((bf16[192,256]{1,0:T(8,128)(2,1)S(1)}, bf16[192,256]{1,0:T(8,128)(2,1)S(1)}, u32[]{:S(2)}, u32[]{:S(2)}) %collective-permute-start.20) | collective-permute-done | bytes 98336 | tf_op jit(solution)/shard_map/ppermute | solution.py:535
  89.2 4.6 %collective-permute-done.21 = bf16[192,256]{1,0:T(8,128)(2,1)S(1)} collective-permute-done((bf16[192,256]{1,0:T(8,128)(2,1)S(1)}, bf16[192,256]{1,0:T(8,128)(2,1)S(1)}, u32[]{:S(2)}, u32[]{:S(2)}) %collective-permute-start.21) | collective-permute-done | bytes 98336 | tf_op jit(solution)/shard_map/ppermute | solution.py:694
  94.1 4.1 %collective-permute-done.22 = bf16[320,256]{1,0:T(8,128)(2,1)S(1)} collective-permute-done((bf16[320,256]{1,0:T(8,128)(2,1)S(1)}, bf16[320,256]{1,0:T(8,128)(2,1)S(1)}, u32[]{:S(2)}, u32[]{:S(2)}) %collective-permute-start.22) | collective-permute-done | bytes 163872 | tf_op jit(solution)/shard_map/ppermute | solution.py:694
  99.1 4.9 %collective-permute-done.24 = bf16[576,256]{1,0:T(8,128)(2,1)S(1)} collective-permute-done((bf16[576,256]{1,0:T(8,128)(2,1)S(1)}, bf16[576,256]{1,0:T(8,128)(2,1)S(1)}, u32[]{:S(2)}, u32[]{:S(2)}) %collective-permute-start.24) | collective-permute-done | bytes 294944 | tf_op jit(solution)/shard_map/ppermute | solution.py:694
  104.3 4.2 %collective-permute-start.25 = (bf16[1088,256]{1,0:T(8,128)(2,1)S(1)}, bf16[1088,256]{1,0:T(8,128)(2,1)S(1)}, u32[]{:S(2)}, u32[]{:S(2)}) collective-permute-start(bf16[1088,256]{1,0:T(8,128)(2,1)S(1)} %pad_maximum_fusion), channel_id=1, source_target_pairs={{0,4},{4,0},{8,12},{12,8},{1,5},{5,1},{9,13},{13,9},{2,6},{6,2},{1... | collective-permute-start | bytes 1671176 | tf_op jit(solution)/shard_map/ppermute | solution.py:538
  108.5 0.8 copy.28
  109.3 1.6 %finish_own.1 = (f32[1,256,1024]{2,1,0:T(8,128)}, f32[1,1024,256]{2,1,0:T(8,128)}) custom-call(s32[2]{0:T(128)S(1)} %pad_add_fusion.flags, bf16[1024,256]{1,0:T(8,128)(2,1)S(1)} %maximum_select_fusion.piece), custom_call_target="tpu_custom_call" | custom-call | flops 10000000 | bytes 4194304 | tf_op jit(solution)/shard_map/finish_own/pallas_call | solution.py:499
  110.9 2.2 %finish_got.1 = (f32[1,256,1024]{2,1,0:T(8,128)}, f32[1,1024,256]{2,1,0:T(8,128)}, f32[49,1,256]{2,1,0:T(1,128)}, f32[5,1,256]{2,1,0:T(1,128)}, f32[1,1024]{1,0:T(1,128)}) custom-call(s32[2]{0:T(128)S(1)} %pad_add_fusion.flags, bf16[64,256]{1,0:T(8,128)(2,1)S(1)} %add_convert_fusion.5.small, ...), custom_call_target="tpu_custom_call", output_to_operand_aliasing={{0}: (3, {}), {1}: (4, {})} | custom-call | flops 10000000 | bytes 4194304 | tf_op jit(solution)/shard_map/finish_got/pallas_call | solution.py:499
  (128 shorter events, 10.5 us)
Async XLA Ops:
  0.6 3.0 %copy-start.4 = (bf16[1,49,256]{2,1,0:T(8,128)(2,1)S(1)}, bf16[1,49,256]{2,1,0:T(8,128)(2,1)}, u32[]{:S(2)}) copy-start(bf16[1,49,256]{2,1,0:T(8,128)(2,1)} %param.11) | copy-start | bytes 75268
  0.6 3.0 %copy-start.5 = (bf16[1,5,256]{2,1,0:T(8,128)(2,1)S(1)}, bf16[1,5,256]{2,1,0:T(8,128)(2,1)}, u32[]{:S(2)}) copy-start(bf16[1,5,256]{2,1,0:T(8,128)(2,1)} %param.12) | copy-start | bytes 7684
  0.7 8.5 %copy-start = (bf16[1,256,1024]{2,1,0:T(8,128)(2,1)S(1)}, bf16[1,256,1024]{2,1,0:T(8,128)(2,1)}, u32[]{:S(2)}) copy-start(bf16[1,256,1024]{2,1,0:T(8,128)(2,1)} %param.13) | copy-start | bytes 1572868
  2.2 6.9 %copy-start.1 = (bf16[1,1024,256]{2,1,0:T(8,128)(2,1)S(1)}, bf16[1,1024,256]{2,1,0:T(8,128)(2,1)}, u32[]{:S(2)}) copy-start(bf16[1,1024,256]{2,1,0:T(8,128)(2,1)} %param.15) | copy-start | bytes 1572868
  3.7 5.8 %collective-permute-start = (bf16[64,256]{1,0:T(8,128)(2,1)S(1)}, bf16[64,256]{1,0:T(8,128)(2,1)S(1)}, u32[]{:S(2)}, u32[]{:S(2)}) collective-permute-start(bf16[64,256]{1,0:T(8,128)(2,1)S(1)} %maximum_maximum_fusion.1), channel_id=1, source_target_pairs={{0,16},{16,0},{1,17},{17,1},{2,18},{18,2},{3,19},{19,3},{4,20},{20... | collective-permute-start | bytes 98312 | tf_op jit(solution)/shard_map/ppermute | solution.py:535
  5.8 5.2 %collective-permute-start.2 = (bf16[4,19,256]{2,1,0:T(8,128)(2,1)S(1)}, bf16[4,19,256]{2,1,0:T(8,128)(2,1)S(1)}, u32[]{:S(2)}, u32[]{:S(2)}) collective-permute-start(bf16[4,19,256]{2,1,0:T(8,128)(2,1)S(1)} %pad_maximum_fusion.7), channel_id=1, source_target_pairs={{1,0},{2,1},{3,2},{0,3},{5,4},{6,5},{7,6},{4,7},{9,8},{10,9},{11,1... | collective-permute-start | bytes 116744 | tf_op jit(solution)/shard_map/ppermute | solution.py:563
  9.1 4.7 %collective-permute-start.1 = (bf16[4,19,256]{2,1,0:T(8,128)(2,1)S(1)}, bf16[4,19,256]{2,1,0:T(8,128)(2,1)S(1)}, u32[]{:S(2)}, u32[]{:S(2)}) collective-permute-start(bf16[4,19,256]{2,1,0:T(8,128)(2,1)S(1)} %pad_maximum_fusion.6), channel_id=1, source_target_pairs={{0,1},{1,2},{2,3},{3,0},{4,5},{5,6},{6,7},{7,4},{8,9},{9,10},{10,1... | collective-permute-start | bytes 116744 | tf_op jit(solution)/shard_map/ppermute | solution.py:562
  9.5 17.8 %collective-permute-start.3 = (bf16[128,1024]{1,0:T(8,128)(2,1)S(1)}, bf16[128,1024]{1,0:T(8,128)(2,1)S(1)}, u32[]{:S(2)}, u32[]{:S(2)}) collective-permute-start(bf16[128,1024]{1,0:T(8,128)(2,1)S(1)} %select_bitcast_fusion.1), channel_id=1, source_target_pairs={{0,16},{16,0},{1,17},{17,1},{2,18},{18,2},{3,19},{19,3},{4,20},{20... | collective-permute-start | bytes 786440 | tf_op jit(solution)/shard_map/ppermute | solution.py:535
  9.7 17.5 %collective-permute-start.4 = (bf16[512,256]{1,0:T(8,128)(2,1)S(1)}, bf16[512,256]{1,0:T(8,128)(2,1)S(1)}, u32[]{:S(2)}, u32[]{:S(2)}) collective-permute-start(bf16[512,256]{1,0:T(8,128)(2,1)S(1)} %select_bitcast_fusion), channel_id=1, source_target_pairs={{0,16},{16,0},{1,17},{17,1},{2,18},{18,2},{3,19},{19,3},{4,20},{20... | collective-permute-start | bytes 786440 | tf_op jit(solution)/shard_map/ppermute | solution.py:535
  14.0 8.5 %collective-permute-start.6 = (bf16[3,96,256]{2,1,0:T(8,128)(2,1)S(1)}, bf16[3,96,256]{2,1,0:T(8,128)(2,1)S(1)}, u32[]{:S(2)}, u32[]{:S(2)}) collective-permute-start(bf16[3,96,256]{2,1,0:T(8,128)(2,1)S(1)} %get-tuple-element.140), channel_id=1, source_target_pairs={{4,8},{8,4},{5,9},{9,5},{6,10},{10,6},{7,11},{11,7},{20,24},{24,20... | collective-permute-start | bytes 442376 | tf_op jit(solution)/shard_map/ppermute | solution.py:543
  19.6 3.0 %collective-permute-start.5 = (bf16[3,96,256]{2,1,0:T(8,128)(2,1)S(1)}, bf16[3,96,256]{2,1,0:T(8,128)(2,1)S(1)}, u32[]{:S(2)}, u32[]{:S(2)}) collective-permute-start(bf16[3,96,256]{2,1,0:T(8,128)(2,1)S(1)} %get-tuple-element.141), channel_id=1, source_target_pairs={{0,4},{4,0},{8,12},{12,8},{1,5},{5,1},{9,13},{13,9},{2,6},{6,2},{1... | collective-permute-start | bytes 442376 | tf_op jit(solution)/shard_map/ppermute | solution.py:538
  27.3 1.6 %collective-permute-start.7 = (bf16[128,1024]{1,0:T(8,128)(2,1)S(1)}, bf16[128,1024]{1,0:T(8,128)(2,1)S(1)}, u32[]{:S(2)}, u32[]{:S(2)}) collective-permute-start(bf16[128,1024]{1,0:T(8,128)(2,1)S(1)} %collective-permute-done.3.refs_2_), channel_id=1, source_target_pairs={{0,4},{4,0},{8,12},{12,8},{1,5},{5,1},{9,13},{13,9},{2,6},{6,2},{1... | collective-permute-start | bytes 786440 | tf_op jit(solution)/shard_map/ppermute | solution.py:538
  27.3 1.9 %collective-permute-start.8 = (bf16[512,256]{1,0:T(8,128)(2,1)S(1)}, bf16[512,256]{1,0:T(8,128)(2,1)S(1)}, u32[]{:S(2)}, u32[]{:S(2)}) collective-permute-start(bf16[512,256]{1,0:T(8,128)(2,1)S(1)} %collective-permute-done.4.refs_3_), channel_id=1, source_target_pairs={{0,4},{4,0},{8,12},{12,8},{1,5},{5,1},{9,13},{13,9},{2,6},{6,2},{1... | collective-permute-start | bytes 786440 | tf_op jit(solution)/shard_map/ppermute | solution.py:538
  31.8 0.7 copy-start.2
  32.5 6.3 %collective-permute-start.10 = (bf16[3,88,256]{2,1,0:T(8,128)(2,1)S(1)}, bf16[3,88,256]{2,1,0:T(8,128)(2,1)S(1)}, u32[]{:S(2)}, u32[]{:S(2)}) collective-permute-start(bf16[3,88,256]{2,1,0:T(8,128)(2,1)S(1)} %get-tuple-element.75), channel_id=1, source_target_pairs={{4,8},{8,4},{5,9},{9,5},{6,10},{10,6},{7,11},{11,7},{20,24},{24,20... | collective-permute-start | bytes 405512 | tf_op jit(solution)/shard_map/ppermute | solution.py:543
  36.0 2.8 %collective-permute-start.9 = (bf16[3,88,256]{2,1,0:T(8,128)(2,1)S(1)}, bf16[3,88,256]{2,1,0:T(8,128)(2,1)S(1)}, u32[]{:S(2)}, u32[]{:S(2)}) collective-permute-start(bf16[3,88,256]{2,1,0:T(8,128)(2,1)S(1)} %get-tuple-element.74), channel_id=1, source_target_pairs={{0,4},{4,0},{8,12},{12,8},{1,5},{5,1},{9,13},{13,9},{2,6},{6,2},{1... | collective-permute-start | bytes 405512 | tf_op jit(solution)/shard_map/ppermute | solution.py:538
  39.0 0.9 copy-start.3
  45.5 6.3 %collective-permute-start.11 = (bf16[3,80,256]{2,1,0:T(8,128)(2,1)S(1)}, bf16[3,80,256]{2,1,0:T(8,128)(2,1)S(1)}, u32[]{:S(2)}, u32[]{:S(2)}) collective-permute-start(bf16[3,80,256]{2,1,0:T(8,128)(2,1)S(1)} %get-tuple-element.78), channel_id=1, source_target_pairs={{0,4},{4,0},{8,12},{12,8},{1,5},{5,1},{9,13},{13,9},{2,6},{6,2},{1... | collective-permute-start | bytes 368648 | tf_op jit(solution)/shard_map/ppermute | solution.py:538
  45.6 6.2 %collective-permute-start.12 = (bf16[3,80,256]{2,1,0:T(8,128)(2,1)S(1)}, bf16[3,80,256]{2,1,0:T(8,128)(2,1)S(1)}, u32[]{:S(2)}, u32[]{:S(2)}) collective-permute-start(bf16[3,80,256]{2,1,0:T(8,128)(2,1)S(1)} %get-tuple-element.79), channel_id=1, source_target_pairs={{4,8},{8,4},{5,9},{9,5},{6,10},{10,6},{7,11},{11,7},{20,24},{24,20... | collective-permute-start | bytes 368648 | tf_op jit(solution)/shard_map/ppermute | solution.py:543
  51.8 7.2 %collective-permute-start.14 = (bf16[1024,256]{1,0:T(8,128)(2,1)S(1)}, bf16[1024,256]{1,0:T(8,128)(2,1)S(1)}, u32[]{:S(2)}, u32[]{:S(2)}) collective-permute-start(bf16[1024,256]{1,0:T(8,128)(2,1)S(1)} %get-tuple-element.96), channel_id=1, source_target_pairs={{0,4},{4,0},{8,12},{12,8},{1,5},{5,1},{9,13},{13,9},{2,6},{6,2},{1... | collective-permute-start | bytes 1572872 | tf_op jit(solution)/shard_map/ppermute | solution.py:538
  56.5 2.4 %collective-permute-start.13 = (bf16[1024,256]{1,0:T(8,128)(2,1)S(1)}, bf16[1024,256]{1,0:T(8,128)(2,1)S(1)}, u32[]{:S(2)}, u32[]{:S(2)}) collective-permute-start(bf16[1024,256]{1,0:T(8,128)(2,1)S(1)} %get-tuple-element.90), channel_id=1, source_target_pairs={{0,4},{4,0},{8,12},{12,8},{1,5},{5,1},{9,13},{13,9},{2,6},{6,2},{1... | collective-permute-start | bytes 1572872 | tf_op jit(solution)/shard_map/ppermute | solution.py:538
  59.4 8.4 %collective-permute-start.15 = (bf16[2,512,256]{2,1,0:T(8,128)(2,1)S(1)}, bf16[2,512,256]{2,1,0:T(8,128)(2,1)S(1)}, u32[]{:S(2)}, u32[]{:S(2)}) collective-permute-start(bf16[2,512,256]{2,1,0:T(8,128)(2,1)S(1)} %broadcast_select_fusion), channel_id=1, source_target_pairs={{0,8},{1,9},{2,10},{3,11},{4,5},{5,4},{6,7},{7,6},{8,0},{9,1},{10,... | collective-permute-start | bytes 1572872 | tf_op jit(solution)/shard_map/ppermute | solution.py:694
  68.0 7.5 %collective-permute-start.16 = (bf16[2,256,256]{2,1,0:T(8,128)(2,1)S(1)}, bf16[2,256,256]{2,1,0:T(8,128)(2,1)S(1)}, u32[]{:S(2)}, u32[]{:S(2)}) collective-permute-start(bf16[2,256,256]{2,1,0:T(8,128)(2,1)S(1)} %broadcast_select_fusion.1), channel_id=1, source_target_pairs={{0,1},{1,0},{2,3},{3,2},{4,12},{5,13},{6,14},{7,15},{8,9},{9,8},{1... | collective-permute-start | bytes 786440 | tf_op jit(solution)/shard_map/ppermute | solution.py:694
  69.2 6.5 %collective-permute-start.17 = (bf16[3,88,256]{2,1,0:T(8,128)(2,1)S(1)}, bf16[3,88,256]{2,1,0:T(8,128)(2,1)S(1)}, u32[]{:S(2)}, u32[]{:S(2)}) collective-permute-start(bf16[3,88,256]{2,1,0:T(8,128)(2,1)S(1)} %get-tuple-element.102), channel_id=1, source_target_pairs={{0,4},{4,0},{8,12},{12,8},{1,5},{5,1},{9,13},{13,9},{2,6},{6,2},{1... | collective-permute-start | bytes 405512 | tf_op jit(solution)/shard_map/ppermute | solution.py:538
  69.2 6.3 %collective-permute-start.18 = (bf16[3,88,256]{2,1,0:T(8,128)(2,1)S(1)}, bf16[3,88,256]{2,1,0:T(8,128)(2,1)S(1)}, u32[]{:S(2)}, u32[]{:S(2)}) collective-permute-start(bf16[3,88,256]{2,1,0:T(8,128)(2,1)S(1)} %get-tuple-element.103), channel_id=1, source_target_pairs={{4,8},{8,4},{5,9},{9,5},{6,10},{10,6},{7,11},{11,7},{20,24},{24,20... | collective-permute-start | bytes 405512 | tf_op jit(solution)/shard_map/ppermute | solution.py:543
  75.7 9.0 %collective-permute-start.19 = (bf16[2,128,256]{2,1,0:T(8,128)(2,1)S(1)}, bf16[2,128,256]{2,1,0:T(8,128)(2,1)S(1)}, u32[]{:S(2)}, u32[]{:S(2)}) collective-permute-start(bf16[2,128,256]{2,1,0:T(8,128)(2,1)S(1)} %broadcast_select_fusion.8), channel_id=1, source_target_pairs={{0,2},{1,3},{2,0},{3,1},{4,6},{5,7},{6,4},{7,5},{8,10},{9,11},{10,... | collective-permute-start | bytes 393224 | tf_op jit(solution)/shard_map/ppermute | solution.py:694
  84.7 4.0 %collective-permute-start.20 = (bf16[192,256]{1,0:T(8,128)(2,1)S(1)}, bf16[192,256]{1,0:T(8,128)(2,1)S(1)}, u32[]{:S(2)}, u32[]{:S(2)}) collective-permute-start(bf16[192,256]{1,0:T(8,128)(2,1)S(1)} %pad_maximum_fusion.4), channel_id=1, source_target_pairs={{0,16},{16,0},{1,17},{17,1},{2,18},{18,2},{3,19},{19,3},{4,20},{20... | collective-permute-start | bytes 294920 | tf_op jit(solution)/shard_map/ppermute | solution.py:535
  88.8 5.0 %collective-permute-start.21 = (bf16[192,256]{1,0:T(8,128)(2,1)S(1)}, bf16[192,256]{1,0:T(8,128)(2,1)S(1)}, u32[]{:S(2)}, u32[]{:S(2)}) collective-permute-start(bf16[192,256]{1,0:T(8,128)(2,1)S(1)} %pad_maximum_fusion.5), channel_id=1, source_target_pairs={{0,2},{1,3},{2,0},{3,1},{4,6},{5,7},{6,4},{7,5},{8,10},{9,11},{10,... | collective-permute-start | bytes 294920 | tf_op jit(solution)/shard_map/ppermute | solution.py:694
  88.9 5.1 %collective-permute-start.23 = (bf16[4,68,256]{2,1,0:T(8,128)(2,1)S(1)}, bf16[4,68,256]{2,1,0:T(8,128)(2,1)S(1)}, u32[]{:S(2)}, u32[]{:S(2)}) collective-permute-start(bf16[4,68,256]{2,1,0:T(8,128)(2,1)S(1)} %broadcast_select_fusion.2), channel_id=1, source_target_pairs={{0,16},{16,0},{1,17},{17,1},{2,18},{18,2},{3,19},{19,3},{4,20},{20... | collective-permute-start | bytes 417800 | tf_op jit(solution)/shard_map/ppermute | solution.py:535
  93.9 4.2 %collective-permute-start.22 = (bf16[320,256]{1,0:T(8,128)(2,1)S(1)}, bf16[320,256]{1,0:T(8,128)(2,1)S(1)}, u32[]{:S(2)}, u32[]{:S(2)}) collective-permute-start(bf16[320,256]{1,0:T(8,128)(2,1)S(1)} %pad_maximum_fusion.3), channel_id=1, source_target_pairs={{0,1},{1,0},{2,3},{3,2},{4,12},{5,13},{6,14},{7,15},{8,9},{9,8},{1... | collective-permute-start | bytes 491528 | tf_op jit(solution)/shard_map/ppermute | solution.py:694
  98.3 5.6 %collective-permute-start.24 = (bf16[576,256]{1,0:T(8,128)(2,1)S(1)}, bf16[576,256]{1,0:T(8,128)(2,1)S(1)}, u32[]{:S(2)}, u32[]{:S(2)}) collective-permute-start(bf16[576,256]{1,0:T(8,128)(2,1)S(1)} %pad_maximum_fusion.2), channel_id=1, source_target_pairs={{0,8},{1,9},{2,10},{3,11},{4,5},{5,4},{6,7},{7,6},{8,0},{9,1},{10,... | collective-permute-start | bytes 884744 | tf_op jit(solution)/shard_map/ppermute | solution.py:694
  104.3 6.6 %collective-permute-start.25 = (bf16[1088,256]{1,0:T(8,128)(2,1)S(1)}, bf16[1088,256]{1,0:T(8,128)(2,1)S(1)}, u32[]{:S(2)}, u32[]{:S(2)}) collective-permute-start(bf16[1088,256]{1,0:T(8,128)(2,1)S(1)} %pad_maximum_fusion), channel_id=1, source_target_pairs={{0,4},{4,0},{8,12},{12,8},{1,5},{5,1},{9,13},{13,9},{2,6},{6,2},{1... | collective-permute-start | bytes 1671176 | tf_op jit(solution)/shard_map/ppermute | solution.py:538

commit v4 on v3

--- a/solution.py
+++ b/solution.py
@@ -537,10 +537,12 @@
     def over_core(value):
         return lax.ppermute(value, "lat", swap_pairs(n_lat, 1))
 
-    def lat_halo(send_a, send_b):
+    def lat_halo(send_a, send_b, choose=False):
         pairs = [(i, i + 1) for i in range(1, n_lat - 1, 2)]
         pairs += [(j, i) for i, j in pairs]
         got_b = lax.ppermute(send_b, "lat", pairs)
+        if not choose:
+            return over_core(send_a), got_b
         beside = jnp.where(odd == 1, lat < n_lat - 1, lat > 0)
         return over_core(send_a), jnp.where(beside, got_b, jnp.zeros_like(got_b))
 
@@ -577,7 +579,7 @@
     before = SIDE_0 - SIDE_1
     sea_at = SIDE_X + SIDE_1
     x_wide = jnp.concatenate([left[:, :SIDE_X], x, right[:, :SIDE_X], jnp.zeros((ROWS_DEV, W_X - COLS_DEV - 2 * SIDE_X, channels), bf16)], axis=1)
-    x_a, x_b = lat_halo(by_core(x_wide[1:], x_wide[:REACH]), by_core(x_wide[:REACH], x_wide[1:]))
+    x_a, x_b = lat_halo(by_core(x_wide[1:], x_wide[:REACH]), by_core(x_wide[:REACH], x_wide[1:]), True)
     mask_wide = jnp.concatenate(
         [left[:, sea_at, :SIDE_0], sea, right[:, sea_at, :SIDE_0], jnp.zeros((ROWS_DEV, W_0 - COLS_DEV - 2 * SIDE_0), bf16)], axis=1
     )
@@ -648,6 +650,50 @@
         sems=((6,), (1,)),
     )
     du1_a, du1_b = lat_halo(du1_send_a, du1_send_b)
+    bits = [("lat", 1 << i) for i in range(1, n_lat.bit_length() - 1)] + [("lon", 1 << i) for i in range(n_lon.bit_length() - 1)]
+    orders = (bits, bits[1:2] + bits[:1] + bits[2:])
+
+    def partner(place, step):
+        row, col = place
+        axis, bit = orders[row % 2][step]
+        return (row ^ bit, col) if axis == "lat" else (row, col ^ bit)
+
+    def exchange(value, step):
+        pairs = []
+        for row in range(n_lat):
+            for col in range(n_lon):
+                other = partner((row, col), step)
+                pairs.append((row * n_lon + col, other[0] * n_lon + other[1]))
+        return lax.ppermute(value, ("lat", "lon"), pairs)
+
+    def side(step):
+        def of(order):
+            axis, bit = order[step]
+            return ((lat if axis == "lat" else lon) // bit) % 2
+
+        return jnp.where(odd == 0, of(orders[0]), of(orders[1]))
+
+    def plus(first, second):
+        return (first.astype(f32) + second.astype(f32)).astype(bf16)
+
+    def reduce_scatter(keep, send):
+        piece = plus(keep, over_core(send))
+        for step in range(len(bits)):
+            half = piece.shape[0] // 2
+            low, high = piece[:half], piece[half:]
+            which = side(step) == 0
+            piece = plus(jnp.where(which, low, high), exchange(jnp.where(which, high, low), step))
+        return piece
+
+    def reduce_send(piece, step):
+        half = piece.shape[-2] // 2
+        low, high = piece[..., :half, :], piece[..., half:, :]
+        which = side(step) == 0
+        return jnp.where(which, low, high), exchange(jnp.where(which, high, low), step)
+
+    def reduce_step(piece, step):
+        return plus(*reduce_send(piece, step))
+
     small_again, _ = lax.optimization_barrier((small_0, du1_send_a))
     active, slope, branch, w_up, w_down = call(
         first_again,
@@ -659,7 +705,8 @@
         hbm_in=7,
         sems=((6,), (1,)),
     )
-    send_1, du1_a, du1_b, active = lax.optimization_barrier((send_1, du1_a, du1_b, active))
+    send_1, du1_a = lax.optimization_barrier((send_1, du1_a))
+    held_1, got_1 = reduce_send(plus(keep_1, over_core(send_1)), 0)
     e_own, du0, du0_send_a, du0_send_b, keep_0, send_0, sums_0 = call(
         first_backward,
         "first_backward",
@@ -677,69 +724,28 @@
         hbm_in=1,
         sems=((3,),),
     )
-    bits = [("lat", 1 << i) for i in range(1, n_lat.bit_length() - 1)] + [("lon", 1 << i) for i in range(n_lon.bit_length() - 1)]
-    orders = (bits, bits[1:2] + bits[:1] + bits[2:])
-
-    def partner(place, step):
-        row, col = place
-        axis, bit = orders[row % 2][step]
-        return (row ^ bit, col) if axis == "lat" else (row, col ^ bit)
-
-    def exchange(value, step):
-        pairs = []
-        for row in range(n_lat):
-            for col in range(n_lon):
-                other = partner((row, col), step)
-                pairs.append((row * n_lon + col, other[0] * n_lon + other[1]))
-        return lax.ppermute(value, ("lat", "lon"), pairs)
-
-    def side(step):
-        def of(order):
-            axis, bit = order[step]
-            return ((lat if axis == "lat" else lon) // bit) % 2
-
-        return jnp.where(odd == 0, of(orders[0]), of(orders[1]))
-
-    def plus(first, second):
-        return (first.astype(f32) + second.astype(f32)).astype(bf16)
-
-    def reduce_scatter(keep, send):
-        piece = plus(keep, over_core(send))
-        for step in range(len(bits)):
-            half = piece.shape[0] // 2
-            low, high = piece[:half], piece[half:]
-            which = side(step) == 0
-            piece = plus(jnp.where(which, low, high), exchange(jnp.where(which, high, low), step))
-        return piece
-
-    def reduce_step(pieces, step):
-        half = pieces.shape[1] // 2
-        low, high = pieces[:, :half], pieces[:, half:]
-        which = side(step) == 0
-        return plus(jnp.where(which, low, high), exchange(jnp.where(which, high, low), step))
-
     to_first = section == 0
 
     def chosen(first, second):
         return jnp.where(to_first, first, second)
 
-    core_1 = over_core(send_1)
     core_0 = over_core(send_0)
     (taps_0,) = call(
         tap_grads_0, "tap_grads_0", (flags, x_wide, x_a, x_b, du0, own_0, sums_0), [((SMALL, WIDE), bf16)],
         [((2, deep, W_X, HALF), f32), ((ROWS_DEV, W_0, WIDE), f32), ((SMALL, WIDE), f32)], 2_000_000_000,
     )
     core_0, taps_0, pad_1 = lax.optimization_barrier((core_0, taps_0, pad_1))
-    pieces = jnp.stack([plus(keep_0, core_0), plus(keep_1, core_1)])
+    piece_0 = plus(keep_0, core_0)
     (taps_1,) = call(
         tap_grads_1, "tap_grads_1", (flags, pad_1, du1, own_1, sums_1), [((SMALL, WIDE), bf16)],
         [((ROWS_DEV, W_1, WIDE), f32), ((SMALL, WIDE), f32)], 2_000_000_000,
     )
-    pieces = reduce_step(pieces, 0)
-    pieces, taps_1, du0_send_a, du0_send_b = lax.optimization_barrier((pieces, taps_1, du0_send_a, du0_send_b))
+    held_0, got_0 = reduce_send(piece_0, 0)
+    taps_1, du0_send_a, du0_send_b = lax.optimization_barrier((taps_1, du0_send_a, du0_send_b))
     du0_a, du0_b = lat_halo(du0_send_a, du0_send_b)
+    got_0, got_1, du0_a, du0_b = lax.optimization_barrier((got_0, got_1, du0_a, du0_b))
+    pieces = jnp.stack([plus(held_0, got_0), plus(held_1, got_1)])
     pieces = reduce_step(pieces, 1)
-    pieces, du0_a, du0_b = lax.optimization_barrier((pieces, du0_a, du0_b))
     (start,) = call(
         input_grad, "input_grad", (flags, du0, du0_a, du0_b, small_0, e_own), [((ROWS_DEV, COLS_DEV, WIDE), bf16)],
         [((2, deep, W_0, HALF), f32), taps_scratch, ((ROWS_DEV, W_OWN, WIDE), f32)], 2_000_000_000,

time: 114 us -> 112 us (0.982)
  waiting for transfers between devices: 43.5 us -> 39.5 us
  starting transfers between devices: 31 us -> 33.6 us
    ppermute x1, waiting for transfers between devices: 2.8 us -> 0.01 us  [on_device(): left = lax.ppermute(to_right, 'lon', ring)]
    ppermute x9, starting transfers between devices: 5.45 us -> 7.47 us  [over_core(): return lax.ppermute(value, 'lat', swap_pairs(n_lat, 1))]
    ppermute x6 -> x7, starting transfers between devices: 2.72 us -> 4.03 us  [exchange(): return lax.ppermute(value, ('lat', 'lon'), pairs)]
    ppermute x1, starting transfers between devices: 0.01 us -> 1.3 us  [on_device(): left = lax.ppermute(to_right, 'lon', ring)]
    ppermute x1, starting transfers between devices: 3.32 us -> 2.03 us  [on_device(): right = lax.ppermute(to_left, 'lon', [(j, i) for i, j in ring])]
    ppermute x6 -> x7, waiting for transfers between devices: 27 us -> 25.9 us  [exchange(): return lax.ppermute(value, ('lat', 'lon'), pairs)]
  transfers between devices with their start and end apart: 26 -> 27, of which waited for: 12 -> 11; matrix products, arithmetic and copies ran while one was open for 2% -> 2% of each run, Pallas kernels for 16% -> 17%
where the time goes in v4:
time: 112 us
  waiting for transfers between devices  39.5 us (35%)
  starting transfers between devices  33.6 us (30%)
  Pallas kernels  28.7 us (26%)
  local copies, waits for them, and re-layouts  4.78 us (4%)
  other arithmetic  3.62 us (3%)
  between operations  1.51 us (1%)
    pallas_call x10, Pallas kernels, call(): pl.pallas_call(body, name=name, out_shape=[jax.ShapeDtypeStruct(shape, dt...  28.7 us
    ppermute x7, waiting for transfers between devices, exchange(): return lax.ppermute(value, ('lat', 'lon'), pairs)  25.9 us
    ppermute x4, starting transfers between devices, lat_halo(): got_b = lax.ppermute(send_b, 'lat', pairs)  14.5 us
    ppermute x4, waiting for transfers between devices, lat_halo(): got_b = lax.ppermute(send_b, 'lat', pairs)  9.24 us
    ppermute x9, starting transfers between devices, over_core(): return lax.ppermute(value, 'lat', swap_pairs(n_lat, 1))  7.47 us
    ppermute x5, starting transfers between devices, over_section(): return lax.ppermute(value, 'section', [(0, 1), (1, 0)])  4.22 us
    ppermute x7, starting transfers between devices, exchange(): return lax.ppermute(value, ('lat', 'lon'), pairs)  4.03 us
    ppermute x5, waiting for transfers between devices, over_section(): return lax.ppermute(value, 'section', [(0, 1), (1, 0)])  3.22 us
  transfers between devices with their start and end apart: 27, of which 11 were waited for; matrix products, arithmetic and copies ran while one was open for 2% of the time, Pallas kernels for 17%

profile of v4, /device:TPU:1, one launch (start us, length us, event | category | flops | bytes accessed | tf_op | source)
XLA Modules:
  0.0 111.8 jit_solution(3362463957671241843)
XLA Ops:
  2.2 1.1 %constant_dynamic-slice_fusion = (bf16[1,4,68,256]{3,1,2,0:T(4,128)(2,1)S(1)}, bf16[1,4,68,256]{3,1,2,0:T(4,128)(2,1)S(1)}) fusion(bf16[2,4,68,256]{3,1,2,0:T(4,128)(2,1)} %param.9, s32[]{:T(128)S(6)} %select_n.251, bf16[2,4,68,256]{3,1,2,0:T(4,128)(2,1)} %param.8), kind=kLoop, calls=%fused_computation.59 | loop fusion | bytes 557060 | tf_op jit(solution)/shard_map/jit(dynamic_index_in_dim)/dynamic_slice | solution.py:553
  3.7 2.1 %collective-permute-start = (bf16[64,256]{1,0:T(8,128)(2,1)S(1)}, bf16[64,256]{1,0:T(8,128)(2,1)S(1)}, u32[]{:S(2)}, u32[]{:S(2)}) collective-permute-start(bf16[64,256]{1,0:T(8,128)(2,1)S(1)} %maximum_maximum_fusion.1), channel_id=1, source_target_pairs={{0,16},{16,0},{1,17},{17,1},{2,18},{18,2},{3,19},{19,3},{4,20},{20... | collective-permute-start | bytes 98312 | tf_op jit(solution)/shard_map/ppermute | solution.py:535
  5.8 1.3 %collective-permute-start.1 = (bf16[4,19,256]{2,1,0:T(8,128)(2,1)S(1)}, bf16[4,19,256]{2,1,0:T(8,128)(2,1)S(1)}, u32[]{:S(2)}, u32[]{:S(2)}) collective-permute-start(bf16[4,19,256]{2,1,0:T(8,128)(2,1)S(1)} %pad_maximum_fusion.6), channel_id=1, source_target_pairs={{0,1},{1,2},{2,3},{3,0},{4,5},{5,6},{6,7},{7,4},{8,9},{9,10},{10,1... | collective-permute-start | bytes 116744 | tf_op jit(solution)/shard_map/ppermute | solution.py:564
  7.1 2.0 %collective-permute-start.2 = (bf16[4,19,256]{2,1,0:T(8,128)(2,1)S(1)}, bf16[4,19,256]{2,1,0:T(8,128)(2,1)S(1)}, u32[]{:S(2)}, u32[]{:S(2)}) collective-permute-start(bf16[4,19,256]{2,1,0:T(8,128)(2,1)S(1)} %pad_maximum_fusion.7), channel_id=1, source_target_pairs={{1,0},{2,1},{3,2},{0,3},{5,4},{6,5},{7,6},{4,7},{9,8},{10,9},{11,1... | collective-permute-start | bytes 116744 | tf_op jit(solution)/shard_map/ppermute | solution.py:565
  9.7 1.2 %collective-permute-start.4 = (bf16[512,256]{1,0:T(8,128)(2,1)S(1)}, bf16[512,256]{1,0:T(8,128)(2,1)S(1)}, u32[]{:S(2)}, u32[]{:S(2)}) collective-permute-start(bf16[512,256]{1,0:T(8,128)(2,1)S(1)} %select_bitcast_fusion), channel_id=1, source_target_pairs={{0,16},{16,0},{1,17},{17,1},{2,18},{18,2},{3,19},{19,3},{4,20},{20... | collective-permute-start | bytes 786440 | tf_op jit(solution)/shard_map/ppermute | solution.py:535
  11.2 5.1 %collective-permute-start.6 = (bf16[3,96,256]{2,1,0:T(8,128)(2,1)S(1)}, bf16[3,96,256]{2,1,0:T(8,128)(2,1)S(1)}, u32[]{:S(2)}, u32[]{:S(2)}) collective-permute-start(bf16[3,96,256]{2,1,0:T(8,128)(2,1)S(1)} %get-tuple-element.136), channel_id=1, source_target_pairs={{4,8},{8,4},{5,9},{9,5},{6,10},{10,6},{7,11},{11,7},{20,24},{24,20... | collective-permute-start | bytes 442376 | tf_op jit(solution)/shard_map/ppermute | solution.py:543
  16.5 2.9 %collective-permute-done.6 = bf16[3,96,256]{2,1,0:T(8,128)(2,1)S(1)} collective-permute-done((bf16[3,96,256]{2,1,0:T(8,128)(2,1)S(1)}, bf16[3,96,256]{2,1,0:T(8,128)(2,1)S(1)}, u32[]{:S(2)}, u32[]{:S(2)}) %collective-permute-start.6) | collective-permute-done | bytes 147488 | tf_op jit(solution)/shard_map/ppermute | solution.py:543
  19.6 4.5 %first_conv.1.kept = f32[40960,256]{1,0:T(8,128)} custom-call(s32[2]{0:T(128)S(1)} %pad_add_fusion.flags, bf16[4,96,256]{2,1,0:T(8,128)(2,1)S(1)} %maximum_maximum_fusion.x.v, bf16[3,96,256]{2,1,0:T(8,128)(2,1)S(1)} %collective-permute-done.5.x_a.v_a, bf16[3,96,256]{2,1,0:T(8,128)(2,1)S(1)} %broadcast_select_fusion.4.x_b.v_b, ...), custom_call_target="tpu_custom_call" | custom-call | flops 20000000000 | bytes 4194304 | tf_op jit(solution)/shard_map/first_conv/pallas_call | solution.py:499
  26.1 2.5 %first_forward.1 = (bf16[4,88,256]{2,1,0:T(8,128)(2,1)S(1)}, bf16[3,88,256]{2,1,0:T(8,128)(2,1)S(1)}, bf16[3,88,256]{2,1,0:T(8,128)(2,1)S(1)}) custom-call(s32[2]{0:T(128)S(1)} %pad_add_fusion.flags, f32[64,256]{1,0:T(8,128)S(1)} %get-tuple-element.79.small.small0, f32[352,128]{1,0:T(8,128)S(1)} %broadcast_in_dim.72.mask, f32[40960,256]{1,0:T(8,128)} %first_conv.1.kept, ...), custom_call_target="tpu_custom_call" | custom-call | flops 20000000000 | bytes 4194304 | tf_op jit(solution)/shard_map/first_forward/pallas_call | solution.py:499
  29.5 3.3 %collective-permute-start.10 = (bf16[3,88,256]{2,1,0:T(8,128)(2,1)S(1)}, bf16[3,88,256]{2,1,0:T(8,128)(2,1)S(1)}, u32[]{:S(2)}, u32[]{:S(2)}) collective-permute-start(bf16[3,88,256]{2,1,0:T(8,128)(2,1)S(1)} %get-tuple-element.73), channel_id=1, source_target_pairs={{4,8},{8,4},{5,9},{9,5},{6,10},{10,6},{7,11},{11,7},{20,24},{24,20... | collective-permute-start | bytes 405512 | tf_op jit(solution)/shard_map/ppermute | solution.py:543
  33.0 2.8 %collective-permute-done.10.y_b = bf16[3,88,256]{2,1,0:T(8,128)(2,1)S(1)} collective-permute-done((bf16[3,88,256]{2,1,0:T(8,128)(2,1)S(1)}, bf16[3,88,256]{2,1,0:T(8,128)(2,1)S(1)}, u32[]{:S(2)}, u32[]{:S(2)}) %collective-permute-start.10) | collective-permute-done | bytes 135200 | tf_op jit(solution)/shard_map/ppermute | solution.py:543
  36.0 0.9 copy-done.3
  36.9 5.5 %second_block.1 = (bf16[4,68,256]{2,1,0:T(8,128)(2,1)S(1)}, bf16[4,80,256]{2,1,0:T(8,128)(2,1)S(1)}, bf16[3,80,256]{2,1,0:T(8,128)(2,1)S(1)}, bf16[3,80,256]{2,1...) custom-call(s32[2]{0:T(128)S(1)} %pad_add_fusion.flags, ...), custom_call_target="tpu_custom_call" | custom-call | flops 40000000000 | bytes 4194304 | tf_op jit(solution)/shard_map/second_block/pallas_call | solution.py:499
  42.5 3.3 %collective-permute-start.12 = (bf16[3,80,256]{2,1,0:T(8,128)(2,1)S(1)}, bf16[3,80,256]{2,1,0:T(8,128)(2,1)S(1)}, u32[]{:S(2)}, u32[]{:S(2)}) collective-permute-start(bf16[3,80,256]{2,1,0:T(8,128)(2,1)S(1)} %get-tuple-element.78), channel_id=1, source_target_pairs={{4,8},{8,4},{5,9},{9,5},{6,10},{10,6},{7,11},{11,7},{20,24},{24,20... | collective-permute-start | bytes 368648 | tf_op jit(solution)/shard_map/ppermute | solution.py:543
  45.9 2.8 %first_again.1 = (bf16[352,1024]{1,0:T(8,128)(2,1)S(1)}, f32[352,1024]{1,0:T(8,128)S(1)}, f32[352,256]{1,0:T(8,128)S(1)}, bf16[256,1024]{1,0:T(8,128)(2,1)S(1)}, bf16[1024,256]{1,0:T(8,128)(2,1)S(1)}) custom-call(s32[2]{0:T(128)S(1)} %pad_add_fusion.flags, f32[64,256]{1,0:T(8,128)S(1)} %get-tuple-element.79.small.small0, f32[40960,256]{1,0:T(8,128)} %first_conv.1.kept, ...), custom_call_target="tpu_custom_call" | custom-call | flops 20000000000 | bytes 4194304 | tf_op jit(solution)/shard_map/first_again/pallas_call | solution.py:499
  48.9 4.5 %first_backward.1 = (f32[4,72,256]{2,1,0:T(8,128)S(1)}, bf16[4,88,256]{2,1,0:T(8,128)(2,1)S(1)}, bf16[3,88,256]{2,1,0:T(8,128)(2,1)S(1)}, bf16[3,88,256]{2,1,0:T...) custom-call(s32[2]{0:T(128)S(1)} %pad_add_fusion.flags, ...), custom_call_target="tpu_custom_call" | custom-call | flops 30000001024 | bytes 4194304 | tf_op jit(solution)/shard_map/first_backward/pallas_call | solution.py:499
  53.9 1.8 %tap_grads_0.1 = bf16[64,256]{1,0:T(8,128)(2,1)S(1)} custom-call(s32[2]{0:T(128)S(1)} %pad_add_fusion.flags, bf16[4,96,256]{2,1,0:T(8,128)(2,1)S(1)} %maximum_maximum_fusion.x.v, bf16[3,96,256]{2,1,0:T(8,128)(2,1)S(1)} %collective-permute-done.5.x_a.v_a, bf16[3,96,256]{2,1,0:T(8,128)(2,1)S(1)} %broadcast_select_fusion.4.x_b.v_b, ...), custom_call_target="tpu_custom_call" | custom-call | flops 20000000000 | bytes 4194304 | tf_op jit(solution)/shard_map/tap_grads_0/pallas_call | solution.py:499
  56.9 0.8 collective-permute-start.14
  57.7 1.7 %tap_grads_1.1 = bf16[64,256]{1,0:T(8,128)(2,1)S(1)} custom-call(s32[2]{0:T(128)S(1)} %pad_add_fusion.flags, f32[2,10,88,128]{3,2,1,0:T(8,128)S(1)} %get-tuple-element.93.pad, bf16[4,80,256]{2,1,0:T(8,128)(2,1)S(1)} %get-tuple-element.74.du1.du, f32[320,128]{1,0:T(8,128)S(1)} %broadcast_in_dim.79.own, f32[16,256]{1,0:T(8,128)S(1)} %get-tuple-element.94.sums), custom_call_target="tpu_custom_call" | custom-call | flops 20000000000 | bytes 4194304 | tf_op jit(solution)/shard_map/tap_grads_1/pallas_call | solution.py:499
  60.1 2.8 %collective-permute-start.18 = (bf16[3,88,256]{2,1,0:T(8,128)(2,1)S(1)}, bf16[3,88,256]{2,1,0:T(8,128)(2,1)S(1)}, u32[]{:S(2)}, u32[]{:S(2)}) collective-permute-start(bf16[3,88,256]{2,1,0:T(8,128)(2,1)S(1)} %get-tuple-element.98), channel_id=1, source_target_pairs={{4,8},{8,4},{5,9},{9,5},{6,10},{10,6},{7,11},{11,7},{20,24},{24,20... | collective-permute-start | bytes 405512 | tf_op jit(solution)/shard_map/ppermute | solution.py:543
  62.9 3.5 %collective-permute-done.18.du_b = bf16[3,88,256]{2,1,0:T(8,128)(2,1)S(1)} collective-permute-done((bf16[3,88,256]{2,1,0:T(8,128)(2,1)S(1)}, bf16[3,88,256]{2,1,0:T(8,128)(2,1)S(1)}, u32[]{:S(2)}, u32[]{:S(2)}) %collective-permute-start.18) | collective-permute-done | bytes 135200 | tf_op jit(solution)/shard_map/ppermute | solution.py:543
  66.8 5.2 %collective-permute-done.19 = bf16[2,256,256]{2,1,0:T(8,128)(2,1)S(1)} collective-permute-done((bf16[2,256,256]{2,1,0:T(8,128)(2,1)S(1)}, bf16[2,256,256]{2,1,0:T(8,128)(2,1)S(1)}, u32[]{:S(2)}, u32[]{:S(2)}) %collective-permute-start.19) | collective-permute-done | bytes 262176 | tf_op jit(solution)/shard_map/ppermute | solution.py:667
  72.1 1.7 %collective-permute-start.20 = (bf16[2,128,256]{2,1,0:T(8,128)(2,1)S(1)}, bf16[2,128,256]{2,1,0:T(8,128)(2,1)S(1)}, u32[]{:S(2)}, u32[]{:S(2)}) collective-permute-start(bf16[2,128,256]{2,1,0:T(8,128)(2,1)S(1)} %broadcast_select_fusion.7), channel_id=1, source_target_pairs={{0,2},{1,3},{2,0},{3,1},{4,6},{5,7},{6,4},{7,5},{8,10},{9,11},{10,... | collective-permute-start | bytes 393224 | tf_op jit(solution)/shard_map/ppermute | solution.py:667
  73.8 1.6 %input_grad.1 = bf16[4,68,256]{2,1,0:T(8,128)(2,1)S(1)} custom-call(s32[2]{0:T(128)S(1)} %pad_add_fusion.flags, bf16[4,88,256]{2,1,0:T(8,128)(2,1)S(1)} %get-tuple-element.87.du, bf16[3,88,256]{2,1,0:T(8,128)(2,1)S(1)} %collective-permute-done.17.du_a, bf16[3,88,256]{2,1,0:T(8,128)(2,1)S(1)} %collective-permute-done.18.du_b, ...), custom_call_target="tpu_custom_call" | custom-call | flops 20000000000 | bytes 4194304 | tf_op jit(solution)/shard_map/input_grad/pallas_call | solution.py:499
  75.4 5.7 %collective-permute-done.20 = bf16[2,128,256]{2,1,0:T(8,128)(2,1)S(1)} collective-permute-done((bf16[2,128,256]{2,1,0:T(8,128)(2,1)S(1)}, bf16[2,128,256]{2,1,0:T(8,128)(2,1)S(1)}, u32[]{:S(2)}, u32[]{:S(2)}) %collective-permute-start.20) | collective-permute-done | bytes 131104 | tf_op jit(solution)/shard_map/ppermute | solution.py:667
  81.5 3.2 %collective-permute-done.21 = bf16[192,256]{1,0:T(8,128)(2,1)S(1)} collective-permute-done((bf16[192,256]{1,0:T(8,128)(2,1)S(1)}, bf16[192,256]{1,0:T(8,128)(2,1)S(1)}, u32[]{:S(2)}, u32[]{:S(2)}) %collective-permute-start.21) | collective-permute-done | bytes 98336 | tf_op jit(solution)/shard_map/ppermute | solution.py:535
  85.2 5.1 %collective-permute-done.22 = bf16[192,256]{1,0:T(8,128)(2,1)S(1)} collective-permute-done((bf16[192,256]{1,0:T(8,128)(2,1)S(1)}, bf16[192,256]{1,0:T(8,128)(2,1)S(1)}, u32[]{:S(2)}, u32[]{:S(2)}) %collective-permute-start.22) | collective-permute-done | bytes 98336 | tf_op jit(solution)/shard_map/ppermute | solution.py:667
  90.5 4.1 %collective-permute-done.23 = bf16[320,256]{1,0:T(8,128)(2,1)S(1)} collective-permute-done((bf16[320,256]{1,0:T(8,128)(2,1)S(1)}, bf16[320,256]{1,0:T(8,128)(2,1)S(1)}, u32[]{:S(2)}, u32[]{:S(2)}) %collective-permute-start.23) | collective-permute-done | bytes 163872 | tf_op jit(solution)/shard_map/ppermute | solution.py:667
  95.2 6.0 %collective-permute-done.25 = bf16[576,256]{1,0:T(8,128)(2,1)S(1)} collective-permute-done((bf16[576,256]{1,0:T(8,128)(2,1)S(1)}, bf16[576,256]{1,0:T(8,128)(2,1)S(1)}, u32[]{:S(2)}, u32[]{:S(2)}) %collective-permute-start.25) | collective-permute-done | bytes 294944 | tf_op jit(solution)/shard_map/ppermute | solution.py:667
  101.5 5.4 %collective-permute-start.26 = (bf16[1088,256]{1,0:T(8,128)(2,1)S(1)}, bf16[1088,256]{1,0:T(8,128)(2,1)S(1)}, u32[]{:S(2)}, u32[]{:S(2)}) collective-permute-start(bf16[1088,256]{1,0:T(8,128)(2,1)S(1)} %pad_maximum_fusion), channel_id=1, source_target_pairs={{0,4},{4,0},{8,12},{12,8},{1,5},{5,1},{9,13},{13,9},{2,6},{6,2},{1... | collective-permute-start | bytes 1671176 | tf_op jit(solution)/shard_map/ppermute | solution.py:538
  107.7 1.6 %finish_own.1 = (f32[1,256,1024]{2,1,0:T(8,128)}, f32[1,1024,256]{2,1,0:T(8,128)}) custom-call(s32[2]{0:T(128)S(1)} %pad_add_fusion.flags, bf16[1024,256]{1,0:T(8,128)(2,1)S(1)} %maximum_select_fusion.piece), custom_call_target="tpu_custom_call" | custom-call | flops 10000000 | bytes 4194304 | tf_op jit(solution)/shard_map/finish_own/pallas_call | solution.py:499
  109.4 2.2 %finish_got.1 = (f32[1,256,1024]{2,1,0:T(8,128)}, f32[1,1024,256]{2,1,0:T(8,128)}, f32[49,1,256]{2,1,0:T(1,128)}, f32[5,1,256]{2,1,0:T(1,128)}, f32[1,1024]{1,0:T(1,128)}) custom-call(s32[2]{0:T(128)S(1)} %pad_add_fusion.flags, bf16[64,256]{1,0:T(8,128)(2,1)S(1)} %add_convert_fusion.6.small, ...), custom_call_target="tpu_custom_call", output_to_operand_aliasing={{0}: (3, {}), {1}: (4, {})} | custom-call | flops 10000000 | bytes 4194304 | tf_op jit(solution)/shard_map/finish_got/pallas_call | solution.py:499
  (129 shorter events, 12.0 us)
Async XLA Ops:
  0.6 3.0 %copy-start.4 = (bf16[1,49,256]{2,1,0:T(8,128)(2,1)S(1)}, bf16[1,49,256]{2,1,0:T(8,128)(2,1)}, u32[]{:S(2)}) copy-start(bf16[1,49,256]{2,1,0:T(8,128)(2,1)} %param.11) | copy-start | bytes 75268
  0.6 3.0 %copy-start.5 = (bf16[1,5,256]{2,1,0:T(8,128)(2,1)S(1)}, bf16[1,5,256]{2,1,0:T(8,128)(2,1)}, u32[]{:S(2)}) copy-start(bf16[1,5,256]{2,1,0:T(8,128)(2,1)} %param.12) | copy-start | bytes 7684
  0.7 8.5 %copy-start = (bf16[1,256,1024]{2,1,0:T(8,128)(2,1)S(1)}, bf16[1,256,1024]{2,1,0:T(8,128)(2,1)}, u32[]{:S(2)}) copy-start(bf16[1,256,1024]{2,1,0:T(8,128)(2,1)} %param.13) | copy-start | bytes 1572868
  2.2 6.9 %copy-start.1 = (bf16[1,1024,256]{2,1,0:T(8,128)(2,1)S(1)}, bf16[1,1024,256]{2,1,0:T(8,128)(2,1)}, u32[]{:S(2)}) copy-start(bf16[1,1024,256]{2,1,0:T(8,128)(2,1)} %param.15) | copy-start | bytes 1572868
  3.7 5.8 %collective-permute-start = (bf16[64,256]{1,0:T(8,128)(2,1)S(1)}, bf16[64,256]{1,0:T(8,128)(2,1)S(1)}, u32[]{:S(2)}, u32[]{:S(2)}) collective-permute-start(bf16[64,256]{1,0:T(8,128)(2,1)S(1)} %maximum_maximum_fusion.1), channel_id=1, source_target_pairs={{0,16},{16,0},{1,17},{17,1},{2,18},{18,2},{3,19},{19,3},{4,20},{20... | collective-permute-start | bytes 98312 | tf_op jit(solution)/shard_map/ppermute | solution.py:535
  5.8 5.2 %collective-permute-start.1 = (bf16[4,19,256]{2,1,0:T(8,128)(2,1)S(1)}, bf16[4,19,256]{2,1,0:T(8,128)(2,1)S(1)}, u32[]{:S(2)}, u32[]{:S(2)}) collective-permute-start(bf16[4,19,256]{2,1,0:T(8,128)(2,1)S(1)} %pad_maximum_fusion.6), channel_id=1, source_target_pairs={{0,1},{1,2},{2,3},{3,0},{4,5},{5,6},{6,7},{7,4},{8,9},{9,10},{10,1... | collective-permute-start | bytes 116744 | tf_op jit(solution)/shard_map/ppermute | solution.py:564
  7.1 4.0 %collective-permute-start.2 = (bf16[4,19,256]{2,1,0:T(8,128)(2,1)S(1)}, bf16[4,19,256]{2,1,0:T(8,128)(2,1)S(1)}, u32[]{:S(2)}, u32[]{:S(2)}) collective-permute-start(bf16[4,19,256]{2,1,0:T(8,128)(2,1)S(1)} %pad_maximum_fusion.7), channel_id=1, source_target_pairs={{1,0},{2,1},{3,2},{0,3},{5,4},{6,5},{7,6},{4,7},{9,8},{10,9},{11,1... | collective-permute-start | bytes 116744 | tf_op jit(solution)/shard_map/ppermute | solution.py:565
  9.5 14.7 %collective-permute-start.3 = (bf16[128,1024]{1,0:T(8,128)(2,1)S(1)}, bf16[128,1024]{1,0:T(8,128)(2,1)S(1)}, u32[]{:S(2)}, u32[]{:S(2)}) collective-permute-start(bf16[128,1024]{1,0:T(8,128)(2,1)S(1)} %select_bitcast_fusion.1), channel_id=1, source_target_pairs={{0,16},{16,0},{1,17},{17,1},{2,18},{18,2},{3,19},{19,3},{4,20},{20... | collective-permute-start | bytes 786440 | tf_op jit(solution)/shard_map/ppermute | solution.py:535
  9.7 14.4 %collective-permute-start.4 = (bf16[512,256]{1,0:T(8,128)(2,1)S(1)}, bf16[512,256]{1,0:T(8,128)(2,1)S(1)}, u32[]{:S(2)}, u32[]{:S(2)}) collective-permute-start(bf16[512,256]{1,0:T(8,128)(2,1)S(1)} %select_bitcast_fusion), channel_id=1, source_target_pairs={{0,16},{16,0},{1,17},{17,1},{2,18},{18,2},{3,19},{19,3},{4,20},{20... | collective-permute-start | bytes 786440 | tf_op jit(solution)/shard_map/ppermute | solution.py:535
  11.2 8.2 %collective-permute-start.6 = (bf16[3,96,256]{2,1,0:T(8,128)(2,1)S(1)}, bf16[3,96,256]{2,1,0:T(8,128)(2,1)S(1)}, u32[]{:S(2)}, u32[]{:S(2)}) collective-permute-start(bf16[3,96,256]{2,1,0:T(8,128)(2,1)S(1)} %get-tuple-element.136), channel_id=1, source_target_pairs={{4,8},{8,4},{5,9},{9,5},{6,10},{10,6},{7,11},{11,7},{20,24},{24,20... | collective-permute-start | bytes 442376 | tf_op jit(solution)/shard_map/ppermute | solution.py:543
  16.5 3.0 %collective-permute-start.5 = (bf16[3,96,256]{2,1,0:T(8,128)(2,1)S(1)}, bf16[3,96,256]{2,1,0:T(8,128)(2,1)S(1)}, u32[]{:S(2)}, u32[]{:S(2)}) collective-permute-start(bf16[3,96,256]{2,1,0:T(8,128)(2,1)S(1)} %get-tuple-element.137), channel_id=1, source_target_pairs={{0,4},{4,0},{8,12},{12,8},{1,5},{5,1},{9,13},{13,9},{2,6},{6,2},{1... | collective-permute-start | bytes 442376 | tf_op jit(solution)/shard_map/ppermute | solution.py:538
  24.1 1.6 %collective-permute-start.7 = (bf16[128,1024]{1,0:T(8,128)(2,1)S(1)}, bf16[128,1024]{1,0:T(8,128)(2,1)S(1)}, u32[]{:S(2)}, u32[]{:S(2)}) collective-permute-start(bf16[128,1024]{1,0:T(8,128)(2,1)S(1)} %collective-permute-done.3.refs_2_), channel_id=1, source_target_pairs={{0,4},{4,0},{8,12},{12,8},{1,5},{5,1},{9,13},{13,9},{2,6},{6,2},{1... | collective-permute-start | bytes 786440 | tf_op jit(solution)/shard_map/ppermute | solution.py:538
  24.2 1.9 %collective-permute-start.8 = (bf16[512,256]{1,0:T(8,128)(2,1)S(1)}, bf16[512,256]{1,0:T(8,128)(2,1)S(1)}, u32[]{:S(2)}, u32[]{:S(2)}) collective-permute-start(bf16[512,256]{1,0:T(8,128)(2,1)S(1)} %collective-permute-done.4.refs_3_), channel_id=1, source_target_pairs={{0,4},{4,0},{8,12},{12,8},{1,5},{5,1},{9,13},{13,9},{2,6},{6,2},{1... | collective-permute-start | bytes 786440 | tf_op jit(solution)/shard_map/ppermute | solution.py:538
  29.3 3.6 %collective-permute-start.9 = (bf16[3,88,256]{2,1,0:T(8,128)(2,1)S(1)}, bf16[3,88,256]{2,1,0:T(8,128)(2,1)S(1)}, u32[]{:S(2)}, u32[]{:S(2)}) collective-permute-start(bf16[3,88,256]{2,1,0:T(8,128)(2,1)S(1)} %get-tuple-element.72), channel_id=1, source_target_pairs={{0,4},{4,0},{8,12},{12,8},{1,5},{5,1},{9,13},{13,9},{2,6},{6,2},{1... | collective-permute-start | bytes 405512 | tf_op jit(solution)/shard_map/ppermute | solution.py:538
  29.5 6.3 %collective-permute-start.10 = (bf16[3,88,256]{2,1,0:T(8,128)(2,1)S(1)}, bf16[3,88,256]{2,1,0:T(8,128)(2,1)S(1)}, u32[]{:S(2)}, u32[]{:S(2)}) collective-permute-start(bf16[3,88,256]{2,1,0:T(8,128)(2,1)S(1)} %get-tuple-element.73), channel_id=1, source_target_pairs={{4,8},{8,4},{5,9},{9,5},{6,10},{10,6},{7,11},{11,7},{20,24},{24,20... | collective-permute-start | bytes 405512 | tf_op jit(solution)/shard_map/ppermute | solution.py:543
  36.0 0.9 copy-start.3
  42.4 6.2 %collective-permute-start.11 = (bf16[3,80,256]{2,1,0:T(8,128)(2,1)S(1)}, bf16[3,80,256]{2,1,0:T(8,128)(2,1)S(1)}, u32[]{:S(2)}, u32[]{:S(2)}) collective-permute-start(bf16[3,80,256]{2,1,0:T(8,128)(2,1)S(1)} %get-tuple-element.76), channel_id=1, source_target_pairs={{0,4},{4,0},{8,12},{12,8},{1,5},{5,1},{9,13},{13,9},{2,6},{6,2},{1... | collective-permute-start | bytes 368648 | tf_op jit(solution)/shard_map/ppermute | solution.py:538
  42.5 6.2 %collective-permute-start.12 = (bf16[3,80,256]{2,1,0:T(8,128)(2,1)S(1)}, bf16[3,80,256]{2,1,0:T(8,128)(2,1)S(1)}, u32[]{:S(2)}, u32[]{:S(2)}) collective-permute-start(bf16[3,80,256]{2,1,0:T(8,128)(2,1)S(1)} %get-tuple-element.78), channel_id=1, source_target_pairs={{4,8},{8,4},{5,9},{9,5},{6,10},{10,6},{7,11},{11,7},{20,24},{24,20... | collective-permute-start | bytes 368648 | tf_op jit(solution)/shard_map/ppermute | solution.py:543
  48.7 7.1 %collective-permute-start.15 = (bf16[1024,256]{1,0:T(8,128)(2,1)S(1)}, bf16[1024,256]{1,0:T(8,128)(2,1)S(1)}, u32[]{:S(2)}, u32[]{:S(2)}) collective-permute-start(bf16[1024,256]{1,0:T(8,128)(2,1)S(1)} %get-tuple-element.92), channel_id=1, source_target_pairs={{0,4},{4,0},{8,12},{12,8},{1,5},{5,1},{9,13},{13,9},{2,6},{6,2},{1... | collective-permute-start | bytes 1572872 | tf_op jit(solution)/shard_map/ppermute | solution.py:538
  53.3 3.4 %collective-permute-start.13 = (bf16[1024,256]{1,0:T(8,128)(2,1)S(1)}, bf16[1024,256]{1,0:T(8,128)(2,1)S(1)}, u32[]{:S(2)}, u32[]{:S(2)}) collective-permute-start(bf16[1024,256]{1,0:T(8,128)(2,1)S(1)} %get-tuple-element.86), channel_id=1, source_target_pairs={{0,4},{4,0},{8,12},{12,8},{1,5},{5,1},{9,13},{13,9},{2,6},{6,2},{1... | collective-permute-start | bytes 1572872 | tf_op jit(solution)/shard_map/ppermute | solution.py:538
  55.9 10.5 %collective-permute-start.16 = (bf16[512,256]{1,0:T(8,128)(2,1)S(1)}, bf16[512,256]{1,0:T(8,128)(2,1)S(1)}, u32[]{:S(2)}, u32[]{:S(2)}) collective-permute-start(bf16[512,256]{1,0:T(8,128)(2,1)S(1)} %broadcast_select_fusion), channel_id=1, source_target_pairs={{0,8},{1,9},{2,10},{3,11},{4,5},{5,4},{6,7},{7,6},{8,0},{9,1},{10,... | collective-permute-start | bytes 786440 | tf_op jit(solution)/shard_map/ppermute | solution.py:667
  56.9 9.5 %collective-permute-start.14 = (bf16[512,256]{1,0:T(8,128)(2,1)S(1)}, bf16[512,256]{1,0:T(8,128)(2,1)S(1)}, u32[]{:S(2)}, u32[]{:S(2)}) collective-permute-start(bf16[512,256]{1,0:T(8,128)(2,1)S(1)} %broadcast_select_fusion.1), channel_id=1, source_target_pairs={{0,8},{1,9},{2,10},{3,11},{4,5},{5,4},{6,7},{7,6},{8,0},{9,1},{10,... | collective-permute-start | bytes 786440 | tf_op jit(solution)/shard_map/ppermute | solution.py:667
  59.4 3.5 %collective-permute-start.17 = (bf16[3,88,256]{2,1,0:T(8,128)(2,1)S(1)}, bf16[3,88,256]{2,1,0:T(8,128)(2,1)S(1)}, u32[]{:S(2)}, u32[]{:S(2)}) collective-permute-start(bf16[3,88,256]{2,1,0:T(8,128)(2,1)S(1)} %get-tuple-element.97), channel_id=1, source_target_pairs={{0,4},{4,0},{8,12},{12,8},{1,5},{5,1},{9,13},{13,9},{2,6},{6,2},{1... | collective-permute-start | bytes 405512 | tf_op jit(solution)/shard_map/ppermute | solution.py:538
  60.1 6.3 %collective-permute-start.18 = (bf16[3,88,256]{2,1,0:T(8,128)(2,1)S(1)}, bf16[3,88,256]{2,1,0:T(8,128)(2,1)S(1)}, u32[]{:S(2)}, u32[]{:S(2)}) collective-permute-start(bf16[3,88,256]{2,1,0:T(8,128)(2,1)S(1)} %get-tuple-element.98), channel_id=1, source_target_pairs={{4,8},{8,4},{5,9},{9,5},{6,10},{10,6},{7,11},{11,7},{20,24},{24,20... | collective-permute-start | bytes 405512 | tf_op jit(solution)/shard_map/ppermute | solution.py:543
  66.7 5.3 %collective-permute-start.19 = (bf16[2,256,256]{2,1,0:T(8,128)(2,1)S(1)}, bf16[2,256,256]{2,1,0:T(8,128)(2,1)S(1)}, u32[]{:S(2)}, u32[]{:S(2)}) collective-permute-start(bf16[2,256,256]{2,1,0:T(8,128)(2,1)S(1)} %broadcast_select_fusion.2), channel_id=1, source_target_pairs={{0,1},{1,0},{2,3},{3,2},{4,12},{5,13},{6,14},{7,15},{8,9},{9,8},{1... | collective-permute-start | bytes 786440 | tf_op jit(solution)/shard_map/ppermute | solution.py:667
  72.1 9.0 %collective-permute-start.20 = (bf16[2,128,256]{2,1,0:T(8,128)(2,1)S(1)}, bf16[2,128,256]{2,1,0:T(8,128)(2,1)S(1)}, u32[]{:S(2)}, u32[]{:S(2)}) collective-permute-start(bf16[2,128,256]{2,1,0:T(8,128)(2,1)S(1)} %broadcast_select_fusion.7), channel_id=1, source_target_pairs={{0,2},{1,3},{2,0},{3,1},{4,6},{5,7},{6,4},{7,5},{8,10},{9,11},{10,... | collective-permute-start | bytes 393224 | tf_op jit(solution)/shard_map/ppermute | solution.py:667
  81.1 3.5 %collective-permute-start.21 = (bf16[192,256]{1,0:T(8,128)(2,1)S(1)}, bf16[192,256]{1,0:T(8,128)(2,1)S(1)}, u32[]{:S(2)}, u32[]{:S(2)}) collective-permute-start(bf16[192,256]{1,0:T(8,128)(2,1)S(1)} %pad_maximum_fusion.4), channel_id=1, source_target_pairs={{0,16},{16,0},{1,17},{17,1},{2,18},{18,2},{3,19},{19,3},{4,20},{20... | collective-permute-start | bytes 294920 | tf_op jit(solution)/shard_map/ppermute | solution.py:535
  84.7 5.5 %collective-permute-start.22 = (bf16[192,256]{1,0:T(8,128)(2,1)S(1)}, bf16[192,256]{1,0:T(8,128)(2,1)S(1)}, u32[]{:S(2)}, u32[]{:S(2)}) collective-permute-start(bf16[192,256]{1,0:T(8,128)(2,1)S(1)} %pad_maximum_fusion.5), channel_id=1, source_target_pairs={{0,2},{1,3},{2,0},{3,1},{4,6},{5,7},{6,4},{7,5},{8,10},{9,11},{10,... | collective-permute-start | bytes 294920 | tf_op jit(solution)/shard_map/ppermute | solution.py:667
  84.8 5.5 %collective-permute-start.24 = (bf16[4,68,256]{2,1,0:T(8,128)(2,1)S(1)}, bf16[4,68,256]{2,1,0:T(8,128)(2,1)S(1)}, u32[]{:S(2)}, u32[]{:S(2)}) collective-permute-start(bf16[4,68,256]{2,1,0:T(8,128)(2,1)S(1)} %broadcast_select_fusion.3), channel_id=1, source_target_pairs={{0,16},{16,0},{1,17},{17,1},{2,18},{18,2},{3,19},{19,3},{4,20},{20... | collective-permute-start | bytes 417800 | tf_op jit(solution)/shard_map/ppermute | solution.py:535
  90.3 4.2 %collective-permute-start.23 = (bf16[320,256]{1,0:T(8,128)(2,1)S(1)}, bf16[320,256]{1,0:T(8,128)(2,1)S(1)}, u32[]{:S(2)}, u32[]{:S(2)}) collective-permute-start(bf16[320,256]{1,0:T(8,128)(2,1)S(1)} %pad_maximum_fusion.3), channel_id=1, source_target_pairs={{0,1},{1,0},{2,3},{3,2},{4,12},{5,13},{6,14},{7,15},{8,9},{9,8},{1... | collective-permute-start | bytes 491528 | tf_op jit(solution)/shard_map/ppermute | solution.py:667
  94.7 6.5 %collective-permute-start.25 = (bf16[576,256]{1,0:T(8,128)(2,1)S(1)}, bf16[576,256]{1,0:T(8,128)(2,1)S(1)}, u32[]{:S(2)}, u32[]{:S(2)}) collective-permute-start(bf16[576,256]{1,0:T(8,128)(2,1)S(1)} %pad_maximum_fusion.1), channel_id=1, source_target_pairs={{0,8},{1,9},{2,10},{3,11},{4,5},{5,4},{6,7},{7,6},{8,0},{9,1},{10,... | collective-permute-start | bytes 884744 | tf_op jit(solution)/shard_map/ppermute | solution.py:667
  101.5 7.8 %collective-permute-start.26 = (bf16[1088,256]{1,0:T(8,128)(2,1)S(1)}, bf16[1088,256]{1,0:T(8,128)(2,1)S(1)}, u32[]{:S(2)}, u32[]{:S(2)}) collective-permute-start(bf16[1088,256]{1,0:T(8,128)(2,1)S(1)} %pad_maximum_fusion), channel_id=1, source_target_pairs={{0,4},{4,0},{8,12},{12,8},{1,5},{5,1},{9,13},{13,9},{2,6},{6,2},{1... | collective-permute-start | bytes 1671176 | tf_op jit(solution)/shard_map/ppermute | solution.py:538
  (1 other events, 0.7 us)

commit v5 on v4

--- a/solution.py
+++ b/solution.py
@@ -560,7 +560,7 @@
     ring = [(i, (i + 1) % n_lon) for i in range(n_lon)]
     to_right = packed(x[:, -SIDE_X:], cot[:, -SIDE_1:], sea[:, -SIDE_0:])
     to_left = packed(x[:, :SIDE_X], cot[:, :SIDE_1], sea[:, :SIDE_0])
-    to_right, to_left, dw_kernel = lax.optimization_barrier((to_right, to_left, dw_kernel))
+    to_right, to_left, dw_kernel, up_bias = lax.optimization_barrier((to_right, to_left, dw_kernel, up_bias))
     left = lax.ppermute(to_right, "lon", ring)
     right = lax.ppermute(to_left, "lon", [(j, i) for i, j in ring])
     small_own = jnp.concatenate(
@@ -631,7 +631,7 @@
         hbm_in=7,
         sems=((6,), (2,)),
     )
-    y_a, y_b = lat_halo(y_send_a, y_send_b)
+    y_a, y_b = lat_halo(y_send_a, y_send_b, True)
     final, du1, du1_send_a, du1_send_b, keep_1, send_1, sums_1, pad_1 = call(
         second_block,
         "second_block",

time: 112 us -> 111 us (level)
  local copies, waits for them, and re-layouts: 4.78 us -> 3.2 us
    unnamed x15 -> x13, local copies, waits for them, and re-layouts: 2.43 us -> 0.85 us
  transfers between devices with their start and end apart: 27 -> 27, of which waited for: 11 -> 11; matrix products, arithmetic and copies ran while one was open for 2% -> 3% of each run, Pallas kernels for 17% -> 17%
where the time goes in v5:
time: 111 us; the launch traced here: 110 us
  waiting for transfers between devices  39.6 us (36%)
  starting transfers between devices  33.4 us (30%)
  Pallas kernels  28.8 us (26%)
  other arithmetic  3.86 us (3%)
  local copies, waits for them, and re-layouts  3.2 us (3%)
  between operations  1.52 us (1%)
    pallas_call x10, Pallas kernels, call(): pl.pallas_call(body, name=name, out_shape=[jax.ShapeDtypeStruct(shape, dt...  28.8 us
    ppermute x7, waiting for transfers between devices, exchange(): return lax.ppermute(value, ('lat', 'lon'), pairs)  26 us
    ppermute x4, starting transfers between devices, lat_halo(): got_b = lax.ppermute(send_b, 'lat', pairs)  14.6 us
    ppermute x4, waiting for transfers between devices, lat_halo(): got_b = lax.ppermute(send_b, 'lat', pairs)  9.33 us
    ppermute x9, starting transfers between devices, over_core(): return lax.ppermute(value, 'lat', swap_pairs(n_lat, 1))  7.3 us
    ppermute x5, starting transfers between devices, over_section(): return lax.ppermute(value, 'section', [(0, 1), (1, 0)])  4.22 us
    ppermute x7, starting transfers between devices, exchange(): return lax.ppermute(value, ('lat', 'lon'), pairs)  3.99 us
    ppermute x5, waiting for transfers between devices, over_section(): return lax.ppermute(value, 'section', [(0, 1), (1, 0)])  3.22 us
  transfers between devices with their start and end apart: 27, of which 11 were waited for; matrix products, arithmetic and copies ran while one was open for 3% of the time, Pallas kernels for 17%

profile of v5, /device:TPU:1, one launch (start us, length us, event | category | flops | bytes accessed | tf_op | source)
XLA Modules:
  0.0 110.5 jit_solution(17997867854435509487)
XLA Ops:
  1.5 1.1 %constant_dynamic-slice_fusion = (bf16[1,4,68,256]{3,1,2,0:T(4,128)(2,1)S(1)}, bf16[1,4,68,256]{3,1,2,0:T(4,128)(2,1)S(1)}) fusion(bf16[2,4,68,256]{3,1,2,0:T(4,128)(2,1)} %param.9, s32[]{:T(128)S(6)} %select_n.260, bf16[2,4,68,256]{3,1,2,0:T(4,128)(2,1)} %param.8), kind=kLoop, calls=%fused_computation.60 | loop fusion | bytes 557060 | tf_op jit(solution)/shard_map/jit(dynamic_index_in_dim)/dynamic_slice | solution.py:553
  3.0 2.1 %collective-permute-start = (bf16[64,256]{1,0:T(8,128)(2,1)S(1)}, bf16[64,256]{1,0:T(8,128)(2,1)S(1)}, u32[]{:S(2)}, u32[]{:S(2)}) collective-permute-start(bf16[64,256]{1,0:T(8,128)(2,1)S(1)} %maximum_maximum_fusion.1), channel_id=1, source_target_pairs={{0,16},{16,0},{1,17},{17,1},{2,18},{18,2},{3,19},{19,3},{4,20},{20... | collective-permute-start | bytes 98312 | tf_op jit(solution)/shard_map/ppermute | solution.py:535
  5.1 1.3 %collective-permute-start.1 = (bf16[4,19,256]{2,1,0:T(8,128)(2,1)S(1)}, bf16[4,19,256]{2,1,0:T(8,128)(2,1)S(1)}, u32[]{:S(2)}, u32[]{:S(2)}) collective-permute-start(bf16[4,19,256]{2,1,0:T(8,128)(2,1)S(1)} %pad_maximum_fusion.6), channel_id=1, source_target_pairs={{0,1},{1,2},{2,3},{3,0},{4,5},{5,6},{6,7},{7,4},{8,9},{9,10},{10,1... | collective-permute-start | bytes 116744 | tf_op jit(solution)/shard_map/ppermute | solution.py:564
  6.4 2.0 %collective-permute-start.2 = (bf16[4,19,256]{2,1,0:T(8,128)(2,1)S(1)}, bf16[4,19,256]{2,1,0:T(8,128)(2,1)S(1)}, u32[]{:S(2)}, u32[]{:S(2)}) collective-permute-start(bf16[4,19,256]{2,1,0:T(8,128)(2,1)S(1)} %pad_maximum_fusion.7), channel_id=1, source_target_pairs={{1,0},{2,1},{3,2},{0,3},{5,4},{6,5},{7,6},{4,7},{9,8},{10,9},{11,1... | collective-permute-start | bytes 116744 | tf_op jit(solution)/shard_map/ppermute | solution.py:565
  9.1 1.2 %collective-permute-start.4 = (bf16[512,256]{1,0:T(8,128)(2,1)S(1)}, bf16[512,256]{1,0:T(8,128)(2,1)S(1)}, u32[]{:S(2)}, u32[]{:S(2)}) collective-permute-start(bf16[512,256]{1,0:T(8,128)(2,1)S(1)} %select_bitcast_fusion), channel_id=1, source_target_pairs={{0,16},{16,0},{1,17},{17,1},{2,18},{18,2},{3,19},{19,3},{4,20},{20... | collective-permute-start | bytes 786440 | tf_op jit(solution)/shard_map/ppermute | solution.py:535
  10.6 5.1 %collective-permute-start.6 = (bf16[3,96,256]{2,1,0:T(8,128)(2,1)S(1)}, bf16[3,96,256]{2,1,0:T(8,128)(2,1)S(1)}, u32[]{:S(2)}, u32[]{:S(2)}) collective-permute-start(bf16[3,96,256]{2,1,0:T(8,128)(2,1)S(1)} %get-tuple-element.138), channel_id=1, source_target_pairs={{4,8},{8,4},{5,9},{9,5},{6,10},{10,6},{7,11},{11,7},{20,24},{24,20... | collective-permute-start | bytes 442376 | tf_op jit(solution)/shard_map/ppermute | solution.py:543
  15.8 2.9 %collective-permute-done.6 = bf16[3,96,256]{2,1,0:T(8,128)(2,1)S(1)} collective-permute-done((bf16[3,96,256]{2,1,0:T(8,128)(2,1)S(1)}, bf16[3,96,256]{2,1,0:T(8,128)(2,1)S(1)}, u32[]{:S(2)}, u32[]{:S(2)}) %collective-permute-start.6) | collective-permute-done | bytes 147488 | tf_op jit(solution)/shard_map/ppermute | solution.py:543
  18.9 4.5 %first_conv.1.kept = f32[40960,256]{1,0:T(8,128)} custom-call(s32[2]{0:T(128)S(1)} %pad_add_fusion.flags, bf16[4,96,256]{2,1,0:T(8,128)(2,1)S(1)} %maximum_maximum_fusion.x.v, bf16[3,96,256]{2,1,0:T(8,128)(2,1)S(1)} %collective-permute-done.5.x_a.v_a, bf16[3,96,256]{2,1,0:T(8,128)(2,1)S(1)} %broadcast_select_fusion.4.x_b.v_b, ...), custom_call_target="tpu_custom_call" | custom-call | flops 20000000000 | bytes 4194304 | tf_op jit(solution)/shard_map/first_conv/pallas_call | solution.py:499
  25.4 2.5 %first_forward.1 = (bf16[4,88,256]{2,1,0:T(8,128)(2,1)S(1)}, bf16[3,88,256]{2,1,0:T(8,128)(2,1)S(1)}, bf16[3,88,256]{2,1,0:T(8,128)(2,1)S(1)}) custom-call(s32[2]{0:T(128)S(1)} %pad_add_fusion.flags, f32[64,256]{1,0:T(8,128)S(1)} %get-tuple-element.81.small.small0, f32[352,128]{1,0:T(8,128)S(1)} %broadcast_in_dim.75.mask, f32[40960,256]{1,0:T(8,128)} %first_conv.1.kept, ...), custom_call_target="tpu_custom_call" | custom-call | flops 20000000000 | bytes 4194304 | tf_op jit(solution)/shard_map/first_forward/pallas_call | solution.py:499
  28.0 3.4 %collective-permute-start.10 = (bf16[3,88,256]{2,1,0:T(8,128)(2,1)S(1)}, bf16[3,88,256]{2,1,0:T(8,128)(2,1)}, u32[]{:S(2)}, u32[]{:S(2)}) collective-permute-start(bf16[3,88,256]{2,1,0:T(8,128)(2,1)S(1)} %get-tuple-element.75), channel_id=1, source_target_pairs={{4,8},{8,4},{5,9},{9,5},{6,10},{10,6},{7,11},{11,7},{20,24},{24,20... | collective-permute-start | bytes 405512 | tf_op jit(solution)/shard_map/ppermute | solution.py:543
  31.5 2.9 %collective-permute-done.10 = bf16[3,88,256]{2,1,0:T(8,128)(2,1)} collective-permute-done((bf16[3,88,256]{2,1,0:T(8,128)(2,1)S(1)}, bf16[3,88,256]{2,1,0:T(8,128)(2,1)}, u32[]{:S(2)}, u32[]{:S(2)}) %collective-permute-start.10) | collective-permute-done | bytes 135200 | tf_op jit(solution)/shard_map/ppermute | solution.py:543
  34.4 0.9 broadcast_select_fusion.7.y_b
  35.6 5.6 %second_block.1 = (bf16[4,68,256]{2,1,0:T(8,128)(2,1)S(1)}, bf16[4,80,256]{2,1,0:T(8,128)(2,1)S(1)}, bf16[3,80,256]{2,1,0:T(8,128)(2,1)S(1)}, bf16[3,80,256]{2,1...) custom-call(s32[2]{0:T(128)S(1)} %pad_add_fusion.flags, ...), custom_call_target="tpu_custom_call" | custom-call | flops 40000000000 | bytes 4194304 | tf_op jit(solution)/shard_map/second_block/pallas_call | solution.py:499
  41.2 3.4 %collective-permute-start.12 = (bf16[3,80,256]{2,1,0:T(8,128)(2,1)S(1)}, bf16[3,80,256]{2,1,0:T(8,128)(2,1)S(1)}, u32[]{:S(2)}, u32[]{:S(2)}) collective-permute-start(bf16[3,80,256]{2,1,0:T(8,128)(2,1)S(1)} %get-tuple-element.80), channel_id=1, source_target_pairs={{4,8},{8,4},{5,9},{9,5},{6,10},{10,6},{7,11},{11,7},{20,24},{24,20... | collective-permute-start | bytes 368648 | tf_op jit(solution)/shard_map/ppermute | solution.py:543
  44.6 2.8 %first_again.1 = (bf16[352,1024]{1,0:T(8,128)(2,1)S(1)}, f32[352,1024]{1,0:T(8,128)S(1)}, f32[352,256]{1,0:T(8,128)S(1)}, bf16[256,1024]{1,0:T(8,128)(2,1)S(1)}, bf16[1024,256]{1,0:T(8,128)(2,1)S(1)}) custom-call(s32[2]{0:T(128)S(1)} %pad_add_fusion.flags, f32[64,256]{1,0:T(8,128)S(1)} %get-tuple-element.81.small.small0, f32[40960,256]{1,0:T(8,128)} %first_conv.1.kept, ...), custom_call_target="tpu_custom_call" | custom-call | flops 20000000000 | bytes 4194304 | tf_op jit(solution)/shard_map/first_again/pallas_call | solution.py:499
  47.6 4.5 %first_backward.1 = (f32[4,72,256]{2,1,0:T(8,128)S(1)}, bf16[4,88,256]{2,1,0:T(8,128)(2,1)S(1)}, bf16[3,88,256]{2,1,0:T(8,128)(2,1)S(1)}, bf16[3,88,256]{2,1,0:T...) custom-call(s32[2]{0:T(128)S(1)} %pad_add_fusion.flags, ...), custom_call_target="tpu_custom_call" | custom-call | flops 30000001024 | bytes 4194304 | tf_op jit(solution)/shard_map/first_backward/pallas_call | solution.py:499
  52.6 1.8 %tap_grads_0.1 = bf16[64,256]{1,0:T(8,128)(2,1)S(1)} custom-call(s32[2]{0:T(128)S(1)} %pad_add_fusion.flags, bf16[4,96,256]{2,1,0:T(8,128)(2,1)S(1)} %maximum_maximum_fusion.x.v, bf16[3,96,256]{2,1,0:T(8,128)(2,1)S(1)} %collective-permute-done.5.x_a.v_a, bf16[3,96,256]{2,1,0:T(8,128)(2,1)S(1)} %broadcast_select_fusion.4.x_b.v_b, ...), custom_call_target="tpu_custom_call" | custom-call | flops 20000000000 | bytes 4194304 | tf_op jit(solution)/shard_map/tap_grads_0/pallas_call | solution.py:499
  55.6 0.8 collective-permute-start.14
  56.5 1.7 %tap_grads_1.1 = bf16[64,256]{1,0:T(8,128)(2,1)S(1)} custom-call(s32[2]{0:T(128)S(1)} %pad_add_fusion.flags, f32[2,10,88,128]{3,2,1,0:T(8,128)S(1)} %get-tuple-element.95.pad, bf16[4,80,256]{2,1,0:T(8,128)(2,1)S(1)} %get-tuple-element.76.du1.du, f32[320,128]{1,0:T(8,128)S(1)} %broadcast_in_dim.83.own, f32[16,256]{1,0:T(8,128)S(1)} %get-tuple-element.96.sums), custom_call_target="tpu_custom_call" | custom-call | flops 20000000000 | bytes 4194304 | tf_op jit(solution)/shard_map/tap_grads_1/pallas_call | solution.py:499
  58.8 2.8 %collective-permute-start.18 = (bf16[3,88,256]{2,1,0:T(8,128)(2,1)S(1)}, bf16[3,88,256]{2,1,0:T(8,128)(2,1)S(1)}, u32[]{:S(2)}, u32[]{:S(2)}) collective-permute-start(bf16[3,88,256]{2,1,0:T(8,128)(2,1)S(1)} %get-tuple-element.100), channel_id=1, source_target_pairs={{4,8},{8,4},{5,9},{9,5},{6,10},{10,6},{7,11},{11,7},{20,24},{24,20... | collective-permute-start | bytes 405512 | tf_op jit(solution)/shard_map/ppermute | solution.py:543
  61.6 3.5 %collective-permute-done.18.du_b = bf16[3,88,256]{2,1,0:T(8,128)(2,1)S(1)} collective-permute-done((bf16[3,88,256]{2,1,0:T(8,128)(2,1)S(1)}, bf16[3,88,256]{2,1,0:T(8,128)(2,1)S(1)}, u32[]{:S(2)}, u32[]{:S(2)}) %collective-permute-start.18) | collective-permute-done | bytes 135200 | tf_op jit(solution)/shard_map/ppermute | solution.py:543
  65.5 5.2 %collective-permute-done.19 = bf16[2,256,256]{2,1,0:T(8,128)(2,1)S(1)} collective-permute-done((bf16[2,256,256]{2,1,0:T(8,128)(2,1)S(1)}, bf16[2,256,256]{2,1,0:T(8,128)(2,1)S(1)}, u32[]{:S(2)}, u32[]{:S(2)}) %collective-permute-start.19) | collective-permute-done | bytes 262176 | tf_op jit(solution)/shard_map/ppermute | solution.py:667
  70.8 1.7 %collective-permute-start.20 = (bf16[2,128,256]{2,1,0:T(8,128)(2,1)S(1)}, bf16[2,128,256]{2,1,0:T(8,128)(2,1)S(1)}, u32[]{:S(2)}, u32[]{:S(2)}) collective-permute-start(bf16[2,128,256]{2,1,0:T(8,128)(2,1)S(1)} %broadcast_select_fusion.8), channel_id=1, source_target_pairs={{0,2},{1,3},{2,0},{3,1},{4,6},{5,7},{6,4},{7,5},{8,10},{9,11},{10,... | collective-permute-start | bytes 393224 | tf_op jit(solution)/shard_map/ppermute | solution.py:667
  72.5 1.6 %input_grad.1 = bf16[4,68,256]{2,1,0:T(8,128)(2,1)S(1)} custom-call(s32[2]{0:T(128)S(1)} %pad_add_fusion.flags, bf16[4,88,256]{2,1,0:T(8,128)(2,1)S(1)} %get-tuple-element.89.du, bf16[3,88,256]{2,1,0:T(8,128)(2,1)S(1)} %collective-permute-done.17.du_a, bf16[3,88,256]{2,1,0:T(8,128)(2,1)S(1)} %collective-permute-done.18.du_b, ...), custom_call_target="tpu_custom_call" | custom-call | flops 20000000000 | bytes 4194304 | tf_op jit(solution)/shard_map/input_grad/pallas_call | solution.py:499
  74.1 5.7 %collective-permute-done.20 = bf16[2,128,256]{2,1,0:T(8,128)(2,1)S(1)} collective-permute-done((bf16[2,128,256]{2,1,0:T(8,128)(2,1)S(1)}, bf16[2,128,256]{2,1,0:T(8,128)(2,1)S(1)}, u32[]{:S(2)}, u32[]{:S(2)}) %collective-permute-start.20) | collective-permute-done | bytes 131104 | tf_op jit(solution)/shard_map/ppermute | solution.py:667
  80.2 3.2 %collective-permute-done.21 = bf16[192,256]{1,0:T(8,128)(2,1)S(1)} collective-permute-done((bf16[192,256]{1,0:T(8,128)(2,1)S(1)}, bf16[192,256]{1,0:T(8,128)(2,1)S(1)}, u32[]{:S(2)}, u32[]{:S(2)}) %collective-permute-start.21) | collective-permute-done | bytes 98336 | tf_op jit(solution)/shard_map/ppermute | solution.py:535
  83.9 5.1 %collective-permute-done.22 = bf16[192,256]{1,0:T(8,128)(2,1)S(1)} collective-permute-done((bf16[192,256]{1,0:T(8,128)(2,1)S(1)}, bf16[192,256]{1,0:T(8,128)(2,1)S(1)}, u32[]{:S(2)}, u32[]{:S(2)}) %collective-permute-start.22) | collective-permute-done | bytes 98336 | tf_op jit(solution)/shard_map/ppermute | solution.py:667
  89.2 4.1 %collective-permute-done.23 = bf16[320,256]{1,0:T(8,128)(2,1)S(1)} collective-permute-done((bf16[320,256]{1,0:T(8,128)(2,1)S(1)}, bf16[320,256]{1,0:T(8,128)(2,1)S(1)}, u32[]{:S(2)}, u32[]{:S(2)}) %collective-permute-start.23) | collective-permute-done | bytes 163872 | tf_op jit(solution)/shard_map/ppermute | solution.py:667
  94.0 6.0 %collective-permute-done.25 = bf16[576,256]{1,0:T(8,128)(2,1)S(1)} collective-permute-done((bf16[576,256]{1,0:T(8,128)(2,1)S(1)}, bf16[576,256]{1,0:T(8,128)(2,1)S(1)}, u32[]{:S(2)}, u32[]{:S(2)}) %collective-permute-start.25) | collective-permute-done | bytes 294944 | tf_op jit(solution)/shard_map/ppermute | solution.py:667
  100.3 5.4 %collective-permute-start.26 = (bf16[1088,256]{1,0:T(8,128)(2,1)S(1)}, bf16[1088,256]{1,0:T(8,128)(2,1)S(1)}, u32[]{:S(2)}, u32[]{:S(2)}) collective-permute-start(bf16[1088,256]{1,0:T(8,128)(2,1)S(1)} %pad_maximum_fusion), channel_id=1, source_target_pairs={{0,4},{4,0},{8,12},{12,8},{1,5},{5,1},{9,13},{13,9},{2,6},{6,2},{1... | collective-permute-start | bytes 1671176 | tf_op jit(solution)/shard_map/ppermute | solution.py:538
  106.5 1.6 %finish_own.1 = (f32[1,256,1024]{2,1,0:T(8,128)}, f32[1,1024,256]{2,1,0:T(8,128)}) custom-call(s32[2]{0:T(128)S(1)} %pad_add_fusion.flags, bf16[1024,256]{1,0:T(8,128)(2,1)S(1)} %maximum_select_fusion.piece), custom_call_target="tpu_custom_call" | custom-call | flops 10000000 | bytes 4194304 | tf_op jit(solution)/shard_map/finish_own/pallas_call | solution.py:499
  108.1 2.2 %finish_got.1 = (f32[1,256,1024]{2,1,0:T(8,128)}, f32[1,1024,256]{2,1,0:T(8,128)}, f32[49,1,256]{2,1,0:T(1,128)}, f32[5,1,256]{2,1,0:T(1,128)}, f32[1,1024]{1,0:T(1,128)}) custom-call(s32[2]{0:T(128)S(1)} %pad_add_fusion.flags, bf16[64,256]{1,0:T(8,128)(2,1)S(1)} %add_convert_fusion.6.small, ...), custom_call_target="tpu_custom_call", output_to_operand_aliasing={{0}: (3, {}), {1}: (4, {})} | custom-call | flops 10000000 | bytes 4194304 | tf_op jit(solution)/shard_map/finish_got/pallas_call | solution.py:499
  (128 shorter events, 10.5 us)
Async XLA Ops:
  0.6 2.2 %copy-start.4 = (bf16[1,1024]{1,0:T(2,128)(2,1)S(1)}, bf16[1,1024]{1,0:T(2,128)(2,1)}, u32[]{:S(2)}) copy-start(bf16[1,1024]{1,0:T(2,128)(2,1)} %param.14) | copy-start | bytes 6148
  0.6 2.3 %copy-start.2 = (bf16[1,49,256]{2,1,0:T(8,128)(2,1)S(1)}, bf16[1,49,256]{2,1,0:T(8,128)(2,1)}, u32[]{:S(2)}) copy-start(bf16[1,49,256]{2,1,0:T(8,128)(2,1)} %param.11) | copy-start | bytes 75268
  0.7 2.3 %copy-start.3 = (bf16[1,5,256]{2,1,0:T(8,128)(2,1)S(1)}, bf16[1,5,256]{2,1,0:T(8,128)(2,1)}, u32[]{:S(2)}) copy-start(bf16[1,5,256]{2,1,0:T(8,128)(2,1)} %param.12) | copy-start | bytes 7684
  0.7 7.8 %copy-start = (bf16[1,256,1024]{2,1,0:T(8,128)(2,1)S(1)}, bf16[1,256,1024]{2,1,0:T(8,128)(2,1)}, u32[]{:S(2)}) copy-start(bf16[1,256,1024]{2,1,0:T(8,128)(2,1)} %param.13) | copy-start | bytes 1572868
  1.5 7.0 %copy-start.1 = (bf16[1,1024,256]{2,1,0:T(8,128)(2,1)S(1)}, bf16[1,1024,256]{2,1,0:T(8,128)(2,1)}, u32[]{:S(2)}) copy-start(bf16[1,1024,256]{2,1,0:T(8,128)(2,1)} %param.15) | copy-start | bytes 1572868
  3.0 5.8 %collective-permute-start = (bf16[64,256]{1,0:T(8,128)(2,1)S(1)}, bf16[64,256]{1,0:T(8,128)(2,1)S(1)}, u32[]{:S(2)}, u32[]{:S(2)}) collective-permute-start(bf16[64,256]{1,0:T(8,128)(2,1)S(1)} %maximum_maximum_fusion.1), channel_id=1, source_target_pairs={{0,16},{16,0},{1,17},{17,1},{2,18},{18,2},{3,19},{19,3},{4,20},{20... | collective-permute-start | bytes 98312 | tf_op jit(solution)/shard_map/ppermute | solution.py:535
  5.1 5.2 %collective-permute-start.1 = (bf16[4,19,256]{2,1,0:T(8,128)(2,1)S(1)}, bf16[4,19,256]{2,1,0:T(8,128)(2,1)S(1)}, u32[]{:S(2)}, u32[]{:S(2)}) collective-permute-start(bf16[4,19,256]{2,1,0:T(8,128)(2,1)S(1)} %pad_maximum_fusion.6), channel_id=1, source_target_pairs={{0,1},{1,2},{2,3},{3,0},{4,5},{5,6},{6,7},{7,4},{8,9},{9,10},{10,1... | collective-permute-start | bytes 116744 | tf_op jit(solution)/shard_map/ppermute | solution.py:564
  6.4 4.0 %collective-permute-start.2 = (bf16[4,19,256]{2,1,0:T(8,128)(2,1)S(1)}, bf16[4,19,256]{2,1,0:T(8,128)(2,1)S(1)}, u32[]{:S(2)}, u32[]{:S(2)}) collective-permute-start(bf16[4,19,256]{2,1,0:T(8,128)(2,1)S(1)} %pad_maximum_fusion.7), channel_id=1, source_target_pairs={{1,0},{2,1},{3,2},{0,3},{5,4},{6,5},{7,6},{4,7},{9,8},{10,9},{11,1... | collective-permute-start | bytes 116744 | tf_op jit(solution)/shard_map/ppermute | solution.py:565
  8.8 14.6 %collective-permute-start.3 = (bf16[128,1024]{1,0:T(8,128)(2,1)S(1)}, bf16[128,1024]{1,0:T(8,128)(2,1)S(1)}, u32[]{:S(2)}, u32[]{:S(2)}) collective-permute-start(bf16[128,1024]{1,0:T(8,128)(2,1)S(1)} %select_bitcast_fusion.1), channel_id=1, source_target_pairs={{0,16},{16,0},{1,17},{17,1},{2,18},{18,2},{3,19},{19,3},{4,20},{20... | collective-permute-start | bytes 786440 | tf_op jit(solution)/shard_map/ppermute | solution.py:535
  9.1 14.4 %collective-permute-start.4 = (bf16[512,256]{1,0:T(8,128)(2,1)S(1)}, bf16[512,256]{1,0:T(8,128)(2,1)S(1)}, u32[]{:S(2)}, u32[]{:S(2)}) collective-permute-start(bf16[512,256]{1,0:T(8,128)(2,1)S(1)} %select_bitcast_fusion), channel_id=1, source_target_pairs={{0,16},{16,0},{1,17},{17,1},{2,18},{18,2},{3,19},{19,3},{4,20},{20... | collective-permute-start | bytes 786440 | tf_op jit(solution)/shard_map/ppermute | solution.py:535
  10.6 8.2 %collective-permute-start.6 = (bf16[3,96,256]{2,1,0:T(8,128)(2,1)S(1)}, bf16[3,96,256]{2,1,0:T(8,128)(2,1)S(1)}, u32[]{:S(2)}, u32[]{:S(2)}) collective-permute-start(bf16[3,96,256]{2,1,0:T(8,128)(2,1)S(1)} %get-tuple-element.138), channel_id=1, source_target_pairs={{4,8},{8,4},{5,9},{9,5},{6,10},{10,6},{7,11},{11,7},{20,24},{24,20... | collective-permute-start | bytes 442376 | tf_op jit(solution)/shard_map/ppermute | solution.py:543
  15.8 3.0 %collective-permute-start.5 = (bf16[3,96,256]{2,1,0:T(8,128)(2,1)S(1)}, bf16[3,96,256]{2,1,0:T(8,128)(2,1)S(1)}, u32[]{:S(2)}, u32[]{:S(2)}) collective-permute-start(bf16[3,96,256]{2,1,0:T(8,128)(2,1)S(1)} %get-tuple-element.139), channel_id=1, source_target_pairs={{0,4},{4,0},{8,12},{12,8},{1,5},{5,1},{9,13},{13,9},{2,6},{6,2},{1... | collective-permute-start | bytes 442376 | tf_op jit(solution)/shard_map/ppermute | solution.py:538
  23.5 1.6 %collective-permute-start.7 = (bf16[128,1024]{1,0:T(8,128)(2,1)S(1)}, bf16[128,1024]{1,0:T(8,128)(2,1)S(1)}, u32[]{:S(2)}, u32[]{:S(2)}) collective-permute-start(bf16[128,1024]{1,0:T(8,128)(2,1)S(1)} %collective-permute-done.3.refs_2_), channel_id=1, source_target_pairs={{0,4},{4,0},{8,12},{12,8},{1,5},{5,1},{9,13},{13,9},{2,6},{6,2},{1... | collective-permute-start | bytes 786440 | tf_op jit(solution)/shard_map/ppermute | solution.py:538
  23.5 1.9 %collective-permute-start.8 = (bf16[512,256]{1,0:T(8,128)(2,1)S(1)}, bf16[512,256]{1,0:T(8,128)(2,1)S(1)}, u32[]{:S(2)}, u32[]{:S(2)}) collective-permute-start(bf16[512,256]{1,0:T(8,128)(2,1)S(1)} %collective-permute-done.4.refs_3_), channel_id=1, source_target_pairs={{0,4},{4,0},{8,12},{12,8},{1,5},{5,1},{9,13},{13,9},{2,6},{6,2},{1... | collective-permute-start | bytes 786440 | tf_op jit(solution)/shard_map/ppermute | solution.py:538
  28.0 6.4 %collective-permute-start.10 = (bf16[3,88,256]{2,1,0:T(8,128)(2,1)S(1)}, bf16[3,88,256]{2,1,0:T(8,128)(2,1)}, u32[]{:S(2)}, u32[]{:S(2)}) collective-permute-start(bf16[3,88,256]{2,1,0:T(8,128)(2,1)S(1)} %get-tuple-element.75), channel_id=1, source_target_pairs={{4,8},{8,4},{5,9},{9,5},{6,10},{10,6},{7,11},{11,7},{20,24},{24,20... | collective-permute-start | bytes 405512 | tf_op jit(solution)/shard_map/ppermute | solution.py:543
  31.5 3.8 %collective-permute-start.9 = (bf16[3,88,256]{2,1,0:T(8,128)(2,1)S(1)}, bf16[3,88,256]{2,1,0:T(8,128)(2,1)S(1)}, u32[]{:S(2)}, u32[]{:S(2)}) collective-permute-start(bf16[3,88,256]{2,1,0:T(8,128)(2,1)S(1)} %get-tuple-element.74), channel_id=1, source_target_pairs={{0,4},{4,0},{8,12},{12,8},{1,5},{5,1},{9,13},{13,9},{2,6},{6,2},{1... | collective-permute-start | bytes 405512 | tf_op jit(solution)/shard_map/ppermute | solution.py:538
  41.1 6.2 %collective-permute-start.11 = (bf16[3,80,256]{2,1,0:T(8,128)(2,1)S(1)}, bf16[3,80,256]{2,1,0:T(8,128)(2,1)S(1)}, u32[]{:S(2)}, u32[]{:S(2)}) collective-permute-start(bf16[3,80,256]{2,1,0:T(8,128)(2,1)S(1)} %get-tuple-element.78), channel_id=1, source_target_pairs={{0,4},{4,0},{8,12},{12,8},{1,5},{5,1},{9,13},{13,9},{2,6},{6,2},{1... | collective-permute-start | bytes 368648 | tf_op jit(solution)/shard_map/ppermute | solution.py:538
  41.2 6.3 %collective-permute-start.12 = (bf16[3,80,256]{2,1,0:T(8,128)(2,1)S(1)}, bf16[3,80,256]{2,1,0:T(8,128)(2,1)S(1)}, u32[]{:S(2)}, u32[]{:S(2)}) collective-permute-start(bf16[3,80,256]{2,1,0:T(8,128)(2,1)S(1)} %get-tuple-element.80), channel_id=1, source_target_pairs={{4,8},{8,4},{5,9},{9,5},{6,10},{10,6},{7,11},{11,7},{20,24},{24,20... | collective-permute-start | bytes 368648 | tf_op jit(solution)/shard_map/ppermute | solution.py:543
  47.4 7.1 %collective-permute-start.15 = (bf16[1024,256]{1,0:T(8,128)(2,1)S(1)}, bf16[1024,256]{1,0:T(8,128)(2,1)S(1)}, u32[]{:S(2)}, u32[]{:S(2)}) collective-permute-start(bf16[1024,256]{1,0:T(8,128)(2,1)S(1)} %get-tuple-element.94), channel_id=1, source_target_pairs={{0,4},{4,0},{8,12},{12,8},{1,5},{5,1},{9,13},{13,9},{2,6},{6,2},{1... | collective-permute-start | bytes 1572872 | tf_op jit(solution)/shard_map/ppermute | solution.py:538
  52.1 3.4 %collective-permute-start.13 = (bf16[1024,256]{1,0:T(8,128)(2,1)S(1)}, bf16[1024,256]{1,0:T(8,128)(2,1)S(1)}, u32[]{:S(2)}, u32[]{:S(2)}) collective-permute-start(bf16[1024,256]{1,0:T(8,128)(2,1)S(1)} %get-tuple-element.88), channel_id=1, source_target_pairs={{0,4},{4,0},{8,12},{12,8},{1,5},{5,1},{9,13},{13,9},{2,6},{6,2},{1... | collective-permute-start | bytes 1572872 | tf_op jit(solution)/shard_map/ppermute | solution.py:538
  54.7 10.5 %collective-permute-start.16 = (bf16[512,256]{1,0:T(8,128)(2,1)S(1)}, bf16[512,256]{1,0:T(8,128)(2,1)S(1)}, u32[]{:S(2)}, u32[]{:S(2)}) collective-permute-start(bf16[512,256]{1,0:T(8,128)(2,1)S(1)} %broadcast_select_fusion), channel_id=1, source_target_pairs={{0,8},{1,9},{2,10},{3,11},{4,5},{5,4},{6,7},{7,6},{8,0},{9,1},{10,... | collective-permute-start | bytes 786440 | tf_op jit(solution)/shard_map/ppermute | solution.py:667
  55.6 9.5 %collective-permute-start.14 = (bf16[512,256]{1,0:T(8,128)(2,1)S(1)}, bf16[512,256]{1,0:T(8,128)(2,1)S(1)}, u32[]{:S(2)}, u32[]{:S(2)}) collective-permute-start(bf16[512,256]{1,0:T(8,128)(2,1)S(1)} %broadcast_select_fusion.1), channel_id=1, source_target_pairs={{0,8},{1,9},{2,10},{3,11},{4,5},{5,4},{6,7},{7,6},{8,0},{9,1},{10,... | collective-permute-start | bytes 786440 | tf_op jit(solution)/shard_map/ppermute | solution.py:667
  58.2 3.5 %collective-permute-start.17 = (bf16[3,88,256]{2,1,0:T(8,128)(2,1)S(1)}, bf16[3,88,256]{2,1,0:T(8,128)(2,1)S(1)}, u32[]{:S(2)}, u32[]{:S(2)}) collective-permute-start(bf16[3,88,256]{2,1,0:T(8,128)(2,1)S(1)} %get-tuple-element.99), channel_id=1, source_target_pairs={{0,4},{4,0},{8,12},{12,8},{1,5},{5,1},{9,13},{13,9},{2,6},{6,2},{1... | collective-permute-start | bytes 405512 | tf_op jit(solution)/shard_map/ppermute | solution.py:538
  58.8 6.3 %collective-permute-start.18 = (bf16[3,88,256]{2,1,0:T(8,128)(2,1)S(1)}, bf16[3,88,256]{2,1,0:T(8,128)(2,1)S(1)}, u32[]{:S(2)}, u32[]{:S(2)}) collective-permute-start(bf16[3,88,256]{2,1,0:T(8,128)(2,1)S(1)} %get-tuple-element.100), channel_id=1, source_target_pairs={{4,8},{8,4},{5,9},{9,5},{6,10},{10,6},{7,11},{11,7},{20,24},{24,20... | collective-permute-start | bytes 405512 | tf_op jit(solution)/shard_map/ppermute | solution.py:543
  65.4 5.3 %collective-permute-start.19 = (bf16[2,256,256]{2,1,0:T(8,128)(2,1)S(1)}, bf16[2,256,256]{2,1,0:T(8,128)(2,1)S(1)}, u32[]{:S(2)}, u32[]{:S(2)}) collective-permute-start(bf16[2,256,256]{2,1,0:T(8,128)(2,1)S(1)} %broadcast_select_fusion.2), channel_id=1, source_target_pairs={{0,1},{1,0},{2,3},{3,2},{4,12},{5,13},{6,14},{7,15},{8,9},{9,8},{1... | collective-permute-start | bytes 786440 | tf_op jit(solution)/shard_map/ppermute | solution.py:667
  70.8 9.0 %collective-permute-start.20 = (bf16[2,128,256]{2,1,0:T(8,128)(2,1)S(1)}, bf16[2,128,256]{2,1,0:T(8,128)(2,1)S(1)}, u32[]{:S(2)}, u32[]{:S(2)}) collective-permute-start(bf16[2,128,256]{2,1,0:T(8,128)(2,1)S(1)} %broadcast_select_fusion.8), channel_id=1, source_target_pairs={{0,2},{1,3},{2,0},{3,1},{4,6},{5,7},{6,4},{7,5},{8,10},{9,11},{10,... | collective-permute-start | bytes 393224 | tf_op jit(solution)/shard_map/ppermute | solution.py:667
  79.9 3.5 %collective-permute-start.21 = (bf16[192,256]{1,0:T(8,128)(2,1)S(1)}, bf16[192,256]{1,0:T(8,128)(2,1)S(1)}, u32[]{:S(2)}, u32[]{:S(2)}) collective-permute-start(bf16[192,256]{1,0:T(8,128)(2,1)S(1)} %pad_maximum_fusion.4), channel_id=1, source_target_pairs={{0,16},{16,0},{1,17},{17,1},{2,18},{18,2},{3,19},{19,3},{4,20},{20... | collective-permute-start | bytes 294920 | tf_op jit(solution)/shard_map/ppermute | solution.py:535
  83.5 5.5 %collective-permute-start.22 = (bf16[192,256]{1,0:T(8,128)(2,1)S(1)}, bf16[192,256]{1,0:T(8,128)(2,1)S(1)}, u32[]{:S(2)}, u32[]{:S(2)}) collective-permute-start(bf16[192,256]{1,0:T(8,128)(2,1)S(1)} %pad_maximum_fusion.5), channel_id=1, source_target_pairs={{0,2},{1,3},{2,0},{3,1},{4,6},{5,7},{6,4},{7,5},{8,10},{9,11},{10,... | collective-permute-start | bytes 294920 | tf_op jit(solution)/shard_map/ppermute | solution.py:667
  83.6 5.5 %collective-permute-start.24 = (bf16[4,68,256]{2,1,0:T(8,128)(2,1)S(1)}, bf16[4,68,256]{2,1,0:T(8,128)(2,1)S(1)}, u32[]{:S(2)}, u32[]{:S(2)}) collective-permute-start(bf16[4,68,256]{2,1,0:T(8,128)(2,1)S(1)} %broadcast_select_fusion.3), channel_id=1, source_target_pairs={{0,16},{16,0},{1,17},{17,1},{2,18},{18,2},{3,19},{19,3},{4,20},{20... | collective-permute-start | bytes 417800 | tf_op jit(solution)/shard_map/ppermute | solution.py:535
  89.1 4.2 %collective-permute-start.23 = (bf16[320,256]{1,0:T(8,128)(2,1)S(1)}, bf16[320,256]{1,0:T(8,128)(2,1)S(1)}, u32[]{:S(2)}, u32[]{:S(2)}) collective-permute-start(bf16[320,256]{1,0:T(8,128)(2,1)S(1)} %pad_maximum_fusion.3), channel_id=1, source_target_pairs={{0,1},{1,0},{2,3},{3,2},{4,12},{5,13},{6,14},{7,15},{8,9},{9,8},{1... | collective-permute-start | bytes 491528 | tf_op jit(solution)/shard_map/ppermute | solution.py:667
  93.5 6.5 %collective-permute-start.25 = (bf16[576,256]{1,0:T(8,128)(2,1)S(1)}, bf16[576,256]{1,0:T(8,128)(2,1)S(1)}, u32[]{:S(2)}, u32[]{:S(2)}) collective-permute-start(bf16[576,256]{1,0:T(8,128)(2,1)S(1)} %pad_maximum_fusion.1), channel_id=1, source_target_pairs={{0,8},{1,9},{2,10},{3,11},{4,5},{5,4},{6,7},{7,6},{8,0},{9,1},{10,... | collective-permute-start | bytes 884744 | tf_op jit(solution)/shard_map/ppermute | solution.py:667
  100.3 7.8 %collective-permute-start.26 = (bf16[1088,256]{1,0:T(8,128)(2,1)S(1)}, bf16[1088,256]{1,0:T(8,128)(2,1)S(1)}, u32[]{:S(2)}, u32[]{:S(2)}) collective-permute-start(bf16[1088,256]{1,0:T(8,128)(2,1)S(1)} %pad_maximum_fusion), channel_id=1, source_target_pairs={{0,4},{4,0},{8,12},{12,8},{1,5},{5,1},{9,13},{13,9},{2,6},{6,2},{1... | collective-permute-start | bytes 1671176 | tf_op jit(solution)/shard_map/ppermute | solution.py:538

commit v6 on v5

--- a/solution.py
+++ b/solution.py
@@ -137,7 +137,7 @@
     chunks(count, scaled, 0)
 
 
-def forward_mlp(width, small, mask, w_up, w_down, z, base, hidden, active, slope, branch, out):
+def forward_mlp(width, small, mask, w_up, w_down, z, base, hidden, active, slope, branch, out, before_down=None):
     count = ROWS_DEV * width
     for quarter in range(QUARTERS):
         cols = slice(quarter * WIDE, (quarter + 1) * WIDE)
@@ -157,6 +157,8 @@
             return carry
 
         chunks(count, gelu, 0)
+    if before_down:
+        before_down()
     branch[...] = dot(active[...], w_down[...]) + small[TAPS + 3 : TAPS + 4, :]
     if out is None:
         return
@@ -238,18 +240,20 @@
         weights(send, keep)
 
 
-def weight_copies(block, flags, parts, w_up, w_down, sems, act):
+def weight_copies(block, flags, parts, w_up, w_down, sems, act, which=(0, 1)):
     odd, section = flags[0], flags[1]
     own_up, own_down, got_up, got_down, other_up, other_down = parts
 
     @pl.when(section == block)
     def _():
-        act(pltpu.make_async_copy(own_up, w_up, sems.at[0]))
-        act(pltpu.make_async_copy(own_down, w_down, sems.at[1]))
+        for index in which:
+            act(pltpu.make_async_copy((own_up, own_down)[index], (w_up, w_down)[index], sems.at[index]))
 
     @pl.when(section != block)
     def _():
         for index, (ref, mine, other) in enumerate(((w_up, got_up, other_up), (w_down, got_down, other_down))):
+            if index not in which:
+                continue
             half = mine.shape[0]
             for place, part in enumerate((mine, other)):
                 first = odd if place == 0 else 1 - odd
@@ -314,8 +318,12 @@
     for copy in copies:
         copy.wait()
     scale_cells(N_0, small, normed, z)
-    weight_copies(0, flags, parts, w_up, w_down, weight_sems, wait_copy)
-    forward_mlp(W_0, small, mask, w_up, w_down, z, base, hidden, active, slope, branch, out)
+    weight_copies(0, flags, parts, w_up, w_down, weight_sems, wait_copy, (0,))
+
+    def down_ready():
+        weight_copies(0, flags, parts, w_up, w_down, weight_sems, wait_copy, (1,))
+
+    forward_mlp(W_0, small, mask, w_up, w_down, z, base, hidden, active, slope, branch, out, down_ready)
     write_rows(out, W_0, y)
     send_rows(flags[0], y, send_a, send_b)
 
@@ -328,8 +336,12 @@
     weight_copies(0, flags, parts, w_up, w_down, weight_sems, start_copy)
     copy.wait()
     scale_cells(N_0, small, normed, z)
-    weight_copies(0, flags, parts, w_up, w_down, weight_sems, wait_copy)
-    forward_mlp(W_0, small, None, w_up, w_down, z, None, hidden, active, slope, branch, None)
+    weight_copies(0, flags, parts, w_up, w_down, weight_sems, wait_copy, (0,))
+
+    def down_ready():
+        weight_copies(0, flags, parts, w_up, w_down, weight_sems, wait_copy, (1,))
+
+    forward_mlp(W_0, small, None, w_up, w_down, z, None, hidden, active, slope, branch, None, down_ready)
 
 
 def second_block(flags, y, y_a, y_b, small, mask, own, own_row, kept, *refs):

time: 111 us -> 112 us (level)
  no operation moved by 1% of the time
where the time goes in v6:
time: 112 us; the launch traced here: 111 us
  waiting for transfers between devices  40 us (36%)
  starting transfers between devices  33.1 us (30%)
  Pallas kernels  29.6 us (26%)
  other arithmetic  3.86 us (3%)
  local copies, waits for them, and re-layouts  3.2 us (3%)
  between operations  1.52 us (1%)
    pallas_call x10, Pallas kernels, call(): pl.pallas_call(body, name=name, out_shape=[jax.ShapeDtypeStruct(shape, dt...  29.6 us
    ppermute x7, waiting for transfers between devices, exchange(): return lax.ppermute(value, ('lat', 'lon'), pairs)  25.9 us
    ppermute x4, starting transfers between devices, lat_halo(): got_b = lax.ppermute(send_b, 'lat', pairs)  14.2 us
    ppermute x4, waiting for transfers between devices, lat_halo(): got_b = lax.ppermute(send_b, 'lat', pairs)  9.7 us
    ppermute x9, starting transfers between devices, over_core(): return lax.ppermute(value, 'lat', swap_pairs(n_lat, 1))  7.3 us
    ppermute x5, starting transfers between devices, over_section(): return lax.ppermute(value, 'section', [(0, 1), (1, 0)])  4.21 us
    ppermute x7, starting transfers between devices, exchange(): return lax.ppermute(value, ('lat', 'lon'), pairs)  4.01 us
    ppermute x5, waiting for transfers between devices, over_section(): return lax.ppermute(value, 'section', [(0, 1), (1, 0)])  3.22 us
  transfers between devices with their start and end apart: 27, of which 11 were waited for; matrix products, arithmetic and copies ran while one was open for 3% of the time, Pallas kernels for 17%

profile of v6, /device:TPU:1, one launch (start us, length us, event | category | flops | bytes accessed | tf_op | source)
XLA Modules:
  0.0 111.3 jit_solution(7490212132209464794)
XLA Ops:
  1.5 1.1 %constant_dynamic-slice_fusion = (bf16[1,4,68,256]{3,1,2,0:T(4,128)(2,1)S(1)}, bf16[1,4,68,256]{3,1,2,0:T(4,128)(2,1)S(1)}) fusion(bf16[2,4,68,256]{3,1,2,0:T(4,128)(2,1)} %param.9, s32[]{:T(128)S(6)} %select_n.260, bf16[2,4,68,256]{3,1,2,0:T(4,128)(2,1)} %param.8), kind=kLoop, calls=%fused_computation.60 | loop fusion | bytes 557060 | tf_op jit(solution)/shard_map/jit(dynamic_index_in_dim)/dynamic_slice | solution.py:565
  3.0 2.1 %collective-permute-start = (bf16[64,256]{1,0:T(8,128)(2,1)S(1)}, bf16[64,256]{1,0:T(8,128)(2,1)S(1)}, u32[]{:S(2)}, u32[]{:S(2)}) collective-permute-start(bf16[64,256]{1,0:T(8,128)(2,1)S(1)} %maximum_maximum_fusion.1), channel_id=1, source_target_pairs={{0,16},{16,0},{1,17},{17,1},{2,18},{18,2},{3,19},{19,3},{4,20},{20... | collective-permute-start | bytes 98312 | tf_op jit(solution)/shard_map/ppermute | solution.py:547
  5.1 1.3 %collective-permute-start.1 = (bf16[4,19,256]{2,1,0:T(8,128)(2,1)S(1)}, bf16[4,19,256]{2,1,0:T(8,128)(2,1)S(1)}, u32[]{:S(2)}, u32[]{:S(2)}) collective-permute-start(bf16[4,19,256]{2,1,0:T(8,128)(2,1)S(1)} %pad_maximum_fusion.6), channel_id=1, source_target_pairs={{0,1},{1,2},{2,3},{3,0},{4,5},{5,6},{6,7},{7,4},{8,9},{9,10},{10,1... | collective-permute-start | bytes 116744 | tf_op jit(solution)/shard_map/ppermute | solution.py:576
  6.4 2.0 %collective-permute-start.2 = (bf16[4,19,256]{2,1,0:T(8,128)(2,1)S(1)}, bf16[4,19,256]{2,1,0:T(8,128)(2,1)S(1)}, u32[]{:S(2)}, u32[]{:S(2)}) collective-permute-start(bf16[4,19,256]{2,1,0:T(8,128)(2,1)S(1)} %pad_maximum_fusion.7), channel_id=1, source_target_pairs={{1,0},{2,1},{3,2},{0,3},{5,4},{6,5},{7,6},{4,7},{9,8},{10,9},{11,1... | collective-permute-start | bytes 116744 | tf_op jit(solution)/shard_map/ppermute | solution.py:577
  9.1 1.2 %collective-permute-start.4 = (bf16[512,256]{1,0:T(8,128)(2,1)S(1)}, bf16[512,256]{1,0:T(8,128)(2,1)S(1)}, u32[]{:S(2)}, u32[]{:S(2)}) collective-permute-start(bf16[512,256]{1,0:T(8,128)(2,1)S(1)} %select_bitcast_fusion), channel_id=1, source_target_pairs={{0,16},{16,0},{1,17},{17,1},{2,18},{18,2},{3,19},{19,3},{4,20},{20... | collective-permute-start | bytes 786440 | tf_op jit(solution)/shard_map/ppermute | solution.py:547
  10.6 5.1 %collective-permute-start.6 = (bf16[3,96,256]{2,1,0:T(8,128)(2,1)S(1)}, bf16[3,96,256]{2,1,0:T(8,128)(2,1)S(1)}, u32[]{:S(2)}, u32[]{:S(2)}) collective-permute-start(bf16[3,96,256]{2,1,0:T(8,128)(2,1)S(1)} %get-tuple-element.138), channel_id=1, source_target_pairs={{4,8},{8,4},{5,9},{9,5},{6,10},{10,6},{7,11},{11,7},{20,24},{24,20... | collective-permute-start | bytes 442376 | tf_op jit(solution)/shard_map/ppermute | solution.py:555
  15.8 2.9 %collective-permute-done.6 = bf16[3,96,256]{2,1,0:T(8,128)(2,1)S(1)} collective-permute-done((bf16[3,96,256]{2,1,0:T(8,128)(2,1)S(1)}, bf16[3,96,256]{2,1,0:T(8,128)(2,1)S(1)}, u32[]{:S(2)}, u32[]{:S(2)}) %collective-permute-start.6) | collective-permute-done | bytes 147488 | tf_op jit(solution)/shard_map/ppermute | solution.py:555
  18.9 4.5 %first_conv.1.kept = f32[40960,256]{1,0:T(8,128)} custom-call(s32[2]{0:T(128)S(1)} %pad_add_fusion.flags, bf16[4,96,256]{2,1,0:T(8,128)(2,1)S(1)} %maximum_maximum_fusion.x.v, bf16[3,96,256]{2,1,0:T(8,128)(2,1)S(1)} %collective-permute-done.5.x_a.v_a, bf16[3,96,256]{2,1,0:T(8,128)(2,1)S(1)} %broadcast_select_fusion.4.x_b.v_b, ...), custom_call_target="tpu_custom_call" | custom-call | flops 20000000000 | bytes 4194304 | tf_op jit(solution)/shard_map/first_conv/pallas_call | solution.py:511
  25.4 3.0 %first_forward.1 = (bf16[4,88,256]{2,1,0:T(8,128)(2,1)S(1)}, bf16[3,88,256]{2,1,0:T(8,128)(2,1)S(1)}, bf16[3,88,256]{2,1,0:T(8,128)(2,1)S(1)}) custom-call(s32[2]{0:T(128)S(1)} %pad_add_fusion.flags, f32[64,256]{1,0:T(8,128)S(1)} %get-tuple-element.81.small.small0, f32[352,128]{1,0:T(8,128)S(1)} %broadcast_in_dim.75.mask, f32[40960,256]{1,0:T(8,128)} %first_conv.1.kept, ...), custom_call_target="tpu_custom_call" | custom-call | flops 20000000000 | bytes 4194304 | tf_op jit(solution)/shard_map/first_forward/pallas_call | solution.py:511
  28.4 3.4 %collective-permute-start.10 = (bf16[3,88,256]{2,1,0:T(8,128)(2,1)S(1)}, bf16[3,88,256]{2,1,0:T(8,128)(2,1)}, u32[]{:S(2)}, u32[]{:S(2)}) collective-permute-start(bf16[3,88,256]{2,1,0:T(8,128)(2,1)S(1)} %get-tuple-element.75), channel_id=1, source_target_pairs={{4,8},{8,4},{5,9},{9,5},{6,10},{10,6},{7,11},{11,7},{20,24},{24,20... | collective-permute-start | bytes 405512 | tf_op jit(solution)/shard_map/ppermute | solution.py:555
  31.9 2.9 %collective-permute-done.10 = bf16[3,88,256]{2,1,0:T(8,128)(2,1)} collective-permute-done((bf16[3,88,256]{2,1,0:T(8,128)(2,1)S(1)}, bf16[3,88,256]{2,1,0:T(8,128)(2,1)}, u32[]{:S(2)}, u32[]{:S(2)}) %collective-permute-start.10) | collective-permute-done | bytes 135200 | tf_op jit(solution)/shard_map/ppermute | solution.py:555
  34.8 0.9 broadcast_select_fusion.7.y_b
  36.0 5.6 %second_block.1 = (bf16[4,68,256]{2,1,0:T(8,128)(2,1)S(1)}, bf16[4,80,256]{2,1,0:T(8,128)(2,1)S(1)}, bf16[3,80,256]{2,1,0:T(8,128)(2,1)S(1)}, bf16[3,80,256]{2,1...) custom-call(s32[2]{0:T(128)S(1)} %pad_add_fusion.flags, ...), custom_call_target="tpu_custom_call" | custom-call | flops 40000000000 | bytes 4194304 | tf_op jit(solution)/shard_map/second_block/pallas_call | solution.py:511
  41.6 3.4 %collective-permute-start.12 = (bf16[3,80,256]{2,1,0:T(8,128)(2,1)S(1)}, bf16[3,80,256]{2,1,0:T(8,128)(2,1)S(1)}, u32[]{:S(2)}, u32[]{:S(2)}) collective-permute-start(bf16[3,80,256]{2,1,0:T(8,128)(2,1)S(1)} %get-tuple-element.80), channel_id=1, source_target_pairs={{4,8},{8,4},{5,9},{9,5},{6,10},{10,6},{7,11},{11,7},{20,24},{24,20... | collective-permute-start | bytes 368648 | tf_op jit(solution)/shard_map/ppermute | solution.py:555
  45.0 3.1 %first_again.1 = (bf16[352,1024]{1,0:T(8,128)(2,1)S(1)}, f32[352,1024]{1,0:T(8,128)S(1)}, f32[352,256]{1,0:T(8,128)S(1)}, bf16[256,1024]{1,0:T(8,128)(2,1)S(1)}, bf16[1024,256]{1,0:T(8,128)(2,1)S(1)}) custom-call(s32[2]{0:T(128)S(1)} %pad_add_fusion.flags, f32[64,256]{1,0:T(8,128)S(1)} %get-tuple-element.81.small.small0, f32[40960,256]{1,0:T(8,128)} %first_conv.1.kept, ...), custom_call_target="tpu_custom_call" | custom-call | flops 20000000000 | bytes 4194304 | tf_op jit(solution)/shard_map/first_again/pallas_call | solution.py:511
  48.4 4.5 %first_backward.1 = (f32[4,72,256]{2,1,0:T(8,128)S(1)}, bf16[4,88,256]{2,1,0:T(8,128)(2,1)S(1)}, bf16[3,88,256]{2,1,0:T(8,128)(2,1)S(1)}, bf16[3,88,256]{2,1,0:T...) custom-call(s32[2]{0:T(128)S(1)} %pad_add_fusion.flags, ...), custom_call_target="tpu_custom_call" | custom-call | flops 30000001024 | bytes 4194304 | tf_op jit(solution)/shard_map/first_backward/pallas_call | solution.py:511
  53.4 1.8 %tap_grads_0.1 = bf16[64,256]{1,0:T(8,128)(2,1)S(1)} custom-call(s32[2]{0:T(128)S(1)} %pad_add_fusion.flags, bf16[4,96,256]{2,1,0:T(8,128)(2,1)S(1)} %maximum_maximum_fusion.x.v, bf16[3,96,256]{2,1,0:T(8,128)(2,1)S(1)} %collective-permute-done.5.x_a.v_a, bf16[3,96,256]{2,1,0:T(8,128)(2,1)S(1)} %broadcast_select_fusion.4.x_b.v_b, ...), custom_call_target="tpu_custom_call" | custom-call | flops 20000000000 | bytes 4194304 | tf_op jit(solution)/shard_map/tap_grads_0/pallas_call | solution.py:511
  56.4 0.8 collective-permute-start.14
  57.2 1.7 %tap_grads_1.1 = bf16[64,256]{1,0:T(8,128)(2,1)S(1)} custom-call(s32[2]{0:T(128)S(1)} %pad_add_fusion.flags, f32[2,10,88,128]{3,2,1,0:T(8,128)S(1)} %get-tuple-element.95.pad, bf16[4,80,256]{2,1,0:T(8,128)(2,1)S(1)} %get-tuple-element.76.du1.du, f32[320,128]{1,0:T(8,128)S(1)} %broadcast_in_dim.83.own, f32[16,256]{1,0:T(8,128)S(1)} %get-tuple-element.96.sums), custom_call_target="tpu_custom_call" | custom-call | flops 20000000000 | bytes 4194304 | tf_op jit(solution)/shard_map/tap_grads_1/pallas_call | solution.py:511
  59.6 2.4 %collective-permute-start.18 = (bf16[3,88,256]{2,1,0:T(8,128)(2,1)S(1)}, bf16[3,88,256]{2,1,0:T(8,128)(2,1)S(1)}, u32[]{:S(2)}, u32[]{:S(2)}) collective-permute-start(bf16[3,88,256]{2,1,0:T(8,128)(2,1)S(1)} %get-tuple-element.100), channel_id=1, source_target_pairs={{4,8},{8,4},{5,9},{9,5},{6,10},{10,6},{7,11},{11,7},{20,24},{24,20... | collective-permute-start | bytes 405512 | tf_op jit(solution)/shard_map/ppermute | solution.py:555
  62.1 3.8 %collective-permute-done.18.du_b = bf16[3,88,256]{2,1,0:T(8,128)(2,1)S(1)} collective-permute-done((bf16[3,88,256]{2,1,0:T(8,128)(2,1)S(1)}, bf16[3,88,256]{2,1,0:T(8,128)(2,1)S(1)}, u32[]{:S(2)}, u32[]{:S(2)}) %collective-permute-start.18) | collective-permute-done | bytes 135200 | tf_op jit(solution)/shard_map/ppermute | solution.py:555
  66.3 5.2 %collective-permute-done.19 = bf16[2,256,256]{2,1,0:T(8,128)(2,1)S(1)} collective-permute-done((bf16[2,256,256]{2,1,0:T(8,128)(2,1)S(1)}, bf16[2,256,256]{2,1,0:T(8,128)(2,1)S(1)}, u32[]{:S(2)}, u32[]{:S(2)}) %collective-permute-start.19) | collective-permute-done | bytes 262176 | tf_op jit(solution)/shard_map/ppermute | solution.py:679
  71.6 1.7 %collective-permute-start.20 = (bf16[2,128,256]{2,1,0:T(8,128)(2,1)S(1)}, bf16[2,128,256]{2,1,0:T(8,128)(2,1)S(1)}, u32[]{:S(2)}, u32[]{:S(2)}) collective-permute-start(bf16[2,128,256]{2,1,0:T(8,128)(2,1)S(1)} %broadcast_select_fusion.8), channel_id=1, source_target_pairs={{0,2},{1,3},{2,0},{3,1},{4,6},{5,7},{6,4},{7,5},{8,10},{9,11},{10,... | collective-permute-start | bytes 393224 | tf_op jit(solution)/shard_map/ppermute | solution.py:679
  73.3 1.6 %input_grad.1 = bf16[4,68,256]{2,1,0:T(8,128)(2,1)S(1)} custom-call(s32[2]{0:T(128)S(1)} %pad_add_fusion.flags, bf16[4,88,256]{2,1,0:T(8,128)(2,1)S(1)} %get-tuple-element.89.du, bf16[3,88,256]{2,1,0:T(8,128)(2,1)S(1)} %collective-permute-done.17.du_a, bf16[3,88,256]{2,1,0:T(8,128)(2,1)S(1)} %collective-permute-done.18.du_b, ...), custom_call_target="tpu_custom_call" | custom-call | flops 20000000000 | bytes 4194304 | tf_op jit(solution)/shard_map/input_grad/pallas_call | solution.py:511
  74.9 5.7 %collective-permute-done.20 = bf16[2,128,256]{2,1,0:T(8,128)(2,1)S(1)} collective-permute-done((bf16[2,128,256]{2,1,0:T(8,128)(2,1)S(1)}, bf16[2,128,256]{2,1,0:T(8,128)(2,1)S(1)}, u32[]{:S(2)}, u32[]{:S(2)}) %collective-permute-start.20) | collective-permute-done | bytes 131104 | tf_op jit(solution)/shard_map/ppermute | solution.py:679
  81.0 3.2 %collective-permute-done.21 = bf16[192,256]{1,0:T(8,128)(2,1)S(1)} collective-permute-done((bf16[192,256]{1,0:T(8,128)(2,1)S(1)}, bf16[192,256]{1,0:T(8,128)(2,1)S(1)}, u32[]{:S(2)}, u32[]{:S(2)}) %collective-permute-start.21) | collective-permute-done | bytes 98336 | tf_op jit(solution)/shard_map/ppermute | solution.py:547
  84.7 5.1 %collective-permute-done.22 = bf16[192,256]{1,0:T(8,128)(2,1)S(1)} collective-permute-done((bf16[192,256]{1,0:T(8,128)(2,1)S(1)}, bf16[192,256]{1,0:T(8,128)(2,1)S(1)}, u32[]{:S(2)}, u32[]{:S(2)}) %collective-permute-start.22) | collective-permute-done | bytes 98336 | tf_op jit(solution)/shard_map/ppermute | solution.py:679
  90.0 4.1 %collective-permute-done.23 = bf16[320,256]{1,0:T(8,128)(2,1)S(1)} collective-permute-done((bf16[320,256]{1,0:T(8,128)(2,1)S(1)}, bf16[320,256]{1,0:T(8,128)(2,1)S(1)}, u32[]{:S(2)}, u32[]{:S(2)}) %collective-permute-start.23) | collective-permute-done | bytes 163872 | tf_op jit(solution)/shard_map/ppermute | solution.py:679
  94.8 6.0 %collective-permute-done.25 = bf16[576,256]{1,0:T(8,128)(2,1)S(1)} collective-permute-done((bf16[576,256]{1,0:T(8,128)(2,1)S(1)}, bf16[576,256]{1,0:T(8,128)(2,1)S(1)}, u32[]{:S(2)}, u32[]{:S(2)}) %collective-permute-start.25) | collective-permute-done | bytes 294944 | tf_op jit(solution)/shard_map/ppermute | solution.py:679
  101.1 5.4 %collective-permute-start.26 = (bf16[1088,256]{1,0:T(8,128)(2,1)S(1)}, bf16[1088,256]{1,0:T(8,128)(2,1)S(1)}, u32[]{:S(2)}, u32[]{:S(2)}) collective-permute-start(bf16[1088,256]{1,0:T(8,128)(2,1)S(1)} %pad_maximum_fusion), channel_id=1, source_target_pairs={{0,4},{4,0},{8,12},{12,8},{1,5},{5,1},{9,13},{13,9},{2,6},{6,2},{1... | collective-permute-start | bytes 1671176 | tf_op jit(solution)/shard_map/ppermute | solution.py:550
  107.3 1.6 %finish_own.1 = (f32[1,256,1024]{2,1,0:T(8,128)}, f32[1,1024,256]{2,1,0:T(8,128)}) custom-call(s32[2]{0:T(128)S(1)} %pad_add_fusion.flags, bf16[1024,256]{1,0:T(8,128)(2,1)S(1)} %maximum_select_fusion.piece), custom_call_target="tpu_custom_call" | custom-call | flops 10000000 | bytes 4194304 | tf_op jit(solution)/shard_map/finish_own/pallas_call | solution.py:511
  108.9 2.2 %finish_got.1 = (f32[1,256,1024]{2,1,0:T(8,128)}, f32[1,1024,256]{2,1,0:T(8,128)}, f32[49,1,256]{2,1,0:T(1,128)}, f32[5,1,256]{2,1,0:T(1,128)}, f32[1,1024]{1,0:T(1,128)}) custom-call(s32[2]{0:T(128)S(1)} %pad_add_fusion.flags, bf16[64,256]{1,0:T(8,128)(2,1)S(1)} %add_convert_fusion.6.small, ...), custom_call_target="tpu_custom_call", output_to_operand_aliasing={{0}: (3, {}), {1}: (4, {})} | custom-call | flops 10000000 | bytes 4194304 | tf_op jit(solution)/shard_map/finish_got/pallas_call | solution.py:511
  (128 shorter events, 10.5 us)
Async XLA Ops:
  0.6 2.2 %copy-start.4 = (bf16[1,1024]{1,0:T(2,128)(2,1)S(1)}, bf16[1,1024]{1,0:T(2,128)(2,1)}, u32[]{:S(2)}) copy-start(bf16[1,1024]{1,0:T(2,128)(2,1)} %param.14) | copy-start | bytes 6148
  0.6 2.3 %copy-start.2 = (bf16[1,49,256]{2,1,0:T(8,128)(2,1)S(1)}, bf16[1,49,256]{2,1,0:T(8,128)(2,1)}, u32[]{:S(2)}) copy-start(bf16[1,49,256]{2,1,0:T(8,128)(2,1)} %param.11) | copy-start | bytes 75268
  0.7 2.3 %copy-start.3 = (bf16[1,5,256]{2,1,0:T(8,128)(2,1)S(1)}, bf16[1,5,256]{2,1,0:T(8,128)(2,1)}, u32[]{:S(2)}) copy-start(bf16[1,5,256]{2,1,0:T(8,128)(2,1)} %param.12) | copy-start | bytes 7684
  0.7 7.8 %copy-start = (bf16[1,256,1024]{2,1,0:T(8,128)(2,1)S(1)}, bf16[1,256,1024]{2,1,0:T(8,128)(2,1)}, u32[]{:S(2)}) copy-start(bf16[1,256,1024]{2,1,0:T(8,128)(2,1)} %param.13) | copy-start | bytes 1572868
  1.5 7.0 %copy-start.1 = (bf16[1,1024,256]{2,1,0:T(8,128)(2,1)S(1)}, bf16[1,1024,256]{2,1,0:T(8,128)(2,1)}, u32[]{:S(2)}) copy-start(bf16[1,1024,256]{2,1,0:T(8,128)(2,1)} %param.15) | copy-start | bytes 1572868
  3.0 5.8 %collective-permute-start = (bf16[64,256]{1,0:T(8,128)(2,1)S(1)}, bf16[64,256]{1,0:T(8,128)(2,1)S(1)}, u32[]{:S(2)}, u32[]{:S(2)}) collective-permute-start(bf16[64,256]{1,0:T(8,128)(2,1)S(1)} %maximum_maximum_fusion.1), channel_id=1, source_target_pairs={{0,16},{16,0},{1,17},{17,1},{2,18},{18,2},{3,19},{19,3},{4,20},{20... | collective-permute-start | bytes 98312 | tf_op jit(solution)/shard_map/ppermute | solution.py:547
  5.1 5.2 %collective-permute-start.1 = (bf16[4,19,256]{2,1,0:T(8,128)(2,1)S(1)}, bf16[4,19,256]{2,1,0:T(8,128)(2,1)S(1)}, u32[]{:S(2)}, u32[]{:S(2)}) collective-permute-start(bf16[4,19,256]{2,1,0:T(8,128)(2,1)S(1)} %pad_maximum_fusion.6), channel_id=1, source_target_pairs={{0,1},{1,2},{2,3},{3,0},{4,5},{5,6},{6,7},{7,4},{8,9},{9,10},{10,1... | collective-permute-start | bytes 116744 | tf_op jit(solution)/shard_map/ppermute | solution.py:576
  6.4 4.0 %collective-permute-start.2 = (bf16[4,19,256]{2,1,0:T(8,128)(2,1)S(1)}, bf16[4,19,256]{2,1,0:T(8,128)(2,1)S(1)}, u32[]{:S(2)}, u32[]{:S(2)}) collective-permute-start(bf16[4,19,256]{2,1,0:T(8,128)(2,1)S(1)} %pad_maximum_fusion.7), channel_id=1, source_target_pairs={{1,0},{2,1},{3,2},{0,3},{5,4},{6,5},{7,6},{4,7},{9,8},{10,9},{11,1... | collective-permute-start | bytes 116744 | tf_op jit(solution)/shard_map/ppermute | solution.py:577
  8.8 14.6 %collective-permute-start.3 = (bf16[128,1024]{1,0:T(8,128)(2,1)S(1)}, bf16[128,1024]{1,0:T(8,128)(2,1)S(1)}, u32[]{:S(2)}, u32[]{:S(2)}) collective-permute-start(bf16[128,1024]{1,0:T(8,128)(2,1)S(1)} %select_bitcast_fusion.1), channel_id=1, source_target_pairs={{0,16},{16,0},{1,17},{17,1},{2,18},{18,2},{3,19},{19,3},{4,20},{20... | collective-permute-start | bytes 786440 | tf_op jit(solution)/shard_map/ppermute | solution.py:547
  9.1 14.4 %collective-permute-start.4 = (bf16[512,256]{1,0:T(8,128)(2,1)S(1)}, bf16[512,256]{1,0:T(8,128)(2,1)S(1)}, u32[]{:S(2)}, u32[]{:S(2)}) collective-permute-start(bf16[512,256]{1,0:T(8,128)(2,1)S(1)} %select_bitcast_fusion), channel_id=1, source_target_pairs={{0,16},{16,0},{1,17},{17,1},{2,18},{18,2},{3,19},{19,3},{4,20},{20... | collective-permute-start | bytes 786440 | tf_op jit(solution)/shard_map/ppermute | solution.py:547
  10.6 8.2 %collective-permute-start.6 = (bf16[3,96,256]{2,1,0:T(8,128)(2,1)S(1)}, bf16[3,96,256]{2,1,0:T(8,128)(2,1)S(1)}, u32[]{:S(2)}, u32[]{:S(2)}) collective-permute-start(bf16[3,96,256]{2,1,0:T(8,128)(2,1)S(1)} %get-tuple-element.138), channel_id=1, source_target_pairs={{4,8},{8,4},{5,9},{9,5},{6,10},{10,6},{7,11},{11,7},{20,24},{24,20... | collective-permute-start | bytes 442376 | tf_op jit(solution)/shard_map/ppermute | solution.py:555
  15.8 3.0 %collective-permute-start.5 = (bf16[3,96,256]{2,1,0:T(8,128)(2,1)S(1)}, bf16[3,96,256]{2,1,0:T(8,128)(2,1)S(1)}, u32[]{:S(2)}, u32[]{:S(2)}) collective-permute-start(bf16[3,96,256]{2,1,0:T(8,128)(2,1)S(1)} %get-tuple-element.139), channel_id=1, source_target_pairs={{0,4},{4,0},{8,12},{12,8},{1,5},{5,1},{9,13},{13,9},{2,6},{6,2},{1... | collective-permute-start | bytes 442376 | tf_op jit(solution)/shard_map/ppermute | solution.py:550
  23.5 1.6 %collective-permute-start.7 = (bf16[128,1024]{1,0:T(8,128)(2,1)S(1)}, bf16[128,1024]{1,0:T(8,128)(2,1)S(1)}, u32[]{:S(2)}, u32[]{:S(2)}) collective-permute-start(bf16[128,1024]{1,0:T(8,128)(2,1)S(1)} %collective-permute-done.3.refs_2_), channel_id=1, source_target_pairs={{0,4},{4,0},{8,12},{12,8},{1,5},{5,1},{9,13},{13,9},{2,6},{6,2},{1... | collective-permute-start | bytes 786440 | tf_op jit(solution)/shard_map/ppermute | solution.py:550
  23.5 1.9 %collective-permute-start.8 = (bf16[512,256]{1,0:T(8,128)(2,1)S(1)}, bf16[512,256]{1,0:T(8,128)(2,1)S(1)}, u32[]{:S(2)}, u32[]{:S(2)}) collective-permute-start(bf16[512,256]{1,0:T(8,128)(2,1)S(1)} %collective-permute-done.4.refs_3_), channel_id=1, source_target_pairs={{0,4},{4,0},{8,12},{12,8},{1,5},{5,1},{9,13},{13,9},{2,6},{6,2},{1... | collective-permute-start | bytes 786440 | tf_op jit(solution)/shard_map/ppermute | solution.py:550
  28.4 6.4 %collective-permute-start.10 = (bf16[3,88,256]{2,1,0:T(8,128)(2,1)S(1)}, bf16[3,88,256]{2,1,0:T(8,128)(2,1)}, u32[]{:S(2)}, u32[]{:S(2)}) collective-permute-start(bf16[3,88,256]{2,1,0:T(8,128)(2,1)S(1)} %get-tuple-element.75), channel_id=1, source_target_pairs={{4,8},{8,4},{5,9},{9,5},{6,10},{10,6},{7,11},{11,7},{20,24},{24,20... | collective-permute-start | bytes 405512 | tf_op jit(solution)/shard_map/ppermute | solution.py:555
  31.9 3.8 %collective-permute-start.9 = (bf16[3,88,256]{2,1,0:T(8,128)(2,1)S(1)}, bf16[3,88,256]{2,1,0:T(8,128)(2,1)S(1)}, u32[]{:S(2)}, u32[]{:S(2)}) collective-permute-start(bf16[3,88,256]{2,1,0:T(8,128)(2,1)S(1)} %get-tuple-element.74), channel_id=1, source_target_pairs={{0,4},{4,0},{8,12},{12,8},{1,5},{5,1},{9,13},{13,9},{2,6},{6,2},{1... | collective-permute-start | bytes 405512 | tf_op jit(solution)/shard_map/ppermute | solution.py:550
  41.6 6.6 %collective-permute-start.11 = (bf16[3,80,256]{2,1,0:T(8,128)(2,1)S(1)}, bf16[3,80,256]{2,1,0:T(8,128)(2,1)S(1)}, u32[]{:S(2)}, u32[]{:S(2)}) collective-permute-start(bf16[3,80,256]{2,1,0:T(8,128)(2,1)S(1)} %get-tuple-element.78), channel_id=1, source_target_pairs={{0,4},{4,0},{8,12},{12,8},{1,5},{5,1},{9,13},{13,9},{2,6},{6,2},{1... | collective-permute-start | bytes 368648 | tf_op jit(solution)/shard_map/ppermute | solution.py:550
  41.6 6.6 %collective-permute-start.12 = (bf16[3,80,256]{2,1,0:T(8,128)(2,1)S(1)}, bf16[3,80,256]{2,1,0:T(8,128)(2,1)S(1)}, u32[]{:S(2)}, u32[]{:S(2)}) collective-permute-start(bf16[3,80,256]{2,1,0:T(8,128)(2,1)S(1)} %get-tuple-element.80), channel_id=1, source_target_pairs={{4,8},{8,4},{5,9},{9,5},{6,10},{10,6},{7,11},{11,7},{20,24},{24,20... | collective-permute-start | bytes 368648 | tf_op jit(solution)/shard_map/ppermute | solution.py:555
  48.2 7.1 %collective-permute-start.15 = (bf16[1024,256]{1,0:T(8,128)(2,1)S(1)}, bf16[1024,256]{1,0:T(8,128)(2,1)S(1)}, u32[]{:S(2)}, u32[]{:S(2)}) collective-permute-start(bf16[1024,256]{1,0:T(8,128)(2,1)S(1)} %get-tuple-element.94), channel_id=1, source_target_pairs={{0,4},{4,0},{8,12},{12,8},{1,5},{5,1},{9,13},{13,9},{2,6},{6,2},{1... | collective-permute-start | bytes 1572872 | tf_op jit(solution)/shard_map/ppermute | solution.py:550
  52.8 3.4 %collective-permute-start.13 = (bf16[1024,256]{1,0:T(8,128)(2,1)S(1)}, bf16[1024,256]{1,0:T(8,128)(2,1)S(1)}, u32[]{:S(2)}, u32[]{:S(2)}) collective-permute-start(bf16[1024,256]{1,0:T(8,128)(2,1)S(1)} %get-tuple-element.88), channel_id=1, source_target_pairs={{0,4},{4,0},{8,12},{12,8},{1,5},{5,1},{9,13},{13,9},{2,6},{6,2},{1... | collective-permute-start | bytes 1572872 | tf_op jit(solution)/shard_map/ppermute | solution.py:550
  55.4 10.5 %collective-permute-start.16 = (bf16[512,256]{1,0:T(8,128)(2,1)S(1)}, bf16[512,256]{1,0:T(8,128)(2,1)S(1)}, u32[]{:S(2)}, u32[]{:S(2)}) collective-permute-start(bf16[512,256]{1,0:T(8,128)(2,1)S(1)} %broadcast_select_fusion), channel_id=1, source_target_pairs={{0,8},{1,9},{2,10},{3,11},{4,5},{5,4},{6,7},{7,6},{8,0},{9,1},{10,... | collective-permute-start | bytes 786440 | tf_op jit(solution)/shard_map/ppermute | solution.py:679
  56.4 9.5 %collective-permute-start.14 = (bf16[512,256]{1,0:T(8,128)(2,1)S(1)}, bf16[512,256]{1,0:T(8,128)(2,1)S(1)}, u32[]{:S(2)}, u32[]{:S(2)}) collective-permute-start(bf16[512,256]{1,0:T(8,128)(2,1)S(1)} %broadcast_select_fusion.1), channel_id=1, source_target_pairs={{0,8},{1,9},{2,10},{3,11},{4,5},{5,4},{6,7},{7,6},{8,0},{9,1},{10,... | collective-permute-start | bytes 786440 | tf_op jit(solution)/shard_map/ppermute | solution.py:679
  58.9 3.1 %collective-permute-start.17 = (bf16[3,88,256]{2,1,0:T(8,128)(2,1)S(1)}, bf16[3,88,256]{2,1,0:T(8,128)(2,1)S(1)}, u32[]{:S(2)}, u32[]{:S(2)}) collective-permute-start(bf16[3,88,256]{2,1,0:T(8,128)(2,1)S(1)} %get-tuple-element.99), channel_id=1, source_target_pairs={{0,4},{4,0},{8,12},{12,8},{1,5},{5,1},{9,13},{13,9},{2,6},{6,2},{1... | collective-permute-start | bytes 405512 | tf_op jit(solution)/shard_map/ppermute | solution.py:550
  59.6 6.3 %collective-permute-start.18 = (bf16[3,88,256]{2,1,0:T(8,128)(2,1)S(1)}, bf16[3,88,256]{2,1,0:T(8,128)(2,1)S(1)}, u32[]{:S(2)}, u32[]{:S(2)}) collective-permute-start(bf16[3,88,256]{2,1,0:T(8,128)(2,1)S(1)} %get-tuple-element.100), channel_id=1, source_target_pairs={{4,8},{8,4},{5,9},{9,5},{6,10},{10,6},{7,11},{11,7},{20,24},{24,20... | collective-permute-start | bytes 405512 | tf_op jit(solution)/shard_map/ppermute | solution.py:555
  66.2 5.3 %collective-permute-start.19 = (bf16[2,256,256]{2,1,0:T(8,128)(2,1)S(1)}, bf16[2,256,256]{2,1,0:T(8,128)(2,1)S(1)}, u32[]{:S(2)}, u32[]{:S(2)}) collective-permute-start(bf16[2,256,256]{2,1,0:T(8,128)(2,1)S(1)} %broadcast_select_fusion.2), channel_id=1, source_target_pairs={{0,1},{1,0},{2,3},{3,2},{4,12},{5,13},{6,14},{7,15},{8,9},{9,8},{1... | collective-permute-start | bytes 786440 | tf_op jit(solution)/shard_map/ppermute | solution.py:679
  71.6 9.0 %collective-permute-start.20 = (bf16[2,128,256]{2,1,0:T(8,128)(2,1)S(1)}, bf16[2,128,256]{2,1,0:T(8,128)(2,1)S(1)}, u32[]{:S(2)}, u32[]{:S(2)}) collective-permute-start(bf16[2,128,256]{2,1,0:T(8,128)(2,1)S(1)} %broadcast_select_fusion.8), channel_id=1, source_target_pairs={{0,2},{1,3},{2,0},{3,1},{4,6},{5,7},{6,4},{7,5},{8,10},{9,11},{10,... | collective-permute-start | bytes 393224 | tf_op jit(solution)/shard_map/ppermute | solution.py:679
  80.7 3.5 %collective-permute-start.21 = (bf16[192,256]{1,0:T(8,128)(2,1)S(1)}, bf16[192,256]{1,0:T(8,128)(2,1)S(1)}, u32[]{:S(2)}, u32[]{:S(2)}) collective-permute-start(bf16[192,256]{1,0:T(8,128)(2,1)S(1)} %pad_maximum_fusion.4), channel_id=1, source_target_pairs={{0,16},{16,0},{1,17},{17,1},{2,18},{18,2},{3,19},{19,3},{4,20},{20... | collective-permute-start | bytes 294920 | tf_op jit(solution)/shard_map/ppermute | solution.py:547
  84.3 5.5 %collective-permute-start.22 = (bf16[192,256]{1,0:T(8,128)(2,1)S(1)}, bf16[192,256]{1,0:T(8,128)(2,1)S(1)}, u32[]{:S(2)}, u32[]{:S(2)}) collective-permute-start(bf16[192,256]{1,0:T(8,128)(2,1)S(1)} %pad_maximum_fusion.5), channel_id=1, source_target_pairs={{0,2},{1,3},{2,0},{3,1},{4,6},{5,7},{6,4},{7,5},{8,10},{9,11},{10,... | collective-permute-start | bytes 294920 | tf_op jit(solution)/shard_map/ppermute | solution.py:679
  84.4 5.5 %collective-permute-start.24 = (bf16[4,68,256]{2,1,0:T(8,128)(2,1)S(1)}, bf16[4,68,256]{2,1,0:T(8,128)(2,1)S(1)}, u32[]{:S(2)}, u32[]{:S(2)}) collective-permute-start(bf16[4,68,256]{2,1,0:T(8,128)(2,1)S(1)} %broadcast_select_fusion.3), channel_id=1, source_target_pairs={{0,16},{16,0},{1,17},{17,1},{2,18},{18,2},{3,19},{19,3},{4,20},{20... | collective-permute-start | bytes 417800 | tf_op jit(solution)/shard_map/ppermute | solution.py:547
  89.9 4.2 %collective-permute-start.23 = (bf16[320,256]{1,0:T(8,128)(2,1)S(1)}, bf16[320,256]{1,0:T(8,128)(2,1)S(1)}, u32[]{:S(2)}, u32[]{:S(2)}) collective-permute-start(bf16[320,256]{1,0:T(8,128)(2,1)S(1)} %pad_maximum_fusion.3), channel_id=1, source_target_pairs={{0,1},{1,0},{2,3},{3,2},{4,12},{5,13},{6,14},{7,15},{8,9},{9,8},{1... | collective-permute-start | bytes 491528 | tf_op jit(solution)/shard_map/ppermute | solution.py:679
  94.3 6.5 %collective-permute-start.25 = (bf16[576,256]{1,0:T(8,128)(2,1)S(1)}, bf16[576,256]{1,0:T(8,128)(2,1)S(1)}, u32[]{:S(2)}, u32[]{:S(2)}) collective-permute-start(bf16[576,256]{1,0:T(8,128)(2,1)S(1)} %pad_maximum_fusion.1), channel_id=1, source_target_pairs={{0,8},{1,9},{2,10},{3,11},{4,5},{5,4},{6,7},{7,6},{8,0},{9,1},{10,... | collective-permute-start | bytes 884744 | tf_op jit(solution)/shard_map/ppermute | solution.py:679
  101.1 7.8 %collective-permute-start.26 = (bf16[1088,256]{1,0:T(8,128)(2,1)S(1)}, bf16[1088,256]{1,0:T(8,128)(2,1)S(1)}, u32[]{:S(2)}, u32[]{:S(2)}) collective-permute-start(bf16[1088,256]{1,0:T(8,128)(2,1)S(1)} %pad_maximum_fusion), channel_id=1, source_target_pairs={{0,4},{4,0},{8,12},{12,8},{1,5},{5,1},{9,13},{13,9},{2,6},{6,2},{1... | collective-permute-start | bytes 1671176 | tf_op jit(solution)/shard_map/ppermute | solution.py:550
